TPU v7x, 32 devices: a whole 2x2x4 slice. The times are simulated.
32 devices in a mesh: slide: 4 (over y, core), tile: 8 (over z, x).
Axes of the slice: x: 2, y: 2, z: 4, core: 2. Of those that a mesh axis runs over, the one named last changes fastest.
Arguments:
- slide_image: bfloat16 [4, 16, 32, 2048], P('slide', 'tile'), may hold values from -6 to 6
- cotangent: bfloat16 [4, 16, 32, 2048], P('slide', 'tile'), may hold values from -0.0234375 to 0.0234375
- weight_one: bfloat16 [3, 3, 64, 64], replicated, may hold values from -0.25 to 0.25
- weight_two: bfloat16 [3, 3, 64, 64], replicated, may hold values from -0.25 to 0.25
- tissue: int32 [4, 16], P('slide', 'tile'), may hold values from 0 to 1, as said below
- neighbours: int32 [4, 16, 8], P('slide', 'tile'), may hold values from -1 to 15, as said below
Outputs:
- output: bfloat16 [4, 16, 32, 2048], P('slide', 'tile')
- grad_input: bfloat16 [4, 16, 32, 2048], P('slide', 'tile')
- grad_one: float32 [3, 3, 64, 64], replicated
- grad_two: float32 [3, 3, 64, 64], replicated
Inputs may be any that keep to these rules, and one draw needn't show every extreme that they name: The tissue tiles of a slide lie on a grid 4 tiles wide in raster order, and device k of the tile axis holds 1 to 2 of them in its first slots, later devices holding later tiles. `neighbours`: slots with tissue 0 have all -1. Neighbour relations are mutual, name only tissue slots, and every neighbour's slot lies on a device at most 5 positions away along the tile axis; that distance is reached in every slide.
All inputs are finite; a program needn't handle non-finite values.
Results may differ from a plain program's by a relative error of at most 0.017.
Values may be sent and summed in bfloat16 or wider, within the bound.
No kernel may reach another device: no remote copies, remote signals or barrier semaphores. Data moves between devices by JAX's collectives and lax.ppermute only.
A program may use at most 64 MiB of HBM per device.

v0:
```python
import jax
import jax.numpy as jnp
from jax import lax
from jax.sharding import PartitionSpec as P

REACH = 5


STRIP_OF_DIRECTION = (1, 0, 3, 2, 1, 1, 0, 0)


def from_behind(value, axis, steps):
    count = lax.axis_size(axis)
    leading, last = (max(0, -steps), min(count, count - steps))
    return lax.ppermute(value, axis, [(source, source + steps) for source in range(leading, last)])


def edge_strips(blocks):
    return jnp.stack([blocks[:, 0], blocks[:, -1], blocks[:, :, 0], blocks[:, :, -1]], axis=1)


def pad_tiles(blocks, fetched):
    top = jnp.concatenate([fetched[:, 4, -1:], fetched[:, 0], fetched[:, 5, :1]], axis=1)
    bottom = jnp.concatenate([fetched[:, 6, -1:], fetched[:, 1], fetched[:, 7, :1]], axis=1)
    middle = jnp.concatenate([fetched[:, 2][:, :, None], blocks, fetched[:, 3][:, :, None]], axis=2)
    return jnp.concatenate([top[:, None], middle, bottom[:, None]], axis=1)


def fetch_edges(blocks, links):
    slots, side, _, channels = blocks.shape
    strips = edge_strips(blocks).reshape(slots, 4, side * channels)
    which = jnp.array(STRIP_OF_DIRECTION, dtype=jnp.int32)[None, :]
    safe_links = jnp.clip(links, 0, None)
    pieces = []
    for offset in range(-REACH, REACH + 1):
        if offset == 0:
            pieces.append(strips)
        else:
            pieces.append(from_behind(strips, "tile", offset))
    stacked = jnp.stack(pieces, axis=0)
    flat_pool = stacked.reshape(stacked.shape[0] * slots * 4, side * channels)
    owner = safe_links // slots
    local_slot = safe_links % slots
    offset_index = jnp.clip(lax.axis_index("tile") - owner + REACH, 0, 2 * REACH)
    lookup = (offset_index * slots + local_slot) * 4 + which
    fetched = jnp.take(flat_pool, lookup.reshape(-1).astype(jnp.int32), axis=0)
    fetched = fetched.reshape(slots, 8, side, channels)
    return jnp.where((links >= 0)[:, :, None, None], fetched, jnp.zeros_like(fetched))


def convolve(padded, kernel):
    return lax.conv_general_dilated(
        padded,
        kernel,
        (1, 1),
        "VALID",
        dimension_numbers=("NHWC", "HWIO", "NHWC"),
        preferred_element_type=jnp.float32,
    )


def flipped(kernel):
    return jnp.transpose(kernel[::-1, ::-1], (0, 1, 3, 2))


def weight_grad(padded, delta_field):
    side = delta_field.shape[1]
    terms = []
    for row_shift in range(3):
        for col_shift in range(3):
            window = padded[:, row_shift : row_shift + side, col_shift : col_shift + side]
            terms.append(
                jnp.einsum("nijc,nijo->co", window, delta_field, preferred_element_type=jnp.float32)
            )
    stacked = jnp.stack(terms, axis=0)
    return stacked.reshape(3, 3, stacked.shape[1], stacked.shape[2])


def local(slide_image, cotangent, weight_one, weight_two, tissue, neighbours):
    slots = slide_image.shape[1]
    side = slide_image.shape[2]
    channels = weight_one.shape[2]
    links = neighbours[0]
    keep_mask = (tissue[0] > 0)[:, None, None, None]
    inputs = jnp.where(keep_mask, slide_image[0].reshape(slots, side, side, channels), 0)
    padded_in = pad_tiles(inputs, fetch_edges(inputs, links))
    hidden = jnp.where(keep_mask, jax.nn.relu(convolve(padded_in, weight_one)), 0.0).astype(
        jnp.bfloat16
    )
    padded_hidden = pad_tiles(hidden, fetch_edges(hidden, links))
    output = jnp.where(keep_mask, convolve(padded_hidden, weight_two), 0.0).astype(jnp.bfloat16)
    upstream = jnp.where(keep_mask, cotangent[0].reshape(slots, side, side, channels), 0)
    padded_up = pad_tiles(upstream, fetch_edges(upstream, links))
    back_hidden = convolve(padded_up, flipped(weight_two))
    delta = jnp.where(hidden > 0, back_hidden, 0.0).astype(jnp.bfloat16)
    grad_two = weight_grad(padded_hidden, upstream)
    padded_delta = pad_tiles(delta, fetch_edges(delta, links))
    grad_input = jnp.where(keep_mask, convolve(padded_delta, flipped(weight_one)), 0.0).astype(
        jnp.bfloat16
    )
    grad_one = weight_grad(padded_in, delta)
    grad_one, grad_two = lax.psum((grad_one, grad_two), ("slide", "tile"))
    return (
        output.reshape(1, slots, side, side * channels),
        grad_input.reshape(1, slots, side, side * channels),
        grad_one,
        grad_two,
    )


def solution(mesh):
    placed = (
        P("slide", "tile", None, None),
        P("slide", "tile", None, None),
        P(),
        P(),
        P("slide", "tile"),
        P("slide", "tile", None),
    )
    return jax.shard_map(
        local,
        mesh=mesh,
        in_specs=placed,
        out_specs=(P("slide", "tile", None, None), P("slide", "tile", None, None), P(), P()),
        check_vma=False,
    )
```

profile of v0, /device:TPU:0, one launch (start us, length us, event | category | flops | bytes accessed | tf_op | source)
XLA Modules:
  0.0 412.3 jit_solution(1776691180103803015)
XLA Ops:
  10.9 6.9 %collective-permute-start.9 = (bf16[2,4,2048]{2,0,1:T(2,128)(2,1)S(1)}, bf16[2,4,2048]{2,0,1:T(2,128)(2,1)S(1)}, u32[]{:S(2)}, u32[]{:S(2)}) collective-permute-start(bf16[2,4,2048]{2,0,1:T(2,128)(2,1)S(1)} %constant_dynamic-update-slice_fusion), channel_id=1, source_target_pairs={{0,5},{1,6},{2,7},{8,13},{9,14},{10,15},{16,21},{17,22},{18,23},{2... | collective-permute-start | bytes 98312 | tf_op jit(solution)/shard_map/ppermute | solution.py:15
  19.1 3.5 collective-permute-start.7
  26.9 5.4 %collective-permute-done.20 = bf16[2,4,2048]{2,0,1:T(2,128)(2,1)S(1)} collective-permute-done((bf16[2,4,2048]{2,0,1:T(2,128)(2,1)S(1)}, bf16[2,4,2048]{2,0,1:T(2,128)(2,1)S(1)}, u32[]{:S(2)}, u32[]{:S(2)}) %collective-permute-start.20) | collective-permute-done | bytes 32800 | tf_op jit(solution)/shard_map/ppermute | solution.py:15
  33.7 6.4 %collective-permute-done = bf16[2,4,2048]{2,0,1:T(2,128)(2,1)S(1)} collective-permute-done((bf16[2,4,2048]{2,0,1:T(2,128)(2,1)S(1)}, bf16[2,4,2048]{2,0,1:T(2,128)(2,1)S(1)}, u32[]{:S(2)}, u32[]{:S(2)}) %collective-permute-start) | collective-permute-done | bytes 32800 | tf_op jit(solution)/shard_map/ppermute | solution.py:15
  41.4 5.4 %collective-permute-done.21 = bf16[2,4,2048]{2,0,1:T(2,128)(2,1)S(1)} collective-permute-done((bf16[2,4,2048]{2,0,1:T(2,128)(2,1)S(1)}, bf16[2,4,2048]{2,0,1:T(2,128)(2,1)S(1)}, u32[]{:S(2)}, u32[]{:S(2)}) %collective-permute-start.21) | collective-permute-done | bytes 32800 | tf_op jit(solution)/shard_map/ppermute | solution.py:15
  48.1 5.4 %collective-permute-done.22 = bf16[2,4,2048]{2,0,1:T(2,128)(2,1)S(1)} collective-permute-done((bf16[2,4,2048]{2,0,1:T(2,128)(2,1)S(1)}, bf16[2,4,2048]{2,0,1:T(2,128)(2,1)S(1)}, u32[]{:S(2)}, u32[]{:S(2)}) %collective-permute-start.22) | collective-permute-done | bytes 32800 | tf_op jit(solution)/shard_map/ppermute | solution.py:15
  54.8 4.5 %collective-permute-done.23 = bf16[2,4,2048]{2,0,1:T(2,128)(2,1)S(1)} collective-permute-done((bf16[2,4,2048]{2,0,1:T(2,128)(2,1)S(1)}, bf16[2,4,2048]{2,0,1:T(2,128)(2,1)S(1)}, u32[]{:S(2)}, u32[]{:S(2)}) %collective-permute-start.23) | collective-permute-done | bytes 32800 | tf_op jit(solution)/shard_map/ppermute | solution.py:15
  60.6 5.9 %collective-permute-done.24 = bf16[2,4,2048]{2,0,1:T(2,128)(2,1)S(1)} collective-permute-done((bf16[2,4,2048]{2,0,1:T(2,128)(2,1)S(1)}, bf16[2,4,2048]{2,0,1:T(2,128)(2,1)S(1)}, u32[]{:S(2)}, u32[]{:S(2)}) %collective-permute-start.24) | collective-permute-done | bytes 32800 | tf_op jit(solution)/shard_map/ppermute | solution.py:15
  66.4 4.8 %collective-permute-start.25 = (bf16[2,4,2048]{2,0,1:T(2,128)(2,1)S(1)}, bf16[2,4,2048]{2,0,1:T(2,128)(2,1)S(1)}, u32[]{:S(2)}, u32[]{:S(2)}) collective-permute-start(bf16[2,4,2048]{2,0,1:T(2,128)(2,1)S(1)} %constant_dynamic-update-slice_fusion.30), channel_id=1, source_target_pairs={{0,1},{1,2},{2,3},{3,4},{4,5},{5,6},{6,7},{8,9},{9,10},{10,11},{11... | collective-permute-start | bytes 98312 | tf_op jit(solution)/shard_map/ppermute | solution.py:15
  72.8 3.7 collective-permute-start.26
  76.5 1.5 collective-permute-done.26
  78.1 3.9 collective-permute-start.27
  82.0 1.5 collective-permute-done.27
  83.6 5.8 %collective-permute-start.28 = (bf16[2,4,2048]{2,0,1:T(2,128)(2,1)S(1)}, bf16[2,4,2048]{2,0,1:T(2,128)(2,1)S(1)}, u32[]{:S(2)}, u32[]{:S(2)}) collective-permute-start(bf16[2,4,2048]{2,0,1:T(2,128)(2,1)S(1)} %constant_dynamic-update-slice_fusion.30), channel_id=1, source_target_pairs={{0,4},{1,5},{2,6},{3,7},{8,12},{9,13},{10,14},{11,15},{16,20},{17,... | collective-permute-start | bytes 98312 | tf_op jit(solution)/shard_map/ppermute | solution.py:15
  89.4 1.5 collective-permute-done.28
  90.9 3.9 collective-permute-start.29
  94.9 1.5 collective-permute-done.29
  97.7 5.4 %collective-permute-done.1 = bf16[2,4,2048]{2,0,1:T(2,128)(2,1)S(1)} collective-permute-done((bf16[2,4,2048]{2,0,1:T(2,128)(2,1)S(1)}, bf16[2,4,2048]{2,0,1:T(2,128)(2,1)S(1)}, u32[]{:S(2)}, u32[]{:S(2)}) %collective-permute-start.1) | collective-permute-done | bytes 32800 | tf_op jit(solution)/shard_map/ppermute | solution.py:15
  104.4 5.4 %collective-permute-done.2 = bf16[2,4,2048]{2,0,1:T(2,128)(2,1)S(1)} collective-permute-done((bf16[2,4,2048]{2,0,1:T(2,128)(2,1)S(1)}, bf16[2,4,2048]{2,0,1:T(2,128)(2,1)S(1)}, u32[]{:S(2)}, u32[]{:S(2)}) %collective-permute-start.2) | collective-permute-done | bytes 32800 | tf_op jit(solution)/shard_map/ppermute | solution.py:15
  111.1 4.8 %collective-permute-done.3 = bf16[2,4,2048]{2,0,1:T(2,128)(2,1)S(1)} collective-permute-done((bf16[2,4,2048]{2,0,1:T(2,128)(2,1)S(1)}, bf16[2,4,2048]{2,0,1:T(2,128)(2,1)S(1)}, u32[]{:S(2)}, u32[]{:S(2)}) %collective-permute-start.3) | collective-permute-done | bytes 32800 | tf_op jit(solution)/shard_map/ppermute | solution.py:15
  117.3 4.8 %collective-permute-done.4 = bf16[2,4,2048]{2,0,1:T(2,128)(2,1)S(1)} collective-permute-done((bf16[2,4,2048]{2,0,1:T(2,128)(2,1)S(1)}, bf16[2,4,2048]{2,0,1:T(2,128)(2,1)S(1)}, u32[]{:S(2)}, u32[]{:S(2)}) %collective-permute-start.4) | collective-permute-done | bytes 32800 | tf_op jit(solution)/shard_map/ppermute | solution.py:15
  122.1 5.0 %collective-permute-start.5 = (bf16[2,4,2048]{2,0,1:T(2,128)(2,1)S(1)}, bf16[2,4,2048]{2,0,1:T(2,128)(2,1)S(1)}, u32[]{:S(2)}, u32[]{:S(2)}) collective-permute-start(bf16[2,4,2048]{2,0,1:T(2,128)(2,1)S(1)} %constant_dynamic-update-slice_fusion), channel_id=1, source_target_pairs={{0,1},{1,2},{2,3},{3,4},{4,5},{5,6},{6,7},{8,9},{9,10},{10,11},{11... | collective-permute-start | bytes 98312 | tf_op jit(solution)/shard_map/ppermute | solution.py:15
  139.3 1.7 fusion.11
  144.5 3.8 collective-permute-start.39
  148.2 1.9 collective-permute-start.38
  150.1 1.9 collective-permute-start.37
  152.0 2.7 collective-permute-start.36
  156.2 1.5 pad_maximum_fusion
  170.1 6.1 %collective-permute-done.10 = bf16[2,4,2048]{2,0,1:T(2,128)(2,1)S(1)} collective-permute-done((bf16[2,4,2048]{2,0,1:T(2,128)(2,1)}, bf16[2,4,2048]{2,0,1:T(2,128)(2,1)S(1)}, u32[]{:S(2)}, u32[]{:S(2)}) %collective-permute-start.10) | collective-permute-done | bytes 32800 | tf_op jit(solution)/shard_map/ppermute | solution.py:15
  178.1 5.0 %collective-permute-done.31 = bf16[2,4,2048]{2,0,1:T(2,128)(2,1)S(1)} collective-permute-done((bf16[2,4,2048]{2,0,1:T(2,128)(2,1)}, bf16[2,4,2048]{2,0,1:T(2,128)(2,1)S(1)}, u32[]{:S(2)}, u32[]{:S(2)}) %collective-permute-start.31) | collective-permute-done | bytes 32800 | tf_op jit(solution)/shard_map/ppermute | solution.py:15
  184.5 5.6 %collective-permute-done.32 = bf16[2,4,2048]{2,0,1:T(2,128)(2,1)S(1)} collective-permute-done((bf16[2,4,2048]{2,0,1:T(2,128)(2,1)}, bf16[2,4,2048]{2,0,1:T(2,128)(2,1)S(1)}, u32[]{:S(2)}, u32[]{:S(2)}) %collective-permute-start.32) | collective-permute-done | bytes 32800 | tf_op jit(solution)/shard_map/ppermute | solution.py:15
  191.4 4.7 %collective-permute-done.33 = bf16[2,4,2048]{2,0,1:T(2,128)(2,1)S(1)} collective-permute-done((bf16[2,4,2048]{2,0,1:T(2,128)(2,1)}, bf16[2,4,2048]{2,0,1:T(2,128)(2,1)S(1)}, u32[]{:S(2)}, u32[]{:S(2)}) %collective-permute-start.33) | collective-permute-done | bytes 32800 | tf_op jit(solution)/shard_map/ppermute | solution.py:15
  197.4 4.7 %collective-permute-done.34 = bf16[2,4,2048]{2,0,1:T(2,128)(2,1)S(1)} collective-permute-done((bf16[2,4,2048]{2,0,1:T(2,128)(2,1)}, bf16[2,4,2048]{2,0,1:T(2,128)(2,1)S(1)}, u32[]{:S(2)}, u32[]{:S(2)}) %collective-permute-start.34) | collective-permute-done | bytes 32800 | tf_op jit(solution)/shard_map/ppermute | solution.py:15
  202.1 4.6 %collective-permute-start.35 = (bf16[2,4,2048]{2,0,1:T(2,128)(2,1)}, bf16[2,4,2048]{2,0,1:T(2,128)(2,1)S(1)}, u32[]{:S(2)}, u32[]{:S(2)}) collective-permute-start(bf16[2,4,2048]{2,0,1:T(2,128)(2,1)} %constant_dynamic-update-slice_fusion.45), channel_id=1, source_target_pairs={{0,1},{1,2},{2,3},{3,4},{4,5},{5,6},{6,7},{8,9},{9,10},{10,11},{11... | collective-permute-start | bytes 98312 | tf_op jit(solution)/shard_map/ppermute | solution.py:15
  206.8 1.8 collective-permute-done.35
  210.0 2.1 collective-permute-start.18
  212.9 1.8 collective-permute-start.17
  215.6 2.1 collective-permute-start.16
  220.6 4.8 %collective-permute-done.11 = bf16[2,4,2048]{2,0,1:T(2,128)(2,1)S(1)} collective-permute-done((bf16[2,4,2048]{2,0,1:T(2,128)(2,1)}, bf16[2,4,2048]{2,0,1:T(2,128)(2,1)S(1)}, u32[]{:S(2)}, u32[]{:S(2)}) %collective-permute-start.11) | collective-permute-done | bytes 32800 | tf_op jit(solution)/shard_map/ppermute | solution.py:15
  227.3 5.0 %collective-permute-done.12 = bf16[2,4,2048]{2,0,1:T(2,128)(2,1)S(1)} collective-permute-done((bf16[2,4,2048]{2,0,1:T(2,128)(2,1)}, bf16[2,4,2048]{2,0,1:T(2,128)(2,1)S(1)}, u32[]{:S(2)}, u32[]{:S(2)}) %collective-permute-start.12) | collective-permute-done | bytes 32800 | tf_op jit(solution)/shard_map/ppermute | solution.py:15
  234.3 4.1 collective-permute-done.13
  240.3 4.1 collective-permute-done.14
  244.4 4.5 %collective-permute-start.15 = (bf16[2,4,2048]{2,0,1:T(2,128)(2,1)}, bf16[2,4,2048]{2,0,1:T(2,128)(2,1)S(1)}, u32[]{:S(2)}, u32[]{:S(2)}) collective-permute-start(bf16[2,4,2048]{2,0,1:T(2,128)(2,1)} %constant_dynamic-update-slice_fusion.15), channel_id=1, source_target_pairs={{0,1},{1,2},{2,3},{3,4},{4,5},{5,6},{6,7},{8,9},{9,10},{10,11},{11... | collective-permute-start | bytes 98312 | tf_op jit(solution)/shard_map/ppermute | solution.py:15
  257.7 1.5 pad_maximum_fusion.1
  262.4 1.8 fusion.12
  276.5 125.5 %all-reduce.3.cloned.1.call-done = (f32[3,3,64,64]{3,2,1,0:T(8,128)}, f32[3,3,64,64]{3,2,1,0:T(8,128)}) async-done(((f32[3,3,64,64]{3,2,1,0:T(8,128)}, f32[3,3,64,64]{3,2,1,0:T(8,128)}), (f32[3,3,64,64]{3,2,1,0:T(8,128)}, f32[3,3,64,64]{3,2,1,0:T(8,128)})) %all-reduce.3.cloned.1.call-update) | async-done | bytes 294928 | tf_op jit(solution)/shard_map/psum | solution.py:102
  402.1 1.7 copy.340
  403.7 1.7 copy.341
  (327 shorter events, 92.8 us)
Async XLA Ops:
  7.2 127.4 %copy-start = (bf16[3,3,64,64]{3,2,1,0:T(8,128)(2,1)S(1)}, bf16[3,3,64,64]{3,2,1,0:T(8,128)(2,1)}, u32[]{:S(2)}) copy-start(bf16[3,3,64,64]{3,2,1,0:T(8,128)(2,1)} %param.14) | copy-start | bytes 221188
  7.2 394.9 %all-reduce.3.cloned.1.call-start = ((), (), s32[]{:S(2)}) async-start(), calls=%async_computation | async-start | bytes 1179648 | tf_op jit(solution)/shard_map/psum | solution.py:102
  10.2 15.5 %copy-start.20 = (s32[1,2,8]{2,1,0:T(2,128)S(1)}, s32[1,2,8]{2,1,0:T(2,128)}, u32[]{:S(2)}) copy-start(s32[1,2,8]{2,1,0:T(2,128)} %param.17) | copy-start | bytes 196
  10.2 15.5 %copy-start.23 = (s32[8]{0:T(128)S(1)}, s32[8]{0:T(128)}, u32[]{:S(2)}) copy-start(s32[8]{0:T(128)} %constant.84.clone) | copy-start | bytes 100
  10.9 118.1 %collective-permute-start.9 = (bf16[2,4,2048]{2,0,1:T(2,128)(2,1)S(1)}, bf16[2,4,2048]{2,0,1:T(2,128)(2,1)S(1)}, u32[]{:S(2)}, u32[]{:S(2)}) collective-permute-start(bf16[2,4,2048]{2,0,1:T(2,128)(2,1)S(1)} %constant_dynamic-update-slice_fusion), channel_id=1, source_target_pairs={{0,5},{1,6},{2,7},{8,13},{9,14},{10,15},{16,21},{17,22},{18,23},{2... | collective-permute-start | bytes 98312 | tf_op jit(solution)/shard_map/ppermute | solution.py:15
  17.8 110.9 %collective-permute-start.8 = (bf16[2,4,2048]{2,0,1:T(2,128)(2,1)S(1)}, bf16[2,4,2048]{2,0,1:T(2,128)(2,1)S(1)}, u32[]{:S(2)}, u32[]{:S(2)}) collective-permute-start(bf16[2,4,2048]{2,0,1:T(2,128)(2,1)S(1)} %constant_dynamic-update-slice_fusion), channel_id=1, source_target_pairs={{0,4},{1,5},{2,6},{3,7},{8,12},{9,13},{10,14},{11,15},{16,20},{17,... | collective-permute-start | bytes 98312 | tf_op jit(solution)/shard_map/ppermute | solution.py:15
  19.1 109.5 %collective-permute-start.7 = (bf16[2,4,2048]{2,0,1:T(2,128)(2,1)S(1)}, bf16[2,4,2048]{2,0,1:T(2,128)(2,1)S(1)}, u32[]{:S(2)}, u32[]{:S(2)}) collective-permute-start(bf16[2,4,2048]{2,0,1:T(2,128)(2,1)S(1)} %constant_dynamic-update-slice_fusion), channel_id=1, source_target_pairs={{0,3},{1,4},{2,5},{3,6},{4,7},{8,11},{9,12},{10,13},{11,14},{12,15... | collective-permute-start | bytes 98312 | tf_op jit(solution)/shard_map/ppermute | solution.py:15
  22.6 106.0 %collective-permute-start.6 = (bf16[2,4,2048]{2,0,1:T(2,128)(2,1)S(1)}, bf16[2,4,2048]{2,0,1:T(2,128)(2,1)S(1)}, u32[]{:S(2)}, u32[]{:S(2)}) collective-permute-start(bf16[2,4,2048]{2,0,1:T(2,128)(2,1)S(1)} %constant_dynamic-update-slice_fusion), channel_id=1, source_target_pairs={{0,2},{1,3},{2,4},{3,5},{4,6},{5,7},{8,10},{9,11},{10,12},{11,13},... | collective-permute-start | bytes 98312 | tf_op jit(solution)/shard_map/ppermute | solution.py:15
  24.4 8.0 %collective-permute-start.20 = (bf16[2,4,2048]{2,0,1:T(2,128)(2,1)S(1)}, bf16[2,4,2048]{2,0,1:T(2,128)(2,1)S(1)}, u32[]{:S(2)}, u32[]{:S(2)}) collective-permute-start(bf16[2,4,2048]{2,0,1:T(2,128)(2,1)S(1)} %constant_dynamic-update-slice_fusion.30), channel_id=1, source_target_pairs={{5,0},{6,1},{7,2},{13,8},{14,9},{15,10},{21,16},{22,17},{23,18},{2... | collective-permute-start | bytes 98312 | tf_op jit(solution)/shard_map/ppermute | solution.py:15
  26.9 104.0 %copy-start.18 = (pred[2,8]{0,1:T(8,128)(4,1)}, pred[2,8]{0,1:T(8,128)(4,1)S(1)}, u32[]{:S(2)}) copy-start(pred[2,8]{0,1:T(8,128)(4,1)S(1)} %copy.131) | copy-start | bytes 52
  32.3 7.7 %collective-permute-start = (bf16[2,4,2048]{2,0,1:T(2,128)(2,1)S(1)}, bf16[2,4,2048]{2,0,1:T(2,128)(2,1)S(1)}, u32[]{:S(2)}, u32[]{:S(2)}) collective-permute-start(bf16[2,4,2048]{2,0,1:T(2,128)(2,1)S(1)} %constant_dynamic-update-slice_fusion), channel_id=1, source_target_pairs={{5,0},{6,1},{7,2},{13,8},{14,9},{15,10},{21,16},{22,17},{23,18},{2... | collective-permute-start | bytes 98312 | tf_op jit(solution)/shard_map/ppermute | solution.py:15
  40.0 6.7 %collective-permute-start.21 = (bf16[2,4,2048]{2,0,1:T(2,128)(2,1)S(1)}, bf16[2,4,2048]{2,0,1:T(2,128)(2,1)S(1)}, u32[]{:S(2)}, u32[]{:S(2)}) collective-permute-start(bf16[2,4,2048]{2,0,1:T(2,128)(2,1)S(1)} %constant_dynamic-update-slice_fusion.30), channel_id=1, source_target_pairs={{4,0},{5,1},{6,2},{7,3},{12,8},{13,9},{14,10},{15,11},{20,16},{21,... | collective-permute-start | bytes 98312 | tf_op jit(solution)/shard_map/ppermute | solution.py:15
  46.7 6.7 %collective-permute-start.22 = (bf16[2,4,2048]{2,0,1:T(2,128)(2,1)S(1)}, bf16[2,4,2048]{2,0,1:T(2,128)(2,1)S(1)}, u32[]{:S(2)}, u32[]{:S(2)}) collective-permute-start(bf16[2,4,2048]{2,0,1:T(2,128)(2,1)S(1)} %constant_dynamic-update-slice_fusion.30), channel_id=1, source_target_pairs={{3,0},{4,1},{5,2},{6,3},{7,4},{11,8},{12,9},{13,10},{14,11},{15,12... | collective-permute-start | bytes 98312 | tf_op jit(solution)/shard_map/ppermute | solution.py:15
  53.4 5.8 %collective-permute-start.23 = (bf16[2,4,2048]{2,0,1:T(2,128)(2,1)S(1)}, bf16[2,4,2048]{2,0,1:T(2,128)(2,1)S(1)}, u32[]{:S(2)}, u32[]{:S(2)}) collective-permute-start(bf16[2,4,2048]{2,0,1:T(2,128)(2,1)S(1)} %constant_dynamic-update-slice_fusion.30), channel_id=1, source_target_pairs={{2,0},{3,1},{4,2},{5,3},{6,4},{7,5},{10,8},{11,9},{12,10},{13,11},... | collective-permute-start | bytes 98312 | tf_op jit(solution)/shard_map/ppermute | solution.py:15
  59.2 7.2 %collective-permute-start.24 = (bf16[2,4,2048]{2,0,1:T(2,128)(2,1)S(1)}, bf16[2,4,2048]{2,0,1:T(2,128)(2,1)S(1)}, u32[]{:S(2)}, u32[]{:S(2)}) collective-permute-start(bf16[2,4,2048]{2,0,1:T(2,128)(2,1)S(1)} %constant_dynamic-update-slice_fusion.30), channel_id=1, source_target_pairs={{1,0},{2,1},{3,2},{4,3},{5,4},{6,5},{7,6},{9,8},{10,9},{11,10},{12... | collective-permute-start | bytes 98312 | tf_op jit(solution)/shard_map/ppermute | solution.py:15
  66.4 6.4 %collective-permute-start.25 = (bf16[2,4,2048]{2,0,1:T(2,128)(2,1)S(1)}, bf16[2,4,2048]{2,0,1:T(2,128)(2,1)S(1)}, u32[]{:S(2)}, u32[]{:S(2)}) collective-permute-start(bf16[2,4,2048]{2,0,1:T(2,128)(2,1)S(1)} %constant_dynamic-update-slice_fusion.30), channel_id=1, source_target_pairs={{0,1},{1,2},{2,3},{3,4},{4,5},{5,6},{6,7},{8,9},{9,10},{10,11},{11... | collective-permute-start | bytes 98312 | tf_op jit(solution)/shard_map/ppermute | solution.py:15
  72.8 5.2 %collective-permute-start.26 = (bf16[2,4,2048]{2,0,1:T(2,128)(2,1)S(1)}, bf16[2,4,2048]{2,0,1:T(2,128)(2,1)S(1)}, u32[]{:S(2)}, u32[]{:S(2)}) collective-permute-start(bf16[2,4,2048]{2,0,1:T(2,128)(2,1)S(1)} %constant_dynamic-update-slice_fusion.30), channel_id=1, source_target_pairs={{0,2},{1,3},{2,4},{3,5},{4,6},{5,7},{8,10},{9,11},{10,12},{11,13},... | collective-permute-start | bytes 98312 | tf_op jit(solution)/shard_map/ppermute | solution.py:15
  78.1 5.5 %collective-permute-start.27 = (bf16[2,4,2048]{2,0,1:T(2,128)(2,1)S(1)}, bf16[2,4,2048]{2,0,1:T(2,128)(2,1)S(1)}, u32[]{:S(2)}, u32[]{:S(2)}) collective-permute-start(bf16[2,4,2048]{2,0,1:T(2,128)(2,1)S(1)} %constant_dynamic-update-slice_fusion.30), channel_id=1, source_target_pairs={{0,3},{1,4},{2,5},{3,6},{4,7},{8,11},{9,12},{10,13},{11,14},{12,15... | collective-permute-start | bytes 98312 | tf_op jit(solution)/shard_map/ppermute | solution.py:15
  83.6 7.3 %collective-permute-start.28 = (bf16[2,4,2048]{2,0,1:T(2,128)(2,1)S(1)}, bf16[2,4,2048]{2,0,1:T(2,128)(2,1)S(1)}, u32[]{:S(2)}, u32[]{:S(2)}) collective-permute-start(bf16[2,4,2048]{2,0,1:T(2,128)(2,1)S(1)} %constant_dynamic-update-slice_fusion.30), channel_id=1, source_target_pairs={{0,4},{1,5},{2,6},{3,7},{8,12},{9,13},{10,14},{11,15},{16,20},{17,... | collective-permute-start | bytes 98312 | tf_op jit(solution)/shard_map/ppermute | solution.py:15
  90.9 5.5 %collective-permute-start.29 = (bf16[2,4,2048]{2,0,1:T(2,128)(2,1)S(1)}, bf16[2,4,2048]{2,0,1:T(2,128)(2,1)S(1)}, u32[]{:S(2)}, u32[]{:S(2)}) collective-permute-start(bf16[2,4,2048]{2,0,1:T(2,128)(2,1)S(1)} %constant_dynamic-update-slice_fusion.30), channel_id=1, source_target_pairs={{0,5},{1,6},{2,7},{8,13},{9,14},{10,15},{16,21},{17,22},{18,23},{2... | collective-permute-start | bytes 98312 | tf_op jit(solution)/shard_map/ppermute | solution.py:15
  96.4 6.7 %collective-permute-start.1 = (bf16[2,4,2048]{2,0,1:T(2,128)(2,1)S(1)}, bf16[2,4,2048]{2,0,1:T(2,128)(2,1)S(1)}, u32[]{:S(2)}, u32[]{:S(2)}) collective-permute-start(bf16[2,4,2048]{2,0,1:T(2,128)(2,1)S(1)} %constant_dynamic-update-slice_fusion), channel_id=1, source_target_pairs={{4,0},{5,1},{6,2},{7,3},{12,8},{13,9},{14,10},{15,11},{20,16},{21,... | collective-permute-start | bytes 98312 | tf_op jit(solution)/shard_map/ppermute | solution.py:15
  103.1 6.7 %collective-permute-start.2 = (bf16[2,4,2048]{2,0,1:T(2,128)(2,1)S(1)}, bf16[2,4,2048]{2,0,1:T(2,128)(2,1)S(1)}, u32[]{:S(2)}, u32[]{:S(2)}) collective-permute-start(bf16[2,4,2048]{2,0,1:T(2,128)(2,1)S(1)} %constant_dynamic-update-slice_fusion), channel_id=1, source_target_pairs={{3,0},{4,1},{5,2},{6,3},{7,4},{11,8},{12,9},{13,10},{14,11},{15,12... | collective-permute-start | bytes 98312 | tf_op jit(solution)/shard_map/ppermute | solution.py:15
  109.8 6.2 %collective-permute-start.3 = (bf16[2,4,2048]{2,0,1:T(2,128)(2,1)S(1)}, bf16[2,4,2048]{2,0,1:T(2,128)(2,1)S(1)}, u32[]{:S(2)}, u32[]{:S(2)}) collective-permute-start(bf16[2,4,2048]{2,0,1:T(2,128)(2,1)S(1)} %constant_dynamic-update-slice_fusion), channel_id=1, source_target_pairs={{2,0},{3,1},{4,2},{5,3},{6,4},{7,5},{10,8},{11,9},{12,10},{13,11},... | collective-permute-start | bytes 98312 | tf_op jit(solution)/shard_map/ppermute | solution.py:15
  116.0 6.1 %collective-permute-start.4 = (bf16[2,4,2048]{2,0,1:T(2,128)(2,1)S(1)}, bf16[2,4,2048]{2,0,1:T(2,128)(2,1)S(1)}, u32[]{:S(2)}, u32[]{:S(2)}) collective-permute-start(bf16[2,4,2048]{2,0,1:T(2,128)(2,1)S(1)} %constant_dynamic-update-slice_fusion), channel_id=1, source_target_pairs={{1,0},{2,1},{3,2},{4,3},{5,4},{6,5},{7,6},{9,8},{10,9},{11,10},{12... | collective-permute-start | bytes 98312 | tf_op jit(solution)/shard_map/ppermute | solution.py:15
  122.1 6.4 %collective-permute-start.5 = (bf16[2,4,2048]{2,0,1:T(2,128)(2,1)S(1)}, bf16[2,4,2048]{2,0,1:T(2,128)(2,1)S(1)}, u32[]{:S(2)}, u32[]{:S(2)}) collective-permute-start(bf16[2,4,2048]{2,0,1:T(2,128)(2,1)S(1)} %constant_dynamic-update-slice_fusion), channel_id=1, source_target_pairs={{0,1},{1,2},{2,3},{3,4},{4,5},{5,6},{6,7},{8,9},{9,10},{10,11},{11... | collective-permute-start | bytes 98312 | tf_op jit(solution)/shard_map/ppermute | solution.py:15
  144.5 14.2 %copy-start.1 = (bf16[32,16,5,64]{3,0,2,1:T(8,128)(2,1)S(1)}, bf16[32,16,5,64]{3,0,2,1:T(8,128)(2,1)}, u32[]{:S(2)}) copy-start(bf16[32,16,5,64]{3,0,2,1:T(8,128)(2,1)} %copy.150) | copy-start | bytes 983044
  144.5 74.0 %collective-permute-start.39 = (bf16[2,4,2048]{2,0,1:T(2,128)(2,1)}, bf16[2,4,2048]{2,0,1:T(2,128)(2,1)}, u32[]{:S(2)}, u32[]{:S(2)}) collective-permute-start(bf16[2,4,2048]{2,0,1:T(2,128)(2,1)} %constant_dynamic-update-slice_fusion.45), channel_id=1, source_target_pairs={{0,5},{1,6},{2,7},{8,13},{9,14},{10,15},{16,21},{17,22},{18,23},{2... | collective-permute-start | bytes 98312 | tf_op jit(solution)/shard_map/ppermute | solution.py:15
  148.2 67.4 %collective-permute-start.38 = (bf16[2,4,2048]{2,0,1:T(2,128)(2,1)}, bf16[2,4,2048]{2,0,1:T(2,128)(2,1)}, u32[]{:S(2)}, u32[]{:S(2)}) collective-permute-start(bf16[2,4,2048]{2,0,1:T(2,128)(2,1)} %constant_dynamic-update-slice_fusion.45), channel_id=1, source_target_pairs={{0,4},{1,5},{2,6},{3,7},{8,12},{9,13},{10,14},{11,15},{16,20},{17,... | collective-permute-start | bytes 98312 | tf_op jit(solution)/shard_map/ppermute | solution.py:15
  150.1 62.8 %collective-permute-start.37 = (bf16[2,4,2048]{2,0,1:T(2,128)(2,1)}, bf16[2,4,2048]{2,0,1:T(2,128)(2,1)}, u32[]{:S(2)}, u32[]{:S(2)}) collective-permute-start(bf16[2,4,2048]{2,0,1:T(2,128)(2,1)} %constant_dynamic-update-slice_fusion.45), channel_id=1, source_target_pairs={{0,3},{1,4},{2,5},{3,6},{4,7},{8,11},{9,12},{10,13},{11,14},{12,15... | collective-permute-start | bytes 98312 | tf_op jit(solution)/shard_map/ppermute | solution.py:15
  152.0 58.0 %collective-permute-start.36 = (bf16[2,4,2048]{2,0,1:T(2,128)(2,1)}, bf16[2,4,2048]{2,0,1:T(2,128)(2,1)}, u32[]{:S(2)}, u32[]{:S(2)}) collective-permute-start(bf16[2,4,2048]{2,0,1:T(2,128)(2,1)} %constant_dynamic-update-slice_fusion.45), channel_id=1, source_target_pairs={{0,2},{1,3},{2,4},{3,5},{4,6},{5,7},{8,10},{9,11},{10,12},{11,13},... | collective-permute-start | bytes 98312 | tf_op jit(solution)/shard_map/ppermute | solution.py:15
  154.7 13.3 %collective-permute-start.30 = (bf16[2,4,2048]{2,0,1:T(2,128)(2,1)}, bf16[2,4,2048]{2,0,1:T(2,128)(2,1)}, u32[]{:S(2)}, u32[]{:S(2)}) collective-permute-start(bf16[2,4,2048]{2,0,1:T(2,128)(2,1)} %constant_dynamic-update-slice_fusion.45), channel_id=1, source_target_pairs={{5,0},{6,1},{7,2},{13,8},{14,9},{15,10},{21,16},{22,17},{23,18},{2... | collective-permute-start | bytes 98312 | tf_op jit(solution)/shard_map/ppermute | solution.py:15
  164.3 3.1 copy-start.17
  164.3 3.3 copy-start.13
  168.0 8.2 %collective-permute-start.10 = (bf16[2,4,2048]{2,0,1:T(2,128)(2,1)}, bf16[2,4,2048]{2,0,1:T(2,128)(2,1)S(1)}, u32[]{:S(2)}, u32[]{:S(2)}) collective-permute-start(bf16[2,4,2048]{2,0,1:T(2,128)(2,1)} %constant_dynamic-update-slice_fusion.15), channel_id=1, source_target_pairs={{5,0},{6,1},{7,2},{13,8},{14,9},{15,10},{21,16},{22,17},{23,18},{2... | collective-permute-start | bytes 98312 | tf_op jit(solution)/shard_map/ppermute | solution.py:15
  176.2 6.9 %collective-permute-start.31 = (bf16[2,4,2048]{2,0,1:T(2,128)(2,1)}, bf16[2,4,2048]{2,0,1:T(2,128)(2,1)S(1)}, u32[]{:S(2)}, u32[]{:S(2)}) collective-permute-start(bf16[2,4,2048]{2,0,1:T(2,128)(2,1)} %constant_dynamic-update-slice_fusion.45), channel_id=1, source_target_pairs={{4,0},{5,1},{6,2},{7,3},{12,8},{13,9},{14,10},{15,11},{20,16},{21,... | collective-permute-start | bytes 98312 | tf_op jit(solution)/shard_map/ppermute | solution.py:15
  183.1 6.9 %collective-permute-start.32 = (bf16[2,4,2048]{2,0,1:T(2,128)(2,1)}, bf16[2,4,2048]{2,0,1:T(2,128)(2,1)S(1)}, u32[]{:S(2)}, u32[]{:S(2)}) collective-permute-start(bf16[2,4,2048]{2,0,1:T(2,128)(2,1)} %constant_dynamic-update-slice_fusion.45), channel_id=1, source_target_pairs={{3,0},{4,1},{5,2},{6,3},{7,4},{11,8},{12,9},{13,10},{14,11},{15,12... | collective-permute-start | bytes 98312 | tf_op jit(solution)/shard_map/ppermute | solution.py:15
  190.0 6.0 %collective-permute-start.33 = (bf16[2,4,2048]{2,0,1:T(2,128)(2,1)}, bf16[2,4,2048]{2,0,1:T(2,128)(2,1)S(1)}, u32[]{:S(2)}, u32[]{:S(2)}) collective-permute-start(bf16[2,4,2048]{2,0,1:T(2,128)(2,1)} %constant_dynamic-update-slice_fusion.45), channel_id=1, source_target_pairs={{2,0},{3,1},{4,2},{5,3},{6,4},{7,5},{10,8},{11,9},{12,10},{13,11},... | collective-permute-start | bytes 98312 | tf_op jit(solution)/shard_map/ppermute | solution.py:15
  196.1 6.0 %collective-permute-start.34 = (bf16[2,4,2048]{2,0,1:T(2,128)(2,1)}, bf16[2,4,2048]{2,0,1:T(2,128)(2,1)S(1)}, u32[]{:S(2)}, u32[]{:S(2)}) collective-permute-start(bf16[2,4,2048]{2,0,1:T(2,128)(2,1)} %constant_dynamic-update-slice_fusion.45), channel_id=1, source_target_pairs={{1,0},{2,1},{3,2},{4,3},{5,4},{6,5},{7,6},{9,8},{10,9},{11,10},{12... | collective-permute-start | bytes 98312 | tf_op jit(solution)/shard_map/ppermute | solution.py:15
  202.1 6.5 %collective-permute-start.35 = (bf16[2,4,2048]{2,0,1:T(2,128)(2,1)}, bf16[2,4,2048]{2,0,1:T(2,128)(2,1)S(1)}, u32[]{:S(2)}, u32[]{:S(2)}) collective-permute-start(bf16[2,4,2048]{2,0,1:T(2,128)(2,1)} %constant_dynamic-update-slice_fusion.45), channel_id=1, source_target_pairs={{0,1},{1,2},{2,3},{3,4},{4,5},{5,6},{6,7},{8,9},{9,10},{10,11},{11... | collective-permute-start | bytes 98312 | tf_op jit(solution)/shard_map/ppermute | solution.py:15
  208.6 45.5 %collective-permute-start.19 = (bf16[2,4,2048]{2,0,1:T(2,128)(2,1)}, bf16[2,4,2048]{2,0,1:T(2,128)(2,1)S(1)}, u32[]{:S(2)}, u32[]{:S(2)}) collective-permute-start(bf16[2,4,2048]{2,0,1:T(2,128)(2,1)} %constant_dynamic-update-slice_fusion.15), channel_id=1, source_target_pairs={{0,5},{1,6},{2,7},{8,13},{9,14},{10,15},{16,21},{17,22},{18,23},{2... | collective-permute-start | bytes 98312 | tf_op jit(solution)/shard_map/ppermute | solution.py:15
  210.0 42.7 %collective-permute-start.18 = (bf16[2,4,2048]{2,0,1:T(2,128)(2,1)}, bf16[2,4,2048]{2,0,1:T(2,128)(2,1)S(1)}, u32[]{:S(2)}, u32[]{:S(2)}) collective-permute-start(bf16[2,4,2048]{2,0,1:T(2,128)(2,1)} %constant_dynamic-update-slice_fusion.15), channel_id=1, source_target_pairs={{0,4},{1,5},{2,6},{3,7},{8,12},{9,13},{10,14},{11,15},{16,20},{17,... | collective-permute-start | bytes 98312 | tf_op jit(solution)/shard_map/ppermute | solution.py:15
  212.9 39.1 %collective-permute-start.17 = (bf16[2,4,2048]{2,0,1:T(2,128)(2,1)}, bf16[2,4,2048]{2,0,1:T(2,128)(2,1)S(1)}, u32[]{:S(2)}, u32[]{:S(2)}) collective-permute-start(bf16[2,4,2048]{2,0,1:T(2,128)(2,1)} %constant_dynamic-update-slice_fusion.15), channel_id=1, source_target_pairs={{0,3},{1,4},{2,5},{3,6},{4,7},{8,11},{9,12},{10,13},{11,14},{12,15... | collective-permute-start | bytes 98312 | tf_op jit(solution)/shard_map/ppermute | solution.py:15
  215.6 35.8 %collective-permute-start.16 = (bf16[2,4,2048]{2,0,1:T(2,128)(2,1)}, bf16[2,4,2048]{2,0,1:T(2,128)(2,1)S(1)}, u32[]{:S(2)}, u32[]{:S(2)}) collective-permute-start(bf16[2,4,2048]{2,0,1:T(2,128)(2,1)} %constant_dynamic-update-slice_fusion.15), channel_id=1, source_target_pairs={{0,2},{1,3},{2,4},{3,5},{4,6},{5,7},{8,10},{9,11},{10,12},{11,13},... | collective-permute-start | bytes 98312 | tf_op jit(solution)/shard_map/ppermute | solution.py:15
  218.5 6.9 %collective-permute-start.11 = (bf16[2,4,2048]{2,0,1:T(2,128)(2,1)}, bf16[2,4,2048]{2,0,1:T(2,128)(2,1)S(1)}, u32[]{:S(2)}, u32[]{:S(2)}) collective-permute-start(bf16[2,4,2048]{2,0,1:T(2,128)(2,1)} %constant_dynamic-update-slice_fusion.15), channel_id=1, source_target_pairs={{4,0},{5,1},{6,2},{7,3},{12,8},{13,9},{14,10},{15,11},{20,16},{21,... | collective-permute-start | bytes 98312 | tf_op jit(solution)/shard_map/ppermute | solution.py:15
  225.4 6.9 %collective-permute-start.12 = (bf16[2,4,2048]{2,0,1:T(2,128)(2,1)}, bf16[2,4,2048]{2,0,1:T(2,128)(2,1)S(1)}, u32[]{:S(2)}, u32[]{:S(2)}) collective-permute-start(bf16[2,4,2048]{2,0,1:T(2,128)(2,1)} %constant_dynamic-update-slice_fusion.15), channel_id=1, source_target_pairs={{3,0},{4,1},{5,2},{6,3},{7,4},{11,8},{12,9},{13,10},{14,11},{15,12... | collective-permute-start | bytes 98312 | tf_op jit(solution)/shard_map/ppermute | solution.py:15
  232.3 6.0 %collective-permute-start.13 = (bf16[2,4,2048]{2,0,1:T(2,128)(2,1)}, bf16[2,4,2048]{2,0,1:T(2,128)(2,1)S(1)}, u32[]{:S(2)}, u32[]{:S(2)}) collective-permute-start(bf16[2,4,2048]{2,0,1:T(2,128)(2,1)} %constant_dynamic-update-slice_fusion.15), channel_id=1, source_target_pairs={{2,0},{3,1},{4,2},{5,3},{6,4},{7,5},{10,8},{11,9},{12,10},{13,11},... | collective-permute-start | bytes 98312 | tf_op jit(solution)/shard_map/ppermute | solution.py:15
  238.3 6.0 %collective-permute-start.14 = (bf16[2,4,2048]{2,0,1:T(2,128)(2,1)}, bf16[2,4,2048]{2,0,1:T(2,128)(2,1)S(1)}, u32[]{:S(2)}, u32[]{:S(2)}) collective-permute-start(bf16[2,4,2048]{2,0,1:T(2,128)(2,1)} %constant_dynamic-update-slice_fusion.15), channel_id=1, source_target_pairs={{1,0},{2,1},{3,2},{4,3},{5,4},{6,5},{7,6},{9,8},{10,9},{11,10},{12... | collective-permute-start | bytes 98312 | tf_op jit(solution)/shard_map/ppermute | solution.py:15
  244.4 6.4 %collective-permute-start.15 = (bf16[2,4,2048]{2,0,1:T(2,128)(2,1)}, bf16[2,4,2048]{2,0,1:T(2,128)(2,1)S(1)}, u32[]{:S(2)}, u32[]{:S(2)}) collective-permute-start(bf16[2,4,2048]{2,0,1:T(2,128)(2,1)} %constant_dynamic-update-slice_fusion.15), channel_id=1, source_target_pairs={{0,1},{1,2},{2,3},{3,4},{4,5},{5,6},{6,7},{8,9},{9,10},{10,11},{11... | collective-permute-start | bytes 98312 | tf_op jit(solution)/shard_map/ppermute | solution.py:15
  (19 other events, 23.8 us)
Sparse Core Ops, SparseCore 0:
  275.2 126.8 all-reduce.2
where the time goes:
time: 414 us; the launch traced here: 412 us
  waiting for transfers between devices  234 us (57%)
  starting transfers between devices  92.7 us (22%)
  local copies, waits for them, and re-layouts  44.7 us (11%)
  between operations  15.7 us (4%)
  matrix products  13.8 us (3%)
  other arithmetic  11.1 us (3%)
    psum x1, waiting for transfers between devices, local(): grad_one, grad_two = lax.psum((grad_one, grad_two), ('slide', 'tile'))  126 us
    ppermute x40, waiting for transfers between devices, from_behind(): lax.ppermute(value, axis, [(source, source + steps) for source in range(l...  109 us
    ppermute x40, starting transfers between devices, from_behind(): lax.ppermute(value, axis, [(source, source + steps) for source in range(l...  92.6 us
    unnamed x110, local copies, waits for them, and re-layouts  24.1 us
  transfers between devices with their start and end apart: 41, of which 28 were waited for; matrix products, arithmetic and copies ran while one was open for 6% of the time, Pallas kernels for 0%

commit v1 on v0

v1 whole, which is shorter than its diff:
```python
import functools

import jax
import jax.numpy as jnp
from jax import lax
from jax.experimental import pallas as pl
from jax.experimental.pallas import tpu as pltpu
from jax.sharding import PartitionSpec as P

F32 = jnp.float32
BF16 = jnp.bfloat16
LANES = 128
SMEM = pl.BlockSpec(memory_space=pltpu.SMEM)
VMEM = pl.BlockSpec(memory_space=pltpu.VMEM)


def pack_kernel(links_ref, image_ref, cotangent_ref, out_ref, strip_ref):
    slots, side, width = image_ref.shape
    pairs = width // LANES
    for slot in range(slots):
        for field, ref in enumerate((image_ref, cotangent_ref)):
            top = ref[slot, 0:16, :].astype(F32)
            bottom = ref[slot, side - 16 : side, :].astype(F32)
            for pair in range(pairs):
                lanes = slice(pair * LANES, (pair + 1) * LANES)
                rows = slice(2 * pair, 2 * pair + 2)
                strip_ref[slot, field, 0, rows, :] = top[0:2, lanes]
                strip_ref[slot, field, 1, rows, :] = bottom[14:16, lanes]
    for slot in range(slots):
        for direction in range(8):
            link = links_ref[slot, direction]

            @pl.when(link >= 0)
            def _(slot=slot, direction=direction, link=link):
                device = link // slots
                there = link % slots
                for field, ref in enumerate((image_ref, cotangent_ref)):
                    if direction < 2:
                        strip = strip_ref[slot, field, direction].astype(BF16)
                        out_ref[device, slot, there, field] = strip
                    elif direction == 2:
                        out_ref[device, slot, there, field] = ref[slot, :, 0:LANES]
                    elif direction == 3:
                        out_ref[device, slot, there, field] = ref[slot, :, width - LANES : width]
                    else:
                        which = 0 if direction < 6 else 1
                        first = 0 if direction % 2 == 0 else side - 16
                        corner = strip_ref[slot, field, which, first : first + 16, :]
                        out_ref[device, slot, there, field, 0:16, :] = corner.astype(BF16)


def mix_kernel(
    links_ref, tissue_ref, image_ref, cotangent_ref, halo_ref, one_ref, two_ref,
    output_ref, grad_input_ref, grads_ref,
    wide_in, wide_up, narrow_hidden, narrow_delta, own_delta,
    taps_in, taps_up, taps_hidden, taps_delta,
    forward_one, forward_two, back_one, back_two, acc_ref,
):
    slots, side, width = image_ref.shape
    pairs = width // LANES
    half = LANES // 2
    tall = side + 16

    zero = jnp.zeros((half, half), BF16)
    for source, forward, back in ((one_ref, forward_one, back_one), (two_ref, forward_two, back_two)):
        for a in range(3):
            taps = [source[a, b] for b in range(3)]
            left = jnp.concatenate(taps + [zero], axis=0)
            right = jnp.concatenate([zero] + taps, axis=0)
            forward[a * 256 : (a + 1) * 256, :] = jnp.concatenate([left, right], axis=1)
            turned = [source[2 - a, 2 - b] for b in range(3)]
            upper = jnp.concatenate(turned + [zero], axis=1)
            lower = jnp.concatenate([zero] + turned, axis=1)
            back[:, a * 256 : (a + 1) * 256] = jnp.concatenate([upper, lower], axis=0)

    for field, (ref, wide) in enumerate(((image_ref, wide_in), (cotangent_ref, wide_up))):
        wide[...] = jnp.zeros(wide.shape, F32)
        for slot in range(slots):
            present = tissue_ref[0, slot] > 0
            for pair in range(pairs):
                block = ref[slot, :, pair * LANES : (pair + 1) * LANES].astype(F32)
                wide[slot, pair + 1, 16 : 16 + side, :] = jnp.where(present, block, 0.0)
            for direction in range(8):
                link = links_ref[slot, direction]

                @pl.when(link >= 0)
                def _(slot=slot, direction=direction, link=link, field=field, wide=wide):
                    got = halo_ref[link // slots, link % slots, slot, field].astype(F32)
                    if direction == 2:
                        wide[slot, 0, 16 : 16 + side, :] = got
                    elif direction == 3:
                        wide[slot, pairs + 1, 16 : 16 + side, :] = got
                    else:
                        north = direction in (0, 4, 5)
                        row = 14 if north else 16 + side
                        if direction < 2:
                            for pair in range(pairs):
                                wide[slot, pair + 1, row : row + 2, :] = got[2 * pair : 2 * pair + 2, :]
                        else:
                            west = direction in (4, 6)
                            at = 14 if west else 0
                            column = 0 if west else pairs + 1
                            wide[slot, column, row : row + 2, :] = got[at : at + 2, :]

    def spread(field, taps, count, start, rows):
        def step(pair, carry):
            for slot in range(slots):
                for a in range(3):
                    block = field[slot, pair, start + a - 1 : start + a - 1 + rows, :].astype(BF16)
                    taps[slot, pair + 1, :, a * 256 : a * 256 + LANES] = block
                    taps[slot, pair, :, a * 256 + LANES : (a + 1) * 256] = block
            return carry

        lax.fori_loop(0, count, step, 0)

    spread(wide_in, taps_in, pairs + 2, 8, tall)
    spread(wide_up, taps_up, pairs + 2, 8, tall)

    row = lax.broadcasted_iota(jnp.int32, (tall, LANES), 0)
    lane = lax.broadcasted_iota(jnp.int32, (tall, LANES), 1)

    def column_mask(north, here, south):
        value = jnp.where(row == 7, north, jnp.where(row == 8 + side, south, here))
        return jnp.where((row >= 7) & (row <= 8 + side), value, 0)

    def across(taps, slot, count, rows):
        return taps[slot, 1 : count + 1].reshape(count * rows, 768)

    contract_last = (((1,), (1,)), ((), ()))
    for slot in range(slots):
        there = [(links_ref[slot, k] >= 0).astype(jnp.int32) for k in range(8)]
        own = tissue_ref[0, slot]
        middle = column_mask(there[0], own, there[1])
        west = jnp.where(lane < half, column_mask(there[4], there[2], there[6]), middle)
        east = jnp.where(lane < half, middle, column_mask(there[5], there[3], there[7]))
        inside = (row >= 8) & (row < 8 + side)

        first = jnp.dot(
            across(taps_in, slot, pairs + 1, tall), forward_one[...], preferred_element_type=F32
        )
        acc_ref[0] = first.reshape(pairs + 1, tall, LANES)
        second = lax.dot_general(
            across(taps_up, slot, pairs + 1, tall), back_two[...], contract_last,
            preferred_element_type=F32,
        )
        acc_ref[1] = second.reshape(pairs + 1, tall, LANES)

        def finish(pair, mask, own_mask, slot=slot):
            hidden = jnp.where(mask > 0, jnp.maximum(acc_ref[0, pair], 0.0), 0.0)
            hidden = hidden.astype(BF16).astype(F32)
            delta = jnp.where(hidden > 0, acc_ref[1, pair], 0.0)
            narrow_hidden[slot, pair] = hidden
            narrow_delta[slot, pair] = delta
            own_delta[slot, pair] = jnp.where(own_mask, delta, 0.0).astype(BF16)

        finish(0, west, inside & (lane >= half))
        finish(pairs, east, inside & (lane < half))

        def middle_step(pair, carry, middle=middle, inside=inside):
            finish(pair, middle, inside)
            return carry

        lax.fori_loop(1, pairs, middle_step, 0)

    spread(narrow_hidden, taps_hidden, pairs + 1, 8, side)
    spread(narrow_delta, taps_delta, pairs + 1, 8, side)

    first_grad = None
    second_grad = None
    contract_first = (((0,), (0,)), ((), ()))
    for slot in range(slots):
        out = jnp.dot(across(taps_hidden, slot, pairs, side), forward_two[...], preferred_element_type=F32)
        back = lax.dot_general(
            across(taps_delta, slot, pairs, side), back_one[...], contract_last, preferred_element_type=F32
        )
        for pair in range(pairs):
            lanes = slice(pair * LANES, (pair + 1) * LANES)
            rows = slice(pair * side, (pair + 1) * side)
            output_ref[slot, :, lanes] = out[rows].astype(BF16)
            grad_input_ref[slot, :, lanes] = back[rows].astype(BF16)
        upstream = wide_up[slot, 1 : pairs + 1, 16 : 16 + side, :].reshape(pairs * side, LANES)
        term_two = lax.dot_general(
            upstream.astype(BF16), across(taps_hidden, slot, pairs, side), contract_first,
            preferred_element_type=F32,
        )
        deltas = own_delta[slot].reshape((pairs + 1) * tall, LANES)
        term_one = lax.dot_general(
            deltas, across(taps_in, slot, pairs + 1, tall), contract_first, preferred_element_type=F32
        )
        first_grad = term_one if first_grad is None else first_grad + term_one
        second_grad = term_two if second_grad is None else second_grad + term_two

    total = grads_ref.shape[0]
    lane = lax.broadcasted_iota(jnp.int32, (192, LANES), 1)
    for a in range(3):
        lanes = slice(a * 256, (a + 1) * 256)
        one = first_grad[:, lanes].T
        two = second_grad[:, lanes].T
        left = one[0:192] + pltpu.roll(one[64:256], half, 1)
        right = pltpu.roll(two[0:192], half, 1) + two[64:256]
        grads_ref[a * 192 : (a + 1) * 192, :] = jnp.where(lane < half, left, right)
    if total > 576:
        grads_ref[576:total, :] = jnp.zeros((total - 576, LANES), F32)


def local(slide_image, cotangent, weight_one, weight_two, tissue, neighbours):
    devices_tile = lax.axis_size("tile")
    devices = devices_tile * lax.axis_size("slide")
    _, slots, side, width = slide_image.shape
    pairs = width // LANES
    tall = side + 16
    image, upstream = slide_image[0], cotangent[0]
    links = neighbours[0]
    packed = pl.pallas_call(
        pack_kernel,
        out_shape=jax.ShapeDtypeStruct((devices_tile, slots, slots, 2, 32, LANES), BF16),
        in_specs=[SMEM, VMEM, VMEM],
        out_specs=VMEM,
        scratch_shapes=[pltpu.VMEM((slots, 2, 2, 32, LANES), F32)],
        compiler_params=pltpu.CompilerParams(vmem_limit_bytes=48 * 2**20),
        name="pack",
    )(links, image, upstream)
    halo = lax.all_to_all(packed, "tile", 0, 0, tiled=True)

    chunk = -(-576 // devices)
    chunk = -(-chunk // 8) * 8
    total = chunk * devices
    output, grad_input, grads = pl.pallas_call(
        mix_kernel,
        out_shape=(
            jax.ShapeDtypeStruct((slots, side, width), BF16),
            jax.ShapeDtypeStruct((slots, side, width), BF16),
            jax.ShapeDtypeStruct((total, LANES), F32),
        ),
        in_specs=[SMEM, SMEM] + [VMEM] * 5,
        out_specs=(VMEM,) * 3,
        scratch_shapes=[
            pltpu.VMEM((slots, pairs + 2, side + 32, LANES), F32),
            pltpu.VMEM((slots, pairs + 2, side + 32, LANES), F32),
            pltpu.VMEM((slots, pairs + 1, tall, LANES), F32),
            pltpu.VMEM((slots, pairs + 1, tall, LANES), F32),
            pltpu.VMEM((slots, pairs + 1, tall, LANES), BF16),
            pltpu.VMEM((slots, pairs + 3, tall, 768), BF16),
            pltpu.VMEM((slots, pairs + 3, tall, 768), BF16),
            pltpu.VMEM((slots, pairs + 2, side, 768), BF16),
            pltpu.VMEM((slots, pairs + 2, side, 768), BF16),
            pltpu.VMEM((768, LANES), BF16),
            pltpu.VMEM((768, LANES), BF16),
            pltpu.VMEM((LANES, 768), BF16),
            pltpu.VMEM((LANES, 768), BF16),
            pltpu.VMEM((2, pairs + 1, tall, LANES), F32),
        ],
        compiler_params=pltpu.CompilerParams(vmem_limit_bytes=48 * 2**20),
        name="mix",
    )(links, tissue, image, upstream, halo, weight_one, weight_two)

    parts = lax.all_to_all(grads.reshape(devices, chunk, LANES), ("slide", "tile"), 0, 0, tiled=True)
    mine = jnp.sum(parts, axis=0)
    whole = lax.all_gather(mine, ("slide", "tile"), axis=0, tiled=True)[:576]
    shape = weight_one.shape
    return (
        output[None],
        grad_input[None],
        whole[:, : LANES // 2].reshape(shape),
        whole[:, LANES // 2 :].reshape(shape),
    )


def solution(mesh):
    placed = (
        P("slide", "tile", None, None),
        P("slide", "tile", None, None),
        P(),
        P(),
        P("slide", "tile"),
        P("slide", "tile", None),
    )
    return jax.shard_map(
        local,
        mesh=mesh,
        in_specs=placed,
        out_specs=(P("slide", "tile", None, None), P("slide", "tile", None, None), P(), P()),
        check_vma=False,
    )
```

time: 414 us -> 117 us (0.28)
  waiting for transfers between devices: 234 us -> 0 us
  blocking collectives: 0 us -> 105 us
  starting transfers between devices: 92.7 us -> 0 us
  local copies, waits for them, and re-layouts: 44.7 us -> 3.48 us
  between operations: 15.7 us -> 0.69 us
  matrix products: 13.8 us -> 0 us
  other arithmetic: 11.1 us -> 0.04 us
  Pallas kernels: 0 us -> 7.39 us
    psum x1 -> x0, waiting for transfers between devices: 126 us -> none  [local(): grad_one, grad_two = lax.psum((grad_one, grad_two), ('slide', 'tile'))]
    ppermute x40 -> x0, waiting for transfers between devices: 109 us -> none  [from_behind(): lax.ppermute(value, axis, [(source, source + steps) for source in range(l...]
    ppermute x40 -> x0, starting transfers between devices: 92.6 us -> none  [from_behind(): lax.ppermute(value, axis, [(source, source + steps) for source in range(l...]
    all_gather x0 -> x1, blocking collectives: none -> 66.6 us  [local(): whole = lax.all_gather(mine, ('slide', 'tile'), axis=0, tiled=True)[:576]]
    all_to_all x0 -> x2, blocking collectives: none -> 38.7 us  [the longest x1 21.7 us: local(): halo = lax.all_to_all(packed, 'tile', 0, 0, tiled=True)]
    unnamed x110 -> x12, local copies, waits for them, and re-layouts: 24.1 us -> 2.59 us
    another operation x54 -> x0, local copies, waits for them, and re-layouts: 8.32 us -> none  [the longest x36 4.19 us: edge_strips(): jnp.stack([blocks[:, 0], blocks[:, -1], blocks[:, :, 0], blocks[:, :, -1]...]
    dot_general x18 -> x0, matrix products: 7.82 us -> none  [weight_grad(): jnp.einsum('nijc,nijo->co', window, delta_field, preferred_element_type=j...]
  transfers between devices with their start and end apart: 41 -> 0, of which waited for: 28 -> 0; matrix products, arithmetic and copies ran while one was open for 6% -> 0% of each run, Pallas kernels for 0% -> 0%
where the time goes in v1:
time: 117 us
  blocking collectives  105 us (90%)
  Pallas kernels  7.39 us (6%)
  local copies, waits for them, and re-layouts  3.48 us (3%)
    all_gather x1, blocking collectives, local(): whole = lax.all_gather(mine, ('slide', 'tile'), axis=0, tiled=True)[:576]  66.6 us
    all_to_all x1, blocking collectives, local(): halo = lax.all_to_all(packed, 'tile', 0, 0, tiled=True)  21.7 us
    all_to_all x1, blocking collectives, local(): lax.all_to_all(grads.reshape(devices, chunk, LANES), ('slide', 'tile'), 0...  17 us
    pallas_call x1, Pallas kernels, local(): pl.pallas_call(mix_kernel, out_shape=(jax.ShapeDtypeStruct((slots, side,...  6.66 us
    unnamed x12, local copies, waits for them, and re-layouts  2.59 us

profile of v1, /device:TPU:0, one launch (start us, length us, event | category | flops | bytes accessed | tf_op | source)
XLA Modules:
  0.0 117.0 jit_solution(13437949563556697039)
XLA Ops:
  0.6 0.0 copy-start.4
  0.6 0.7 copy-done.4
  1.3 0.0 copy-start
  1.3 0.9 copy-done
  2.3 0.0 copy-start.1
  2.3 0.9 copy-done.1
  3.2 0.7 pack.1
  3.9 0.0 copy-start.2
  4.0 0.0 copy-start.3
  4.0 0.0 copy-start.5
  4.0 21.7 %all_to_all.10.halo_ref = bf16[8,2,2,2,32,128]{5,4,3,2,1,0:T(8,128)(2,1)S(1)} all-to-all(bf16[8,2,2,2,32,128]{5,4,3,2,1,0:T(8,128)(2,1)S(1)} %pack.1), channel_id=1, replica_groups=mesh['slide'=4,'tile'=8] {'tile'}, dimensions={0} | all-to-all | bytes 1048576 | tf_op jit(solution)/shard_map/all_to_all | solution.py:223
  25.7 0.0 copy-done.2
  25.7 0.0 copy-done.3
  25.7 0.0 copy-done.5
  25.7 6.7 %mix.1 = (bf16[2,32,2048]{2,1,0:T(8,128)(2,1)}, bf16[2,32,2048]{2,1,0:T(8,128)(2,1)}, f32[768,128]{1,0:T(8,128)S(1)}) custom-call(s32[2,8]{1,0:T(2,128)S(1)} %bitcast.14, s32[1,2]{1,0:T(1,128)S(1)} %copy-done.5, bf16[2,32,2048]{2,1,0:T(8,128)(2,1)S(1)} %bitcast.9, bf16[2,32,2048]{2,1,0:T(8,128)(2,1)S(1)} %bitcast.11, ...), custom_call_target="tpu_custom_call" | custom-call | tf_op jit(solution)/shard_map/mix/pallas_call | solution.py:228
  32.4 17.0 %all_to_all.11 = f32[32,24,128]{2,1,0:T(8,128)S(1)} all-to-all(f32[32,24,128]{2,1,0:T(8,128)S(1)} %bitcast.12), channel_id=1, replica_groups=mesh['slide'=4,'tile'=8] {'slide','tile'}, dimensions={0} | all-to-all | bytes 786432 | tf_op jit(solution)/shard_map/all_to_all | solution.py:257
  49.4 66.6 %all_gather.3 = f32[768,128]{1,0:T(8,128)S(1)} all-gather(f32[24,128]{1,0:T(8,128)S(1)} %reduce_sum.9), channel_id=1, replica_groups=mesh['slide'=4,'tile'=8] {'slide','tile'}, dimensions={0}, use_global_device_ids=true | all-gather | bytes 405504 | tf_op jit(solution)/shard_map/all_gather | solution.py:259
  116.1 0.9 fusion
  (1 shorter events, 0.0 us)
Async XLA Ops:
  0.6 0.7 copy-start.4
  1.3 0.9 copy-start
  2.3 0.9 copy-start.1
  3.9 21.7 %copy-start.2 = (bf16[3,3,64,64]{3,2,1,0:T(8,128)(2,1)S(1)}, bf16[3,3,64,64]{3,2,1,0:T(8,128)(2,1)}, u32[]{:S(2)}) copy-start(bf16[3,3,64,64]{3,2,1,0:T(8,128)(2,1)} %one_ref.1) | copy-start | bytes 221188
  4.0 21.7 %copy-start.3 = (bf16[3,3,64,64]{3,2,1,0:T(8,128)(2,1)S(1)}, bf16[3,3,64,64]{3,2,1,0:T(8,128)(2,1)}, u32[]{:S(2)}) copy-start(bf16[3,3,64,64]{3,2,1,0:T(8,128)(2,1)} %two_ref.1) | copy-start | bytes 221188
  4.0 21.7 %copy-start.5 = (s32[1,2]{1,0:T(1,128)S(1)}, s32[1,2]{1,0:T(1,128)}, u32[]{:S(2)}) copy-start(s32[1,2]{1,0:T(1,128)} %tissue_ref.1) | copy-start | bytes 28

commit v2 on v1

--- a/solution.py
+++ b/solution.py
@@ -14,9 +14,26 @@
 VMEM = pl.BlockSpec(memory_space=pltpu.VMEM)
 
 
-def pack_kernel(links_ref, image_ref, cotangent_ref, out_ref, strip_ref):
+CORNERS = 192
+BLOCK = CORNERS + 16
+
+
+def strip_row(field, slot):
+    return field * 96 + slot * 32
+
+
+def column_row(field):
+    return field * 96 + 64
+
+
+def corner_row(field, slot, there):
+    return 2 * ((field * 2 + slot) * 2 + there)
+
+
+def pack_kernel(links_ref, image_ref, cotangent_ref, out_ref, strip_ref, corner_ref):
     slots, side, width = image_ref.shape
     pairs = width // LANES
+    me = lax.axis_index("tile")
     for slot in range(slots):
         for field, ref in enumerate((image_ref, cotangent_ref)):
             top = ref[slot, 0:16, :].astype(F32)
@@ -36,17 +53,28 @@
                 there = link % slots
                 for field, ref in enumerate((image_ref, cotangent_ref)):
                     if direction < 2:
-                        strip = strip_ref[slot, field, direction].astype(BF16)
-                        out_ref[device, slot, there, field] = strip
-                    elif direction == 2:
-                        out_ref[device, slot, there, field] = ref[slot, :, 0:LANES]
-                    elif direction == 3:
-                        out_ref[device, slot, there, field] = ref[slot, :, width - LANES : width]
+                        rows = slice(strip_row(field, slot), strip_row(field, slot) + 32)
+                        out_ref[device, rows, :] = strip_ref[slot, field, direction].astype(BF16)
+                    elif direction < 4:
+                        first = jnp.where(device == me, strip_row(field, slot), column_row(field))
+                        lanes = slice(0, LANES) if direction == 2 else slice(width - LANES, width)
+                        out_ref[device, pl.ds(pl.multiple_of(first, 32), 32), :] = ref[slot, :, lanes]
                     else:
                         which = 0 if direction < 6 else 1
-                        first = 0 if direction % 2 == 0 else side - 16
-                        corner = strip_ref[slot, field, which, first : first + 16, :]
-                        out_ref[device, slot, there, field, 0:16, :] = corner.astype(BF16)
+                        first = 0 if direction % 2 == 0 else side - 2
+                        corner = strip_ref[slot, field, which, first : first + 2, :]
+                        for target in range(slots):
+                            row = corner_row(field, slot, target)
+
+                            @pl.when(there == target)
+                            def _(row=row, corner=corner):
+                                corner_ref[device, row : row + 2, :] = corner
+
+    def place(device, carry):
+        out_ref[device, CORNERS:BLOCK, :] = corner_ref[device].astype(BF16)
+        return carry
+
+    lax.fori_loop(0, out_ref.shape[0], place, 0)
 
 
 def mix_kernel(
@@ -60,6 +88,7 @@
     pairs = width // LANES
     half = LANES // 2
     tall = side + 16
+    me = lax.axis_index("tile")
 
     zero = jnp.zeros((half, half), BF16)
     for source, forward, back in ((one_ref, forward_one, back_one), (two_ref, forward_two, back_two)):
@@ -85,22 +114,26 @@
 
                 @pl.when(link >= 0)
                 def _(slot=slot, direction=direction, link=link, field=field, wide=wide):
-                    got = halo_ref[link // slots, link % slots, slot, field].astype(F32)
-                    if direction == 2:
-                        wide[slot, 0, 16 : 16 + side, :] = got
-                    elif direction == 3:
-                        wide[slot, pairs + 1, 16 : 16 + side, :] = got
+                    device, there = link // slots, link % slots
+                    if direction in (2, 3):
+                        column = 0 if direction == 2 else pairs + 1
+                        at_home = strip_row(field, 0) + there * 32
+                        first = pl.multiple_of(jnp.where(device == me, at_home, column_row(field)), 32)
+                        got = halo_ref[device, pl.ds(first, 32), :].astype(F32)
+                        wide[slot, column, 16 : 16 + side, :] = got
                     else:
-                        north = direction in (0, 4, 5)
-                        row = 14 if north else 16 + side
+                        row = 14 if direction in (0, 4, 5) else 16 + side
                         if direction < 2:
+                            at = pl.multiple_of(strip_row(field, 0) + there * 32, 32)
+                            got = halo_ref[device, pl.ds(at, 32), :].astype(F32)
                             for pair in range(pairs):
                                 wide[slot, pair + 1, row : row + 2, :] = got[2 * pair : 2 * pair + 2, :]
                         else:
-                            west = direction in (4, 6)
-                            at = 14 if west else 0
-                            column = 0 if west else pairs + 1
-                            wide[slot, column, row : row + 2, :] = got[at : at + 2, :]
+                            column = 0 if direction in (4, 6) else pairs + 1
+                            got = halo_ref[device, CORNERS:BLOCK, :].astype(F32)
+                            one, two = (corner_row(field, k, slot) for k in range(2))
+                            corner = jnp.where(there == 0, got[one : one + 2], got[two : two + 2])
+                            wide[slot, column, row : row + 2, :] = corner
 
     def spread(field, taps, count, start, rows):
         def step(pair, carry):
@@ -198,9 +231,23 @@
         two = second_grad[:, lanes].T
         left = one[0:192] + pltpu.roll(one[64:256], half, 1)
         right = pltpu.roll(two[0:192], half, 1) + two[64:256]
-        grads_ref[a * 192 : (a + 1) * 192, :] = jnp.where(lane < half, left, right)
+        grads_ref[a * 192 : (a + 1) * 192, :] = jnp.where(lane < half, left, right).astype(BF16)
     if total > 576:
-        grads_ref[576:total, :] = jnp.zeros((total - 576, LANES), F32)
+        grads_ref[576:total, :] = jnp.zeros((total - 576, LANES), BF16)
+
+
+def sum_kernel(parts_ref, sums_ref):
+    total = jnp.sum(parts_ref[...].astype(F32), axis=0).astype(BF16)
+    sums_ref[...] = jnp.broadcast_to(total[None], sums_ref.shape)
+
+
+def split_kernel(whole_ref, one_ref, two_ref):
+    chunk = whole_ref.shape[1]
+    rows, half = one_ref.shape
+    for part in range(rows // chunk):
+        block = whole_ref[part].astype(F32)
+        one_ref[part * chunk : (part + 1) * chunk, :] = block[:, :half]
+        two_ref[part * chunk : (part + 1) * chunk, :] = block[:, half:]
 
 
 def local(slide_image, cotangent, weight_one, weight_two, tissue, neighbours):
@@ -213,10 +260,13 @@
     links = neighbours[0]
     packed = pl.pallas_call(
         pack_kernel,
-        out_shape=jax.ShapeDtypeStruct((devices_tile, slots, slots, 2, 32, LANES), BF16),
+        out_shape=jax.ShapeDtypeStruct((devices_tile, BLOCK, LANES), BF16),
         in_specs=[SMEM, VMEM, VMEM],
         out_specs=VMEM,
-        scratch_shapes=[pltpu.VMEM((slots, 2, 2, 32, LANES), F32)],
+        scratch_shapes=[
+            pltpu.VMEM((slots, 2, 2, 32, LANES), F32),
+            pltpu.VMEM((devices_tile, 16, LANES), F32),
+        ],
         compiler_params=pltpu.CompilerParams(vmem_limit_bytes=48 * 2**20),
         name="pack",
     )(links, image, upstream)
@@ -230,7 +280,7 @@
         out_shape=(
             jax.ShapeDtypeStruct((slots, side, width), BF16),
             jax.ShapeDtypeStruct((slots, side, width), BF16),
-            jax.ShapeDtypeStruct((total, LANES), F32),
+            jax.ShapeDtypeStruct((total, LANES), BF16),
         ),
         in_specs=[SMEM, SMEM] + [VMEM] * 5,
         out_specs=(VMEM,) * 3,
@@ -255,15 +305,23 @@
     )(links, tissue, image, upstream, halo, weight_one, weight_two)
 
     parts = lax.all_to_all(grads.reshape(devices, chunk, LANES), ("slide", "tile"), 0, 0, tiled=True)
-    mine = jnp.sum(parts, axis=0)
-    whole = lax.all_gather(mine, ("slide", "tile"), axis=0, tiled=True)[:576]
+    sums = pl.pallas_call(
+        sum_kernel,
+        out_shape=jax.ShapeDtypeStruct(parts.shape, BF16),
+        in_specs=[VMEM],
+        out_specs=VMEM,
+        name="sum",
+    )(parts)
+    whole = lax.all_to_all(sums, ("slide", "tile"), 0, 0, tiled=True)
+    grad_one, grad_two = pl.pallas_call(
+        split_kernel,
+        out_shape=(jax.ShapeDtypeStruct((576, LANES // 2), F32),) * 2,
+        in_specs=[VMEM],
+        out_specs=(VMEM, VMEM),
+        name="split",
+    )(whole)
     shape = weight_one.shape
-    return (
-        output[None],
-        grad_input[None],
-        whole[:, : LANES // 2].reshape(shape),
-        whole[:, LANES // 2 :].reshape(shape),
-    )
+    return output[None], grad_input[None], grad_one.reshape(shape), grad_two.reshape(shape)
 
 
 def solution(mesh):

time: 117 us -> 58.1 us (0.50)
  blocking collectives: 105 us -> 43.6 us
  Pallas kernels: 7.39 us -> 10.9 us
    all_gather x1 -> x0, blocking collectives: 66.6 us -> none  [local(): whole = lax.all_gather(mine, ('slide', 'tile'), axis=0, tiled=True)[:576]]
    all_to_all x0 -> x1, blocking collectives: none -> 11.8 us  [local(): whole = lax.all_to_all(sums, ('slide', 'tile'), 0, 0, tiled=True)]
    all_to_all x1, blocking collectives: 17 us -> 11.9 us  [local(): lax.all_to_all(grads.reshape(devices, chunk, LANES), ('slide', 'tile'), 0...]
    pallas_call x0 -> x2, Pallas kernels: none -> 3.41 us  [the longest x1 1.76 us: local(): pl.pallas_call(split_kernel, out_shape=(jax.ShapeDtypeStruct((576, LANES...]
    all_to_all x1, blocking collectives: 21.7 us -> 19.9 us  [local(): halo = lax.all_to_all(packed, 'tile', 0, 0, tiled=True)]
where the time goes in v2:
time: 58.1 us; the launch traced here: 57.8 us
  blocking collectives  43.6 us (75%)
  Pallas kernels  10.9 us (19%)
  local copies, waits for them, and re-layouts  2.59 us (4%)
  between operations  0.69 us (1%)
    all_to_all x1, blocking collectives, local(): halo = lax.all_to_all(packed, 'tile', 0, 0, tiled=True)  19.9 us
    all_to_all x1, blocking collectives, local(): lax.all_to_all(grads.reshape(devices, chunk, LANES), ('slide', 'tile'), 0...  11.9 us
    all_to_all x1, blocking collectives, local(): whole = lax.all_to_all(sums, ('slide', 'tile'), 0, 0, tiled=True)  11.8 us
    pallas_call x1, Pallas kernels, local(): pl.pallas_call(mix_kernel, out_shape=(jax.ShapeDtypeStruct((slots, side,...  6.67 us
    unnamed x12, local copies, waits for them, and re-layouts  2.59 us
    pallas_call x1, Pallas kernels, local(): pl.pallas_call(split_kernel, out_shape=(jax.ShapeDtypeStruct((576, LANES...  1.76 us
    pallas_call x1, Pallas kernels, local(): pl.pallas_call(sum_kernel, out_shape=jax.ShapeDtypeStruct(parts.shape, BF...  1.65 us

profile of v2, /device:TPU:0, one launch (start us, length us, event | category | flops | bytes accessed | tf_op | source)
XLA Modules:
  0.0 57.8 jit_solution(6081713580013891898)
XLA Ops:
  0.6 0.0 copy-start.4
  0.6 0.7 %copy-done.4 = s32[1,2,8]{2,1,0:T(2,128)S(1)} copy-done((s32[1,2,8]{2,1,0:T(2,128)S(1)}, s32[1,2,8]{2,1,0:T(2,128)}, u32[]{:S(2)}) %copy-start.4) | copy-done | bytes 88
  1.3 0.0 copy-start
  1.3 0.9 %copy-done = bf16[1,2,32,2048]{3,2,1,0:T(8,128)(2,1)S(1)} copy-done((bf16[1,2,32,2048]{3,2,1,0:T(8,128)(2,1)S(1)}, bf16[1,2,32,2048]{3,2,1,0:T(8,128)(2,1)}, u32[]{:S(2)}) %copy-start) | copy-done | bytes 262168
  2.3 0.0 copy-start.1
  2.3 0.9 %copy-done.1 = bf16[1,2,32,2048]{3,2,1,0:T(8,128)(2,1)S(1)} copy-done((bf16[1,2,32,2048]{3,2,1,0:T(8,128)(2,1)S(1)}, bf16[1,2,32,2048]{3,2,1,0:T(8,128)(2,1)}, u32[]{:S(2)}) %copy-start.1) | copy-done | bytes 262168
  3.2 0.8 %pack.1 = bf16[8,208,128]{2,1,0:T(8,128)(2,1)S(1)} custom-call(s32[2,8]{1,0:T(2,128)S(1)} %bitcast.13, bf16[2,32,2048]{2,1,0:T(8,128)(2,1)S(1)} %bitcast.8, bf16[2,32,2048]{2,1,0:T(8,128)(2,1)S(1)} %bitcast.10), custom_call_target="tpu_custom_call" | custom-call | tf_op jit(solution)/shard_map/pack/pallas_call | solution.py:261
  4.0 0.0 copy-start.2
  4.0 0.0 copy-start.3
  4.0 0.0 copy-start.5
  4.0 19.9 %all_to_all.15.halo_ref = bf16[8,208,128]{2,1,0:T(8,128)(2,1)S(1)} all-to-all(bf16[8,208,128]{2,1,0:T(8,128)(2,1)S(1)} %pack.1), channel_id=1, replica_groups=mesh['slide'=4,'tile'=8] {'tile'}, dimensions={0} | all-to-all | bytes 851968 | tf_op jit(solution)/shard_map/all_to_all | solution.py:273
  23.9 0.0 copy-done.2
  23.9 0.0 copy-done.3
  23.9 0.0 copy-done.5
  23.9 6.7 %mix.1 = (bf16[2,32,2048]{2,1,0:T(8,128)(2,1)}, bf16[2,32,2048]{2,1,0:T(8,128)(2,1)}, bf16[768,128]{1,0:T(8,128)(2,1)S(1)}) custom-call(s32[2,8]{1,0:T(2,128)S(1)} %bitcast.14, s32[1,2]{1,0:T(1,128)S(1)} %copy-done.5, bf16[2,32,2048]{2,1,0:T(8,128)(2,1)S(1)} %bitcast.9, bf16[2,32,2048]{2,1,0:T(8,128)(2,1)S(1)} %bitcast.11, ...), custom_call_target="tpu_custom_call" | custom-call | tf_op jit(solution)/shard_map/mix/pallas_call | solution.py:278
  30.6 11.9 %all_to_all.16.parts_ref = bf16[32,24,128]{2,1,0:T(8,128)(2,1)} all-to-all(bf16[32,24,128]{2,1,0:T(8,128)(2,1)S(1)} %bitcast.12), channel_id=1, replica_groups=mesh['slide'=4,'tile'=8] {'slide','tile'}, dimensions={0} | all-to-all | bytes 393216 | tf_op jit(solution)/shard_map/all_to_all | solution.py:307
  42.5 1.7 %sum.1 = bf16[32,24,128]{2,1,0:T(8,128)(2,1)} custom-call(bf16[32,24,128]{2,1,0:T(8,128)(2,1)} %all_to_all.16.parts_ref), custom_call_target="tpu_custom_call" | custom-call | tf_op jit(solution)/shard_map/sum/pallas_call | solution.py:308
  44.2 11.8 %all_to_all.17.whole_ref = bf16[32,24,128]{2,1,0:T(8,128)(2,1)} all-to-all(bf16[32,24,128]{2,1,0:T(8,128)(2,1)} %sum.1), channel_id=1, replica_groups=mesh['slide'=4,'tile'=8] {'slide','tile'}, dimensions={0} | all-to-all | bytes 393216 | tf_op jit(solution)/shard_map/all_to_all | solution.py:315
  56.0 1.8 %split.1 = (f32[576,64]{1,0:T(8,128)}, f32[576,64]{1,0:T(8,128)}) custom-call(bf16[32,24,128]{2,1,0:T(8,128)(2,1)} %all_to_all.17.whole_ref), custom_call_target="tpu_custom_call" | custom-call | tf_op jit(solution)/shard_map/split/pallas_call | solution.py:316
Async XLA Ops:
  0.6 0.7 %copy-start.4 = (s32[1,2,8]{2,1,0:T(2,128)S(1)}, s32[1,2,8]{2,1,0:T(2,128)}, u32[]{:S(2)}) copy-start(s32[1,2,8]{2,1,0:T(2,128)} %param.11) | copy-start | bytes 196
  1.3 0.9 %copy-start = (bf16[1,2,32,2048]{3,2,1,0:T(8,128)(2,1)S(1)}, bf16[1,2,32,2048]{3,2,1,0:T(8,128)(2,1)}, u32[]{:S(2)}) copy-start(bf16[1,2,32,2048]{3,2,1,0:T(8,128)(2,1)} %param.6) | copy-start | bytes 786436
  2.3 0.9 %copy-start.1 = (bf16[1,2,32,2048]{3,2,1,0:T(8,128)(2,1)S(1)}, bf16[1,2,32,2048]{3,2,1,0:T(8,128)(2,1)}, u32[]{:S(2)}) copy-start(bf16[1,2,32,2048]{3,2,1,0:T(8,128)(2,1)} %param.7) | copy-start | bytes 786436
  4.0 19.9 %copy-start.2 = (bf16[3,3,64,64]{3,2,1,0:T(8,128)(2,1)S(1)}, bf16[3,3,64,64]{3,2,1,0:T(8,128)(2,1)}, u32[]{:S(2)}) copy-start(bf16[3,3,64,64]{3,2,1,0:T(8,128)(2,1)} %one_ref.1) | copy-start | bytes 221188
  4.0 19.9 %copy-start.3 = (bf16[3,3,64,64]{3,2,1,0:T(8,128)(2,1)S(1)}, bf16[3,3,64,64]{3,2,1,0:T(8,128)(2,1)}, u32[]{:S(2)}) copy-start(bf16[3,3,64,64]{3,2,1,0:T(8,128)(2,1)} %two_ref.1) | copy-start | bytes 221188
  4.0 19.9 %copy-start.5 = (s32[1,2]{1,0:T(1,128)S(1)}, s32[1,2]{1,0:T(1,128)}, u32[]{:S(2)}) copy-start(s32[1,2]{1,0:T(1,128)} %tissue_ref.1) | copy-start | bytes 28

commit v3 on v2

--- a/solution.py
+++ b/solution.py
@@ -12,6 +12,8 @@
 LANES = 128
 SMEM = pl.BlockSpec(memory_space=pltpu.SMEM)
 VMEM = pl.BlockSpec(memory_space=pltpu.VMEM)
+ANY = pl.BlockSpec(memory_space=pl.ANY)
+PACK_LIMIT = 60 * 2**20
 
 
 CORNERS = 192
@@ -30,7 +32,34 @@
     return 2 * ((field * 2 + slot) * 2 + there)
 
 
-def pack_kernel(links_ref, image_ref, cotangent_ref, out_ref, strip_ref, corner_ref):
+def band_weights(source, forward, back):
+    half = LANES // 2
+    zero = jnp.zeros((half, half), BF16)
+    for a in range(3):
+        taps = [source[a, b] for b in range(3)]
+        left = jnp.concatenate(taps + [zero], axis=0)
+        right = jnp.concatenate([zero] + taps, axis=0)
+        forward[a * 256 : (a + 1) * 256, :] = jnp.concatenate([left, right], axis=1)
+        turned = [source[2 - a, 2 - b] for b in range(3)]
+        upper = jnp.concatenate(turned + [zero], axis=1)
+        lower = jnp.concatenate([zero] + turned, axis=1)
+        back[:, a * 256 : (a + 1) * 256] = jnp.concatenate([upper, lower], axis=0)
+
+
+def pack_kernel(
+    links_hbm, image_hbm, cotangent_hbm, out_ref,
+    links_ref, image_ref, cotangent_ref, strip_ref, corner_ref, sems,
+):
+    sources = (links_hbm, image_hbm, cotangent_hbm)
+    targets = (links_ref, image_ref, cotangent_ref)
+    copies = [
+        pltpu.make_async_copy(source, target, sems.at[k])
+        for k, (source, target) in enumerate(zip(sources, targets))
+    ]
+    for copy in copies:
+        copy.start()
+    for copy in copies:
+        copy.wait()
     slots, side, width = image_ref.shape
     pairs = width // LANES
     me = lax.axis_index("tile")
@@ -79,10 +108,9 @@
 
 def mix_kernel(
     links_ref, tissue_ref, image_ref, cotangent_ref, halo_ref, one_ref, two_ref,
-    output_ref, grad_input_ref, grads_ref,
+    output_hbm, grad_input_hbm, grads_ref,
     wide_in, wide_up, narrow_hidden, narrow_delta, own_delta,
-    taps_in, taps_up, taps_hidden, taps_delta,
-    forward_one, forward_two, back_one, back_two, acc_ref,
+    taps_in, taps_up, taps_hidden, taps_delta, forward_ref, back_ref, acc_ref, output_ref, grad_input_ref, sems,
 ):
     slots, side, width = image_ref.shape
     pairs = width // LANES
@@ -90,20 +118,14 @@
     tall = side + 16
     me = lax.axis_index("tile")
 
-    zero = jnp.zeros((half, half), BF16)
-    for source, forward, back in ((one_ref, forward_one, back_one), (two_ref, forward_two, back_two)):
-        for a in range(3):
-            taps = [source[a, b] for b in range(3)]
-            left = jnp.concatenate(taps + [zero], axis=0)
-            right = jnp.concatenate([zero] + taps, axis=0)
-            forward[a * 256 : (a + 1) * 256, :] = jnp.concatenate([left, right], axis=1)
-            turned = [source[2 - a, 2 - b] for b in range(3)]
-            upper = jnp.concatenate(turned + [zero], axis=1)
-            lower = jnp.concatenate([zero] + turned, axis=1)
-            back[:, a * 256 : (a + 1) * 256] = jnp.concatenate([upper, lower], axis=0)
+    band_weights(one_ref, forward_ref.at[0], back_ref.at[0])
+    band_weights(two_ref, forward_ref.at[1], back_ref.at[1])
 
     for field, (ref, wide) in enumerate(((image_ref, wide_in), (cotangent_ref, wide_up))):
-        wide[...] = jnp.zeros(wide.shape, F32)
+        wide[:, :, 0:16, :] = jnp.zeros((slots, pairs + 2, 16, LANES), F32)
+        wide[:, :, 16 + side : 32 + side, :] = jnp.zeros((slots, pairs + 2, 16, LANES), F32)
+        for column in (0, pairs + 1):
+            wide[:, column, 16 : 16 + side, :] = jnp.zeros((slots, side, LANES), F32)
         for slot in range(slots):
             present = tissue_ref[0, slot] > 0
             for pair in range(pairs):
@@ -144,7 +166,7 @@
                     taps[slot, pair, :, a * 256 + LANES : (a + 1) * 256] = block
             return carry
 
-        lax.fori_loop(0, count, step, 0)
+        lax.fori_loop(0, count, step, 0, unroll=True)
 
     spread(wide_in, taps_in, pairs + 2, 8, tall)
     spread(wide_up, taps_up, pairs + 2, 8, tall)
@@ -169,11 +191,11 @@
         inside = (row >= 8) & (row < 8 + side)
 
         first = jnp.dot(
-            across(taps_in, slot, pairs + 1, tall), forward_one[...], preferred_element_type=F32
+            across(taps_in, slot, pairs + 1, tall), forward_ref[0], preferred_element_type=F32
         )
         acc_ref[0] = first.reshape(pairs + 1, tall, LANES)
         second = lax.dot_general(
-            across(taps_up, slot, pairs + 1, tall), back_two[...], contract_last,
+            across(taps_up, slot, pairs + 1, tall), back_ref[1], contract_last,
             preferred_element_type=F32,
         )
         acc_ref[1] = second.reshape(pairs + 1, tall, LANES)
@@ -193,24 +215,29 @@
             finish(pair, middle, inside)
             return carry
 
-        lax.fori_loop(1, pairs, middle_step, 0)
+        lax.fori_loop(1, pairs, middle_step, 0, unroll=True)
 
     spread(narrow_hidden, taps_hidden, pairs + 1, 8, side)
     spread(narrow_delta, taps_delta, pairs + 1, 8, side)
 
     first_grad = None
     second_grad = None
+    copies = []
     contract_first = (((0,), (0,)), ((), ()))
     for slot in range(slots):
-        out = jnp.dot(across(taps_hidden, slot, pairs, side), forward_two[...], preferred_element_type=F32)
+        out = jnp.dot(across(taps_hidden, slot, pairs, side), forward_ref[1], preferred_element_type=F32)
         back = lax.dot_general(
-            across(taps_delta, slot, pairs, side), back_one[...], contract_last, preferred_element_type=F32
+            across(taps_delta, slot, pairs, side), back_ref[0], contract_last, preferred_element_type=F32
         )
         for pair in range(pairs):
             lanes = slice(pair * LANES, (pair + 1) * LANES)
             rows = slice(pair * side, (pair + 1) * side)
             output_ref[slot, :, lanes] = out[rows].astype(BF16)
             grad_input_ref[slot, :, lanes] = back[rows].astype(BF16)
+        for k, (source, target) in enumerate(((output_ref, output_hbm), (grad_input_ref, grad_input_hbm))):
+            copies.append(pltpu.make_async_copy(source.at[slot], target.at[slot], sems.at[2 * slot + k]))
+            copies[-1].start()
+    for slot in range(slots):
         upstream = wide_up[slot, 1 : pairs + 1, 16 : 16 + side, :].reshape(pairs * side, LANES)
         term_two = lax.dot_general(
             upstream.astype(BF16), across(taps_hidden, slot, pairs, side), contract_first,
@@ -234,11 +261,17 @@
         grads_ref[a * 192 : (a + 1) * 192, :] = jnp.where(lane < half, left, right).astype(BF16)
     if total > 576:
         grads_ref[576:total, :] = jnp.zeros((total - 576, LANES), BF16)
+    for copy in copies:
+        copy.wait()
 
 
 def sum_kernel(parts_ref, sums_ref):
-    total = jnp.sum(parts_ref[...].astype(F32), axis=0).astype(BF16)
-    sums_ref[...] = jnp.broadcast_to(total[None], sums_ref.shape)
+    total = parts_ref[0].astype(F32)
+    for part in range(1, parts_ref.shape[0]):
+        total += parts_ref[part].astype(F32)
+    total = total.astype(BF16)
+    for part in range(parts_ref.shape[0]):
+        sums_ref[part] = total
 
 
 def split_kernel(whole_ref, one_ref, two_ref):
@@ -261,13 +294,17 @@
     packed = pl.pallas_call(
         pack_kernel,
         out_shape=jax.ShapeDtypeStruct((devices_tile, BLOCK, LANES), BF16),
-        in_specs=[SMEM, VMEM, VMEM],
+        in_specs=[ANY] * 3,
         out_specs=VMEM,
         scratch_shapes=[
+            pltpu.SMEM(links.shape, jnp.int32),
+            pltpu.VMEM(image.shape, BF16),
+            pltpu.VMEM(image.shape, BF16),
             pltpu.VMEM((slots, 2, 2, 32, LANES), F32),
             pltpu.VMEM((devices_tile, 16, LANES), F32),
+            pltpu.SemaphoreType.DMA((3,)),
         ],
-        compiler_params=pltpu.CompilerParams(vmem_limit_bytes=48 * 2**20),
+        compiler_params=pltpu.CompilerParams(vmem_limit_bytes=PACK_LIMIT),
         name="pack",
     )(links, image, upstream)
     halo = lax.all_to_all(packed, "tile", 0, 0, tiled=True)
@@ -283,7 +320,7 @@
             jax.ShapeDtypeStruct((total, LANES), BF16),
         ),
         in_specs=[SMEM, SMEM] + [VMEM] * 5,
-        out_specs=(VMEM,) * 3,
+        out_specs=(ANY, ANY, VMEM),
         scratch_shapes=[
             pltpu.VMEM((slots, pairs + 2, side + 32, LANES), F32),
             pltpu.VMEM((slots, pairs + 2, side + 32, LANES), F32),
@@ -294,11 +331,12 @@
             pltpu.VMEM((slots, pairs + 3, tall, 768), BF16),
             pltpu.VMEM((slots, pairs + 2, side, 768), BF16),
             pltpu.VMEM((slots, pairs + 2, side, 768), BF16),
-            pltpu.VMEM((768, LANES), BF16),
-            pltpu.VMEM((768, LANES), BF16),
-            pltpu.VMEM((LANES, 768), BF16),
-            pltpu.VMEM((LANES, 768), BF16),
+            pltpu.VMEM((2, 768, LANES), BF16),
+            pltpu.VMEM((2, LANES, 768), BF16),
             pltpu.VMEM((2, pairs + 1, tall, LANES), F32),
+            pltpu.VMEM((slots, side, width), BF16),
+            pltpu.VMEM((slots, side, width), BF16),
+            pltpu.SemaphoreType.DMA((2 * slots,)),
         ],
         compiler_params=pltpu.CompilerParams(vmem_limit_bytes=48 * 2**20),
         name="mix",

time: 58.1 us -> 55.1 us (0.948)
  local copies, waits for them, and re-layouts: 2.59 us -> 0.04 us
  Pallas kernels: 10.9 us -> 10.2 us
    unnamed x12, local copies, waits for them, and re-layouts: 2.59 us -> 0.04 us
    pallas_call x1, Pallas kernels: 6.67 us -> 4.76 us  [local(): pl.pallas_call(mix_kernel, out_shape=(jax.ShapeDtypeStruct((slots, side,...]
    pallas_call x1, Pallas kernels: 0.78 us -> 2.04 us  [local(): pl.pallas_call(pack_kernel, out_shape=jax.ShapeDtypeStruct((devices_tile,...]
where the time goes in v3:
time: 55.1 us; the launch traced here: 54.7 us
  blocking collectives  43.7 us (79%)
  Pallas kernels  10.2 us (19%)
  between operations  0.72 us (1%)
    all_to_all x1, blocking collectives, local(): halo = lax.all_to_all(packed, 'tile', 0, 0, tiled=True)  20 us
    all_to_all x1, blocking collectives, local(): lax.all_to_all(grads.reshape(devices, chunk, LANES), ('slide', 'tile'), 0...  11.9 us
    all_to_all x1, blocking collectives, local(): whole = lax.all_to_all(sums, ('slide', 'tile'), 0, 0, tiled=True)  11.8 us
    pallas_call x1, Pallas kernels, local(): pl.pallas_call(mix_kernel, out_shape=(jax.ShapeDtypeStruct((slots, side,...  4.76 us
    pallas_call x1, Pallas kernels, local(): pl.pallas_call(pack_kernel, out_shape=jax.ShapeDtypeStruct((devices_tile,...  2.04 us
    pallas_call x1, Pallas kernels, local(): pl.pallas_call(split_kernel, out_shape=(jax.ShapeDtypeStruct((576, LANES...  1.76 us
    pallas_call x1, Pallas kernels, local(): pl.pallas_call(sum_kernel, out_shape=jax.ShapeDtypeStruct(parts.shape, BF...  1.65 us

profile of v3, /device:TPU:0, one launch (start us, length us, event | category | flops | bytes accessed | tf_op | source)
XLA Modules:
  0.0 54.7 jit_solution(8279019008060608719)
XLA Ops:
  0.6 2.0 %pack.1 = bf16[8,208,128]{2,1,0:T(8,128)(2,1)} custom-call(s32[2,8]{1,0:T(2,128)} %bitcast.13, bf16[2,32,2048]{2,1,0:T(8,128)(2,1)} %bitcast.8, bf16[2,32,2048]{2,1,0:T(8,128)(2,1)} %bitcast.10), custom_call_target="tpu_custom_call" | custom-call | tf_op jit(solution)/shard_map/pack/pallas_call | solution.py:294
  2.7 0.0 copy-start
  2.7 0.0 copy-start.1
  2.7 0.0 copy-start.2
  2.7 0.0 copy-start.3
  2.7 0.0 copy-start.4
  2.7 0.0 copy-start.5
  2.7 20.0 %all_to_all.15.halo_ref = bf16[8,208,128]{2,1,0:T(8,128)(2,1)S(1)} all-to-all(bf16[8,208,128]{2,1,0:T(8,128)(2,1)} %pack.1), channel_id=1, replica_groups=mesh['slide'=4,'tile'=8] {'tile'}, dimensions={0} | all-to-all | bytes 851968 | tf_op jit(solution)/shard_map/all_to_all | solution.py:310
  22.8 0.0 copy-done
  22.8 0.0 copy-done.1
  22.8 0.0 copy-done.2
  22.8 0.0 copy-done.3
  22.8 0.0 copy-done.4
  22.8 0.0 copy-done.5
  22.8 4.8 %mix.1 = (bf16[2,32,2048]{2,1,0:T(8,128)(2,1)}, bf16[2,32,2048]{2,1,0:T(8,128)(2,1)}, bf16[768,128]{1,0:T(8,128)(2,1)S(1)}) custom-call(s32[2,8]{1,0:T(2,128)S(1)} %bitcast.14, s32[1,2]{1,0:T(1,128)S(1)} %copy-done.5, bf16[2,32,2048]{2,1,0:T(8,128)(2,1)S(1)} %bitcast.9, bf16[2,32,2048]{2,1,0:T(8,128)(2,1)S(1)} %bitcast.11, ...), custom_call_target="tpu_custom_call" | custom-call | tf_op jit(solution)/shard_map/mix/pallas_call | solution.py:315
  27.6 11.9 %all_to_all.16.parts_ref = bf16[32,24,128]{2,1,0:T(8,128)(2,1)} all-to-all(bf16[32,24,128]{2,1,0:T(8,128)(2,1)S(1)} %bitcast.12), channel_id=1, replica_groups=mesh['slide'=4,'tile'=8] {'slide','tile'}, dimensions={0} | all-to-all | bytes 393216 | tf_op jit(solution)/shard_map/all_to_all | solution.py:345
  39.5 1.7 %sum.1 = bf16[32,24,128]{2,1,0:T(8,128)(2,1)} custom-call(bf16[32,24,128]{2,1,0:T(8,128)(2,1)} %all_to_all.16.parts_ref), custom_call_target="tpu_custom_call" | custom-call | tf_op jit(solution)/shard_map/sum/pallas_call | solution.py:346
  41.1 11.8 %all_to_all.17.whole_ref = bf16[32,24,128]{2,1,0:T(8,128)(2,1)} all-to-all(bf16[32,24,128]{2,1,0:T(8,128)(2,1)} %sum.1), channel_id=1, replica_groups=mesh['slide'=4,'tile'=8] {'slide','tile'}, dimensions={0} | all-to-all | bytes 393216 | tf_op jit(solution)/shard_map/all_to_all | solution.py:353
  53.0 1.8 %split.1 = (f32[576,64]{1,0:T(8,128)}, f32[576,64]{1,0:T(8,128)}) custom-call(bf16[32,24,128]{2,1,0:T(8,128)(2,1)} %all_to_all.17.whole_ref), custom_call_target="tpu_custom_call" | custom-call | tf_op jit(solution)/shard_map/split/pallas_call | solution.py:354
Async XLA Ops:
  2.7 20.1 %copy-start = (bf16[1,2,32,2048]{3,2,1,0:T(8,128)(2,1)S(1)}, bf16[1,2,32,2048]{3,2,1,0:T(8,128)(2,1)}, u32[]{:S(2)}) copy-start(bf16[1,2,32,2048]{3,2,1,0:T(8,128)(2,1)} %param.6) | copy-start | bytes 786436
  2.7 20.1 %copy-start.1 = (bf16[1,2,32,2048]{3,2,1,0:T(8,128)(2,1)S(1)}, bf16[1,2,32,2048]{3,2,1,0:T(8,128)(2,1)}, u32[]{:S(2)}) copy-start(bf16[1,2,32,2048]{3,2,1,0:T(8,128)(2,1)} %param.7) | copy-start | bytes 786436
  2.7 20.1 %copy-start.2 = (bf16[3,3,64,64]{3,2,1,0:T(8,128)(2,1)S(1)}, bf16[3,3,64,64]{3,2,1,0:T(8,128)(2,1)}, u32[]{:S(2)}) copy-start(bf16[3,3,64,64]{3,2,1,0:T(8,128)(2,1)} %one_ref.1) | copy-start | bytes 221188
  2.7 20.1 %copy-start.3 = (bf16[3,3,64,64]{3,2,1,0:T(8,128)(2,1)S(1)}, bf16[3,3,64,64]{3,2,1,0:T(8,128)(2,1)}, u32[]{:S(2)}) copy-start(bf16[3,3,64,64]{3,2,1,0:T(8,128)(2,1)} %two_ref.1) | copy-start | bytes 221188
  2.7 20.1 %copy-start.4 = (s32[1,2,8]{2,1,0:T(2,128)S(1)}, s32[1,2,8]{2,1,0:T(2,128)}, u32[]{:S(2)}) copy-start(s32[1,2,8]{2,1,0:T(2,128)} %param.11) | copy-start | bytes 196
  2.7 20.1 %copy-start.5 = (s32[1,2]{1,0:T(1,128)S(1)}, s32[1,2]{1,0:T(1,128)}, u32[]{:S(2)}) copy-start(s32[1,2]{1,0:T(1,128)} %tissue_ref.1) | copy-start | bytes 28

commit v4 on v3

--- a/solution.py
+++ b/solution.py
@@ -263,24 +263,6 @@
         grads_ref[576:total, :] = jnp.zeros((total - 576, LANES), BF16)
     for copy in copies:
         copy.wait()
-
-
-def sum_kernel(parts_ref, sums_ref):
-    total = parts_ref[0].astype(F32)
-    for part in range(1, parts_ref.shape[0]):
-        total += parts_ref[part].astype(F32)
-    total = total.astype(BF16)
-    for part in range(parts_ref.shape[0]):
-        sums_ref[part] = total
-
-
-def split_kernel(whole_ref, one_ref, two_ref):
-    chunk = whole_ref.shape[1]
-    rows, half = one_ref.shape
-    for part in range(rows // chunk):
-        block = whole_ref[part].astype(F32)
-        one_ref[part * chunk : (part + 1) * chunk, :] = block[:, :half]
-        two_ref[part * chunk : (part + 1) * chunk, :] = block[:, half:]
 
 
 def local(slide_image, cotangent, weight_one, weight_two, tissue, neighbours):
@@ -343,21 +325,12 @@
     )(links, tissue, image, upstream, halo, weight_one, weight_two)
 
     parts = lax.all_to_all(grads.reshape(devices, chunk, LANES), ("slide", "tile"), 0, 0, tiled=True)
-    sums = pl.pallas_call(
-        sum_kernel,
-        out_shape=jax.ShapeDtypeStruct(parts.shape, BF16),
-        in_specs=[VMEM],
-        out_specs=VMEM,
-        name="sum",
-    )(parts)
+    mine = jnp.sum(lax.optimization_barrier(parts.astype(F32)), axis=0).astype(BF16)
+    sums = jnp.broadcast_to(mine[None], parts.shape)
     whole = lax.all_to_all(sums, ("slide", "tile"), 0, 0, tiled=True)
-    grad_one, grad_two = pl.pallas_call(
-        split_kernel,
-        out_shape=(jax.ShapeDtypeStruct((576, LANES // 2), F32),) * 2,
-        in_specs=[VMEM],
-        out_specs=(VMEM, VMEM),
-        name="split",
-    )(whole)
+    whole = lax.optimization_barrier(whole.reshape(total, LANES).astype(F32))
+    grad_one = whole[:576, : LANES // 2]
+    grad_two = whole[:576, LANES // 2 :]
     shape = weight_one.shape
     return output[None], grad_input[None], grad_one.reshape(shape), grad_two.reshape(shape)
 

time: 55.1 us -> 52.1 us (0.946)
  Pallas kernels: 10.2 us -> 6.81 us
  local copies, waits for them, and re-layouts: 0.04 us -> 0.96 us
    pallas_call x2 -> x0, Pallas kernels: 3.41 us -> none  [the longest x1 1.76 us: local(): pl.pallas_call(split_kernel, out_shape=(jax.ShapeDtypeStruct((576, LANES...]
    slice x0 -> x1, local copies, waits for them, and re-layouts: none -> 0.89 us  [local(): grad_two = whole[:576, LANES // 2:]]
where the time goes in v4:
time: 52.1 us; the launch traced here: 51.9 us
  blocking collectives  43.2 us (83%)
  Pallas kernels  6.81 us (13%)
  local copies, waits for them, and re-layouts  0.96 us (2%)
  between operations  0.74 us (1%)
    all_to_all x1, blocking collectives, local(): halo = lax.all_to_all(packed, 'tile', 0, 0, tiled=True)  20 us
    all_to_all x1, blocking collectives, local(): lax.all_to_all(grads.reshape(devices, chunk, LANES), ('slide', 'tile'), 0...  11.8 us
    all_to_all x1, blocking collectives, local(): whole = lax.all_to_all(sums, ('slide', 'tile'), 0, 0, tiled=True)  11.4 us
    pallas_call x1, Pallas kernels, local(): pl.pallas_call(mix_kernel, out_shape=(jax.ShapeDtypeStruct((slots, side,...  4.76 us
    pallas_call x1, Pallas kernels, local(): pl.pallas_call(pack_kernel, out_shape=jax.ShapeDtypeStruct((devices_tile,...  2.05 us

profile of v4, /device:TPU:0, one launch (start us, length us, event | category | flops | bytes accessed | tf_op | source)
XLA Modules:
  0.0 51.9 jit_solution(4009635005731721652)
XLA Ops:
  0.6 2.1 %pack.1 = bf16[8,208,128]{2,1,0:T(8,128)(2,1)} custom-call(s32[2,8]{1,0:T(2,128)} %bitcast.16, bf16[2,32,2048]{2,1,0:T(8,128)(2,1)} %bitcast.11, bf16[2,32,2048]{2,1,0:T(8,128)(2,1)} %bitcast.13), custom_call_target="tpu_custom_call" | custom-call | tf_op jit(solution)/shard_map/pack/pallas_call | solution.py:276
  2.7 0.0 copy-start
  2.7 0.0 copy-start.1
  2.7 0.0 copy-start.2
  2.7 0.0 copy-start.3
  2.7 0.0 copy-start.4
  2.8 0.0 copy-start.5
  2.8 20.0 %all_to_all.15.halo_ref = bf16[8,208,128]{2,1,0:T(8,128)(2,1)S(1)} all-to-all(bf16[8,208,128]{2,1,0:T(8,128)(2,1)} %pack.1), channel_id=1, replica_groups=mesh['slide'=4,'tile'=8] {'tile'}, dimensions={0} | all-to-all | bytes 851968 | tf_op jit(solution)/shard_map/all_to_all | solution.py:292
  22.8 0.0 copy-done
  22.8 0.0 copy-done.1
  22.8 0.0 copy-done.2
  22.8 0.0 copy-done.3
  22.8 0.0 copy-done.4
  22.8 0.0 copy-done.5
  22.8 4.8 %mix.1 = (bf16[2,32,2048]{2,1,0:T(8,128)(2,1)}, bf16[2,32,2048]{2,1,0:T(8,128)(2,1)}, bf16[768,128]{1,0:T(8,128)(2,1)S(1)}) custom-call(s32[2,8]{1,0:T(2,128)S(1)} %bitcast.17, s32[1,2]{1,0:T(1,128)S(1)} %copy-done.5, bf16[2,32,2048]{2,1,0:T(8,128)(2,1)S(1)} %bitcast.12, bf16[2,32,2048]{2,1,0:T(8,128)(2,1)S(1)} %bitcast.14, ...), custom_call_target="tpu_custom_call" | custom-call | tf_op jit(solution)/shard_map/mix/pallas_call | solution.py:297
  27.6 11.8 %all_to_all.16 = bf16[32,24,128]{2,1,0:T(8,128)(2,1)S(1)} all-to-all(bf16[32,24,128]{2,1,0:T(8,128)(2,1)S(1)} %bitcast.15), channel_id=1, replica_groups=mesh['slide'=4,'tile'=8] {'slide','tile'}, dimensions={0} | all-to-all | bytes 393216 | tf_op jit(solution)/shard_map/all_to_all | solution.py:327
  39.5 11.4 %all_to_all.17 = bf16[32,24,128]{2,1,0:T(8,128)(2,1)S(1)} all-to-all(bf16[32,24,128]{2,1,0:T(8,128)(2,1)S(1)} %broadcast_in_dim.14), channel_id=1, replica_groups=mesh['slide'=4,'tile'=8] {'slide','tile'}, dimensions={0} | all-to-all | bytes 393216 | tf_op jit(solution)/shard_map/all_to_all | solution.py:330
  51.0 0.9 %fusion = (f32[576,64]{1,0:T(8,128)}, f32[576,64]{1,0:T(8,128)}) fusion(f32[768,128]{1,0:T(8,128)S(1)} %bitcast_convert_fusion), kind=kLoop, calls=%fused_computation.1 | loop fusion | bytes 589824 | tf_op jit(solution)/shard_map/slice | solution.py:333
  (4 shorter events, 0.1 us)
Async XLA Ops:
  2.7 20.1 %copy-start = (bf16[1,2,32,2048]{3,2,1,0:T(8,128)(2,1)S(1)}, bf16[1,2,32,2048]{3,2,1,0:T(8,128)(2,1)}, u32[]{:S(2)}) copy-start(bf16[1,2,32,2048]{3,2,1,0:T(8,128)(2,1)} %param.6) | copy-start | bytes 786436
  2.7 20.1 %copy-start.1 = (bf16[1,2,32,2048]{3,2,1,0:T(8,128)(2,1)S(1)}, bf16[1,2,32,2048]{3,2,1,0:T(8,128)(2,1)}, u32[]{:S(2)}) copy-start(bf16[1,2,32,2048]{3,2,1,0:T(8,128)(2,1)} %param.7) | copy-start | bytes 786436
  2.7 20.1 %copy-start.2 = (bf16[3,3,64,64]{3,2,1,0:T(8,128)(2,1)S(1)}, bf16[3,3,64,64]{3,2,1,0:T(8,128)(2,1)}, u32[]{:S(2)}) copy-start(bf16[3,3,64,64]{3,2,1,0:T(8,128)(2,1)} %one_ref.1) | copy-start | bytes 221188
  2.7 20.1 %copy-start.3 = (bf16[3,3,64,64]{3,2,1,0:T(8,128)(2,1)S(1)}, bf16[3,3,64,64]{3,2,1,0:T(8,128)(2,1)}, u32[]{:S(2)}) copy-start(bf16[3,3,64,64]{3,2,1,0:T(8,128)(2,1)} %two_ref.1) | copy-start | bytes 221188
  2.7 20.1 %copy-start.4 = (s32[1,2,8]{2,1,0:T(2,128)S(1)}, s32[1,2,8]{2,1,0:T(2,128)}, u32[]{:S(2)}) copy-start(s32[1,2,8]{2,1,0:T(2,128)} %param.11) | copy-start | bytes 196
  2.8 20.1 %copy-start.5 = (s32[1,2]{1,0:T(1,128)S(1)}, s32[1,2]{1,0:T(1,128)}, u32[]{:S(2)}) copy-start(s32[1,2]{1,0:T(1,128)} %tissue_ref.1) | copy-start | bytes 28

commit v5 on v4

--- a/solution.py
+++ b/solution.py
@@ -16,8 +16,7 @@
 PACK_LIMIT = 60 * 2**20
 
 
-CORNERS = 192
-BLOCK = CORNERS + 16
+BLOCK = 2 * 96
 
 
 def strip_row(field, slot):
@@ -26,10 +25,6 @@
 
 def column_row(field):
     return field * 96 + 64
-
-
-def corner_row(field, slot, there):
-    return 2 * ((field * 2 + slot) * 2 + there)
 
 
 def band_weights(source, forward, back):
@@ -48,62 +43,44 @@
 
 def pack_kernel(
     links_hbm, image_hbm, cotangent_hbm, out_ref,
-    links_ref, image_ref, cotangent_ref, strip_ref, corner_ref, sems,
+    links_ref, image_ref, cotangent_ref, strip_ref, sems,
 ):
-    sources = (links_hbm, image_hbm, cotangent_hbm)
-    targets = (links_ref, image_ref, cotangent_ref)
-    copies = [
-        pltpu.make_async_copy(source, target, sems.at[k])
-        for k, (source, target) in enumerate(zip(sources, targets))
-    ]
-    for copy in copies:
-        copy.start()
-    for copy in copies:
-        copy.wait()
     slots, side, width = image_ref.shape
     pairs = width // LANES
+    copies = [pltpu.make_async_copy(links_hbm, links_ref, sems.at[2 * slots])]
+    copies[0].start()
+    fields = ((image_hbm, image_ref), (cotangent_hbm, cotangent_ref))
+    for field, (source, target) in enumerate(fields):
+        for slot in range(slots):
+            copy = pltpu.make_async_copy(source.at[slot], target.at[slot], sems.at[field * slots + slot])
+            copy.start()
+            copies.append(copy)
     me = lax.axis_index("tile")
-    for slot in range(slots):
-        for field, ref in enumerate((image_ref, cotangent_ref)):
+    copies[0].wait()
+    for field, (_, ref) in enumerate(fields):
+        for slot in range(slots):
+            copies[1 + field * slots + slot].wait()
             top = ref[slot, 0:16, :].astype(F32)
             bottom = ref[slot, side - 16 : side, :].astype(F32)
             for pair in range(pairs):
                 lanes = slice(pair * LANES, (pair + 1) * LANES)
                 rows = slice(2 * pair, 2 * pair + 2)
-                strip_ref[slot, field, 0, rows, :] = top[0:2, lanes]
-                strip_ref[slot, field, 1, rows, :] = bottom[14:16, lanes]
-    for slot in range(slots):
-        for direction in range(8):
-            link = links_ref[slot, direction]
-
-            @pl.when(link >= 0)
-            def _(slot=slot, direction=direction, link=link):
-                device = link // slots
-                there = link % slots
-                for field, ref in enumerate((image_ref, cotangent_ref)):
-                    if direction < 2:
-                        rows = slice(strip_row(field, slot), strip_row(field, slot) + 32)
-                        out_ref[device, rows, :] = strip_ref[slot, field, direction].astype(BF16)
-                    elif direction < 4:
+                strip_ref[0, rows, :] = top[0:2, lanes]
+                strip_ref[1, rows, :] = bottom[14:16, lanes]
+            for direction in range(8):
+                link = links_ref[slot, direction]
+
+                @pl.when(link >= 0)
+                def _(slot=slot, direction=direction, link=link, field=field, ref=ref):
+                    device = link // slots
+                    if direction in (2, 3):
                         first = jnp.where(device == me, strip_row(field, slot), column_row(field))
                         lanes = slice(0, LANES) if direction == 2 else slice(width - LANES, width)
                         out_ref[device, pl.ds(pl.multiple_of(first, 32), 32), :] = ref[slot, :, lanes]
                     else:
-                        which = 0 if direction < 6 else 1
-                        first = 0 if direction % 2 == 0 else side - 2
-                        corner = strip_ref[slot, field, which, first : first + 2, :]
-                        for target in range(slots):
-                            row = corner_row(field, slot, target)
-
-                            @pl.when(there == target)
-                            def _(row=row, corner=corner):
-                                corner_ref[device, row : row + 2, :] = corner
-
-    def place(device, carry):
-        out_ref[device, CORNERS:BLOCK, :] = corner_ref[device].astype(BF16)
-        return carry
-
-    lax.fori_loop(0, out_ref.shape[0], place, 0)
+                        which = 0 if direction in (0, 4, 5) else 1
+                        first = strip_row(field, slot)
+                        out_ref[device, first : first + 32, :] = strip_ref[which].astype(BF16)
 
 
 def mix_kernel(
@@ -145,17 +122,15 @@
                         wide[slot, column, 16 : 16 + side, :] = got
                     else:
                         row = 14 if direction in (0, 4, 5) else 16 + side
+                        at = pl.multiple_of(strip_row(field, 0) + there * 32, 32)
+                        got = halo_ref[device, pl.ds(at, 32), :].astype(F32)
                         if direction < 2:
-                            at = pl.multiple_of(strip_row(field, 0) + there * 32, 32)
-                            got = halo_ref[device, pl.ds(at, 32), :].astype(F32)
                             for pair in range(pairs):
                                 wide[slot, pair + 1, row : row + 2, :] = got[2 * pair : 2 * pair + 2, :]
+                        elif direction in (4, 6):
+                            wide[slot, 0, row : row + 2, :] = got[2 * pairs - 2 : 2 * pairs, :]
                         else:
-                            column = 0 if direction in (4, 6) else pairs + 1
-                            got = halo_ref[device, CORNERS:BLOCK, :].astype(F32)
-                            one, two = (corner_row(field, k, slot) for k in range(2))
-                            corner = jnp.where(there == 0, got[one : one + 2], got[two : two + 2])
-                            wide[slot, column, row : row + 2, :] = corner
+                            wide[slot, pairs + 1, row : row + 2, :] = got[0:2, :]
 
     def spread(field, taps, count, start, rows):
         def step(pair, carry):
@@ -282,9 +257,8 @@
             pltpu.SMEM(links.shape, jnp.int32),
             pltpu.VMEM(image.shape, BF16),
             pltpu.VMEM(image.shape, BF16),
-            pltpu.VMEM((slots, 2, 2, 32, LANES), F32),
-            pltpu.VMEM((devices_tile, 16, LANES), F32),
-            pltpu.SemaphoreType.DMA((3,)),
+            pltpu.VMEM((2, 32, LANES), F32),
+            pltpu.SemaphoreType.DMA((2 * slots + 1,)),
         ],
         compiler_params=pltpu.CompilerParams(vmem_limit_bytes=PACK_LIMIT),
         name="pack",

time: 52.1 us -> 51.4 us (0.987)
  blocking collectives: 43.2 us -> 42.6 us
    all_to_all x1, blocking collectives: 20 us -> 19.5 us  [local(): halo = lax.all_to_all(packed, 'tile', 0, 0, tiled=True)]
where the time goes in v5:
time: 51.4 us; the launch traced here: 51.2 us
  blocking collectives  42.6 us (83%)
  Pallas kernels  6.79 us (13%)
  local copies, waits for them, and re-layouts  0.96 us (2%)
  between operations  0.74 us (1%)
    all_to_all x1, blocking collectives, local(): halo = lax.all_to_all(packed, 'tile', 0, 0, tiled=True)  19.5 us
    all_to_all x1, blocking collectives, local(): lax.all_to_all(grads.reshape(devices, chunk, LANES), ('slide', 'tile'), 0...  11.7 us
    all_to_all x1, blocking collectives, local(): whole = lax.all_to_all(sums, ('slide', 'tile'), 0, 0, tiled=True)  11.4 us
    pallas_call x1, Pallas kernels, local(): pl.pallas_call(mix_kernel, out_shape=(jax.ShapeDtypeStruct((slots, side,...  4.76 us
    pallas_call x1, Pallas kernels, local(): pl.pallas_call(pack_kernel, out_shape=jax.ShapeDtypeStruct((devices_tile,...  2.03 us

profile of v5, /device:TPU:0, one launch (start us, length us, event | category | flops | bytes accessed | tf_op | source)
XLA Modules:
  0.0 51.2 jit_solution(212515744742343445)
XLA Ops:
  0.6 0.0 copy-start.3
  0.6 2.0 %pack.1 = bf16[8,192,128]{2,1,0:T(8,128)(2,1)} custom-call(s32[2,8]{1,0:T(2,128)} %bitcast.16, bf16[2,32,2048]{2,1,0:T(8,128)(2,1)} %bitcast.11, bf16[2,32,2048]{2,1,0:T(8,128)(2,1)} %bitcast.13), custom_call_target="tpu_custom_call" | custom-call | tf_op jit(solution)/shard_map/pack/pallas_call | solution.py:251
  2.7 0.0 copy-start
  2.7 0.0 copy-start.1
  2.7 0.0 copy-start.2
  2.7 0.0 copy-start.4
  2.7 0.0 copy-start.5
  2.7 19.5 %all_to_all.15.halo_ref = bf16[8,192,128]{2,1,0:T(8,128)(2,1)S(1)} all-to-all(bf16[8,192,128]{2,1,0:T(8,128)(2,1)} %pack.1), channel_id=1, replica_groups=mesh['slide'=4,'tile'=8] {'tile'}, dimensions={0} | all-to-all | bytes 786432 | tf_op jit(solution)/shard_map/all_to_all | solution.py:266
  22.2 0.0 copy-done.3
  22.2 0.0 copy-done
  22.2 0.0 copy-done.1
  22.2 0.0 copy-done.2
  22.2 0.0 copy-done.4
  22.3 0.0 copy-done.5
  22.3 4.8 %mix.1 = (bf16[2,32,2048]{2,1,0:T(8,128)(2,1)}, bf16[2,32,2048]{2,1,0:T(8,128)(2,1)}, bf16[768,128]{1,0:T(8,128)(2,1)S(1)}) custom-call(s32[2,8]{1,0:T(2,128)S(1)} %bitcast.17, s32[1,2]{1,0:T(1,128)S(1)} %copy-done.5, bf16[2,32,2048]{2,1,0:T(8,128)(2,1)S(1)} %bitcast.12, bf16[2,32,2048]{2,1,0:T(8,128)(2,1)S(1)} %bitcast.14, ...), custom_call_target="tpu_custom_call" | custom-call | tf_op jit(solution)/shard_map/mix/pallas_call | solution.py:271
  27.0 11.7 %all_to_all.16 = bf16[32,24,128]{2,1,0:T(8,128)(2,1)S(1)} all-to-all(bf16[32,24,128]{2,1,0:T(8,128)(2,1)S(1)} %bitcast.15), channel_id=1, replica_groups=mesh['slide'=4,'tile'=8] {'slide','tile'}, dimensions={0} | all-to-all | bytes 393216 | tf_op jit(solution)/shard_map/all_to_all | solution.py:301
  38.8 11.4 %all_to_all.17 = bf16[32,24,128]{2,1,0:T(8,128)(2,1)S(1)} all-to-all(bf16[32,24,128]{2,1,0:T(8,128)(2,1)S(1)} %broadcast_in_dim.14), channel_id=1, replica_groups=mesh['slide'=4,'tile'=8] {'slide','tile'}, dimensions={0} | all-to-all | bytes 393216 | tf_op jit(solution)/shard_map/all_to_all | solution.py:304
  50.3 0.9 %fusion = (f32[576,64]{1,0:T(8,128)}, f32[576,64]{1,0:T(8,128)}) fusion(f32[768,128]{1,0:T(8,128)S(1)} %bitcast_convert_fusion), kind=kLoop, calls=%fused_computation.1 | loop fusion | bytes 589824 | tf_op jit(solution)/shard_map/slice | solution.py:307
  (4 shorter events, 0.1 us)
Async XLA Ops:
  0.6 21.6 %copy-start.3 = (bf16[3,3,64,64]{3,2,1,0:T(8,128)(2,1)S(1)}, bf16[3,3,64,64]{3,2,1,0:T(8,128)(2,1)}, u32[]{:S(2)}) copy-start(bf16[3,3,64,64]{3,2,1,0:T(8,128)(2,1)} %two_ref.1) | copy-start | bytes 221188
  2.7 19.5 %copy-start = (bf16[1,2,32,2048]{3,2,1,0:T(8,128)(2,1)S(1)}, bf16[1,2,32,2048]{3,2,1,0:T(8,128)(2,1)}, u32[]{:S(2)}) copy-start(bf16[1,2,32,2048]{3,2,1,0:T(8,128)(2,1)} %param.6) | copy-start | bytes 786436
  2.7 19.5 %copy-start.1 = (bf16[1,2,32,2048]{3,2,1,0:T(8,128)(2,1)S(1)}, bf16[1,2,32,2048]{3,2,1,0:T(8,128)(2,1)}, u32[]{:S(2)}) copy-start(bf16[1,2,32,2048]{3,2,1,0:T(8,128)(2,1)} %param.7) | copy-start | bytes 786436
  2.7 19.5 %copy-start.2 = (bf16[3,3,64,64]{3,2,1,0:T(8,128)(2,1)S(1)}, bf16[3,3,64,64]{3,2,1,0:T(8,128)(2,1)}, u32[]{:S(2)}) copy-start(bf16[3,3,64,64]{3,2,1,0:T(8,128)(2,1)} %one_ref.1) | copy-start | bytes 221188
  2.7 19.5 %copy-start.4 = (s32[1,2,8]{2,1,0:T(2,128)S(1)}, s32[1,2,8]{2,1,0:T(2,128)}, u32[]{:S(2)}) copy-start(s32[1,2,8]{2,1,0:T(2,128)} %param.11) | copy-start | bytes 196
  2.7 19.5 %copy-start.5 = (s32[1,2]{1,0:T(1,128)S(1)}, s32[1,2]{1,0:T(1,128)}, u32[]{:S(2)}) copy-start(s32[1,2]{1,0:T(1,128)} %tissue_ref.1) | copy-start | bytes 28

commit v6 on v5

--- a/solution.py
+++ b/solution.py
@@ -265,9 +265,8 @@
     )(links, image, upstream)
     halo = lax.all_to_all(packed, "tile", 0, 0, tiled=True)
 
-    chunk = -(-576 // devices)
-    chunk = -(-chunk // 8) * 8
-    total = chunk * devices
+    chunk = -(-576 // (2 * devices))
+    total = 2 * chunk * devices
     output, grad_input, grads = pl.pallas_call(
         mix_kernel,
         out_shape=(
@@ -298,7 +297,7 @@
         name="mix",
     )(links, tissue, image, upstream, halo, weight_one, weight_two)
 
-    parts = lax.all_to_all(grads.reshape(devices, chunk, LANES), ("slide", "tile"), 0, 0, tiled=True)
+    parts = lax.all_to_all(grads.reshape(devices, chunk, 2, LANES), ("slide", "tile"), 0, 0, tiled=True)
     mine = jnp.sum(lax.optimization_barrier(parts.astype(F32)), axis=0).astype(BF16)
     sums = jnp.broadcast_to(mine[None], parts.shape)
     whole = lax.all_to_all(sums, ("slide", "tile"), 0, 0, tiled=True)

time: 51.4 us -> 49.8 us (0.969)
  blocking collectives: 42.6 us -> 40.8 us
    all_to_all x1, blocking collectives: 11.4 us -> 10.4 us  [local(): whole = lax.all_to_all(sums, ('slide', 'tile'), 0, 0, tiled=True)]
    all_to_all x1, blocking collectives: 11.7 us -> 11 us  [local(): lax.all_to_all(grads.reshape(devices, chunk, 2, LANES), ('slide', 'tile')...]
where the time goes in v6:
time: 49.8 us; the launch traced here: 49.6 us
  blocking collectives  40.8 us (82%)
  Pallas kernels  6.79 us (14%)
  local copies, waits for them, and re-layouts  1.01 us (2%)
  between operations  0.73 us (1%)
    all_to_all x1, blocking collectives, local(): halo = lax.all_to_all(packed, 'tile', 0, 0, tiled=True)  19.5 us
    all_to_all x1, blocking collectives, local(): lax.all_to_all(grads.reshape(devices, chunk, 2, LANES), ('slide', 'tile')...  11 us
    all_to_all x1, blocking collectives, local(): whole = lax.all_to_all(sums, ('slide', 'tile'), 0, 0, tiled=True)  10.4 us
    pallas_call x1, Pallas kernels, local(): pl.pallas_call(mix_kernel, out_shape=(jax.ShapeDtypeStruct((slots, side,...  4.76 us
    pallas_call x1, Pallas kernels, local(): pl.pallas_call(pack_kernel, out_shape=jax.ShapeDtypeStruct((devices_tile,...  2.03 us

profile of v6, /device:TPU:0, one launch (start us, length us, event | category | flops | bytes accessed | tf_op | source)
XLA Modules:
  0.0 49.6 jit_solution(14148387717855010418)
XLA Ops:
  0.6 0.0 copy-start.3
  0.6 2.0 %pack.1 = bf16[8,192,128]{2,1,0:T(8,128)(2,1)} custom-call(s32[2,8]{1,0:T(2,128)} %bitcast.15, bf16[2,32,2048]{2,1,0:T(8,128)(2,1)} %bitcast.10, bf16[2,32,2048]{2,1,0:T(8,128)(2,1)} %bitcast.12), custom_call_target="tpu_custom_call" | custom-call | tf_op jit(solution)/shard_map/pack/pallas_call | solution.py:251
  2.7 0.0 copy-start
  2.7 0.0 copy-start.1
  2.7 0.0 copy-start.2
  2.7 0.0 copy-start.4
  2.7 0.0 copy-start.5
  2.7 19.5 %all_to_all.15.halo_ref = bf16[8,192,128]{2,1,0:T(8,128)(2,1)S(1)} all-to-all(bf16[8,192,128]{2,1,0:T(8,128)(2,1)} %pack.1), channel_id=1, replica_groups=mesh['slide'=4,'tile'=8] {'tile'}, dimensions={0} | all-to-all | bytes 786432 | tf_op jit(solution)/shard_map/all_to_all | solution.py:266
  22.2 0.0 copy-done.3
  22.2 0.0 copy-done
  22.2 0.0 copy-done.1
  22.2 0.0 copy-done.2
  22.2 0.0 copy-done.4
  22.2 0.0 copy-done.5
  22.3 4.8 %mix.1 = (bf16[2,32,2048]{2,1,0:T(8,128)(2,1)}, bf16[2,32,2048]{2,1,0:T(8,128)(2,1)}, bf16[576,128]{1,0:T(8,128)(2,1)S(1)}) custom-call(s32[2,8]{1,0:T(2,128)S(1)} %bitcast.16, s32[1,2]{1,0:T(1,128)S(1)} %copy-done.5, bf16[2,32,2048]{2,1,0:T(8,128)(2,1)S(1)} %bitcast.11, bf16[2,32,2048]{2,1,0:T(8,128)(2,1)S(1)} %bitcast.13, ...), custom_call_target="tpu_custom_call" | custom-call | tf_op jit(solution)/shard_map/mix/pallas_call | solution.py:270
  27.0 11.0 %all_to_all.16 = bf16[32,9,2,128]{3,2,1,0:T(2,128)(2,1)S(1)} all-to-all(bf16[32,9,2,128]{3,2,1,0:T(2,128)(2,1)S(1)} %bitcast.14), channel_id=1, replica_groups=mesh['slide'=4,'tile'=8] {'slide','tile'}, dimensions={0} | all-to-all | bytes 294912 | tf_op jit(solution)/shard_map/all_to_all | solution.py:300
  38.0 0.1 convert_element_type.16
  38.1 0.1 reduce_sum.9
  38.2 0.1 broadcast_in_dim.14
  38.3 10.4 %all_to_all.17 = bf16[32,9,2,128]{3,2,1,0:T(2,128)(2,1)S(1)} all-to-all(bf16[32,9,2,128]{3,2,1,0:T(2,128)(2,1)S(1)} %broadcast_in_dim.14), channel_id=1, replica_groups=mesh['slide'=4,'tile'=8] {'slide','tile'}, dimensions={0} | all-to-all | bytes 294912 | tf_op jit(solution)/shard_map/all_to_all | solution.py:303
  48.7 0.9 %fusion = (f32[576,64]{1,0:T(8,128)}, f32[576,64]{1,0:T(8,128)}) fusion(f32[576,128]{1,0:T(8,128)S(1)} %convert.1), kind=kLoop, calls=%fused_computation | loop fusion | bytes 589824 | tf_op jit(solution)/shard_map/slice | solution.py:306
  (1 shorter events, 0.0 us)
Async XLA Ops:
  0.6 21.6 %copy-start.3 = (bf16[3,3,64,64]{3,2,1,0:T(8,128)(2,1)S(1)}, bf16[3,3,64,64]{3,2,1,0:T(8,128)(2,1)}, u32[]{:S(2)}) copy-start(bf16[3,3,64,64]{3,2,1,0:T(8,128)(2,1)} %two_ref.1) | copy-start | bytes 221188
  2.7 19.5 %copy-start = (bf16[1,2,32,2048]{3,2,1,0:T(8,128)(2,1)S(1)}, bf16[1,2,32,2048]{3,2,1,0:T(8,128)(2,1)}, u32[]{:S(2)}) copy-start(bf16[1,2,32,2048]{3,2,1,0:T(8,128)(2,1)} %param.6) | copy-start | bytes 786436
  2.7 19.5 %copy-start.1 = (bf16[1,2,32,2048]{3,2,1,0:T(8,128)(2,1)S(1)}, bf16[1,2,32,2048]{3,2,1,0:T(8,128)(2,1)}, u32[]{:S(2)}) copy-start(bf16[1,2,32,2048]{3,2,1,0:T(8,128)(2,1)} %param.7) | copy-start | bytes 786436
  2.7 19.5 %copy-start.2 = (bf16[3,3,64,64]{3,2,1,0:T(8,128)(2,1)S(1)}, bf16[3,3,64,64]{3,2,1,0:T(8,128)(2,1)}, u32[]{:S(2)}) copy-start(bf16[3,3,64,64]{3,2,1,0:T(8,128)(2,1)} %one_ref.1) | copy-start | bytes 221188
  2.7 19.5 %copy-start.4 = (s32[1,2,8]{2,1,0:T(2,128)S(1)}, s32[1,2,8]{2,1,0:T(2,128)}, u32[]{:S(2)}) copy-start(s32[1,2,8]{2,1,0:T(2,128)} %param.11) | copy-start | bytes 196
  2.7 19.5 %copy-start.5 = (s32[1,2]{1,0:T(1,128)S(1)}, s32[1,2]{1,0:T(1,128)}, u32[]{:S(2)}) copy-start(s32[1,2]{1,0:T(1,128)} %tissue_ref.1) | copy-start | bytes 28

commit v7 on v6

--- a/solution.py
+++ b/solution.py
@@ -10,7 +10,6 @@
 F32 = jnp.float32
 BF16 = jnp.bfloat16
 LANES = 128
-SMEM = pl.BlockSpec(memory_space=pltpu.SMEM)
 VMEM = pl.BlockSpec(memory_space=pltpu.VMEM)
 ANY = pl.BlockSpec(memory_space=pl.ANY)
 PACK_LIMIT = 60 * 2**20
@@ -84,9 +83,9 @@
 
 
 def mix_kernel(
-    links_ref, tissue_ref, image_ref, cotangent_ref, halo_ref, one_ref, two_ref,
+    links_hbm, tissue_hbm, image_ref, cotangent_ref, halo_ref, one_ref, two_ref,
     output_hbm, grad_input_hbm, grads_ref,
-    wide_in, wide_up, narrow_hidden, narrow_delta, own_delta,
+    links_ref, tissue_ref, wide_in, wide_up, narrow_hidden, narrow_delta,
     taps_in, taps_up, taps_hidden, taps_delta, forward_ref, back_ref, acc_ref, output_ref, grad_input_ref, sems,
 ):
     slots, side, width = image_ref.shape
@@ -95,14 +94,20 @@
     tall = side + 16
     me = lax.axis_index("tile")
 
+    small = [
+        pltpu.make_async_copy(tissue_hbm, tissue_ref, sems.at[2 * slots]),
+        pltpu.make_async_copy(links_hbm, links_ref, sems.at[2 * slots + 1]),
+    ]
+    for copy in small:
+        copy.start()
     band_weights(one_ref, forward_ref.at[0], back_ref.at[0])
     band_weights(two_ref, forward_ref.at[1], back_ref.at[1])
+    for copy in small:
+        copy.wait()
 
     for field, (ref, wide) in enumerate(((image_ref, wide_in), (cotangent_ref, wide_up))):
         wide[:, :, 0:16, :] = jnp.zeros((slots, pairs + 2, 16, LANES), F32)
         wide[:, :, 16 + side : 32 + side, :] = jnp.zeros((slots, pairs + 2, 16, LANES), F32)
-        for column in (0, pairs + 1):
-            wide[:, column, 16 : 16 + side, :] = jnp.zeros((slots, side, LANES), F32)
         for slot in range(slots):
             present = tissue_ref[0, slot] > 0
             for pair in range(pairs):
@@ -110,38 +115,28 @@
                 wide[slot, pair + 1, 16 : 16 + side, :] = jnp.where(present, block, 0.0)
             for direction in range(8):
                 link = links_ref[slot, direction]
-
-                @pl.when(link >= 0)
-                def _(slot=slot, direction=direction, link=link, field=field, wide=wide):
-                    device, there = link // slots, link % slots
-                    if direction in (2, 3):
-                        column = 0 if direction == 2 else pairs + 1
-                        at_home = strip_row(field, 0) + there * 32
-                        first = pl.multiple_of(jnp.where(device == me, at_home, column_row(field)), 32)
-                        got = halo_ref[device, pl.ds(first, 32), :].astype(F32)
-                        wide[slot, column, 16 : 16 + side, :] = got
-                    else:
-                        row = 14 if direction in (0, 4, 5) else 16 + side
-                        at = pl.multiple_of(strip_row(field, 0) + there * 32, 32)
-                        got = halo_ref[device, pl.ds(at, 32), :].astype(F32)
-                        if direction < 2:
-                            for pair in range(pairs):
-                                wide[slot, pair + 1, row : row + 2, :] = got[2 * pair : 2 * pair + 2, :]
-                        elif direction in (4, 6):
-                            wide[slot, 0, row : row + 2, :] = got[2 * pairs - 2 : 2 * pairs, :]
-                        else:
-                            wide[slot, pairs + 1, row : row + 2, :] = got[0:2, :]
+                device, there = jnp.maximum(link, 0) // slots, jnp.maximum(link, 0) % slots
+                first = strip_row(field, 0) + there * 32
+                if direction in (2, 3):
+                    first = jnp.where(device == me, first, column_row(field))
+                got = halo_ref[device, pl.ds(pl.multiple_of(first, 32), 32), :].astype(F32)
+                got = jnp.where(link >= 0, got, 0.0)
+                row = 14 if direction in (0, 4, 5) else 16 + side
+                if direction in (2, 3):
+                    wide[slot, 0 if direction == 2 else pairs + 1, 16 : 16 + side, :] = got
+                elif direction < 2:
+                    for pair in range(pairs):
+                        wide[slot, pair + 1, row : row + 2, :] = got[2 * pair : 2 * pair + 2, :]
+                elif direction in (4, 6):
+                    wide[slot, 0, row : row + 2, :] = got[2 * pairs - 2 : 2 * pairs, :]
+                else:
+                    wide[slot, pairs + 1, row : row + 2, :] = got[0:2, :]
 
     def spread(field, taps, count, start, rows):
-        def step(pair, carry):
+        for pair in range(count):
             for slot in range(slots):
                 for a in range(3):
-                    block = field[slot, pair, start + a - 1 : start + a - 1 + rows, :].astype(BF16)
-                    taps[slot, pair + 1, :, a * 256 : a * 256 + LANES] = block
-                    taps[slot, pair, :, a * 256 + LANES : (a + 1) * 256] = block
-            return carry
-
-        lax.fori_loop(0, count, step, 0, unroll=True)
+                    taps[slot, a, pair] = field[slot, pair, start + a - 1 : start + a - 1 + rows, :].astype(BF16)
 
     spread(wide_in, taps_in, pairs + 2, 8, tall)
     spread(wide_up, taps_up, pairs + 2, 8, tall)
@@ -154,7 +149,12 @@
         return jnp.where((row >= 7) & (row <= 8 + side), value, 0)
 
     def across(taps, slot, count, rows):
-        return taps[slot, 1 : count + 1].reshape(count * rows, 768)
+        parts = [
+            taps[slot, a, right : count + right].reshape(count * rows, LANES)
+            for a in range(3)
+            for right in range(2)
+        ]
+        return jnp.concatenate(parts, axis=1)
 
     contract_last = (((1,), (1,)), ((), ()))
     for slot in range(slots):
@@ -163,34 +163,23 @@
         middle = column_mask(there[0], own, there[1])
         west = jnp.where(lane < half, column_mask(there[4], there[2], there[6]), middle)
         east = jnp.where(lane < half, middle, column_mask(there[5], there[3], there[7]))
-        inside = (row >= 8) & (row < 8 + side)
 
         first = jnp.dot(
             across(taps_in, slot, pairs + 1, tall), forward_ref[0], preferred_element_type=F32
         )
-        acc_ref[0] = first.reshape(pairs + 1, tall, LANES)
+        acc_ref[slot, 0] = first.reshape(pairs + 1, tall, LANES)
         second = lax.dot_general(
             across(taps_up, slot, pairs + 1, tall), back_ref[1], contract_last,
             preferred_element_type=F32,
         )
-        acc_ref[1] = second.reshape(pairs + 1, tall, LANES)
-
-        def finish(pair, mask, own_mask, slot=slot):
-            hidden = jnp.where(mask > 0, jnp.maximum(acc_ref[0, pair], 0.0), 0.0)
+        acc_ref[slot, 1] = second.reshape(pairs + 1, tall, LANES)
+
+        for pair in range(pairs + 1):
+            mask = west if pair == 0 else east if pair == pairs else middle
+            hidden = jnp.where(mask > 0, jnp.maximum(acc_ref[slot, 0, pair], 0.0), 0.0)
             hidden = hidden.astype(BF16).astype(F32)
-            delta = jnp.where(hidden > 0, acc_ref[1, pair], 0.0)
             narrow_hidden[slot, pair] = hidden
-            narrow_delta[slot, pair] = delta
-            own_delta[slot, pair] = jnp.where(own_mask, delta, 0.0).astype(BF16)
-
-        finish(0, west, inside & (lane >= half))
-        finish(pairs, east, inside & (lane < half))
-
-        def middle_step(pair, carry, middle=middle, inside=inside):
-            finish(pair, middle, inside)
-            return carry
-
-        lax.fori_loop(1, pairs, middle_step, 0, unroll=True)
+            narrow_delta[slot, pair] = jnp.where(hidden > 0, acc_ref[slot, 1, pair], 0.0)
 
     spread(narrow_hidden, taps_hidden, pairs + 1, 8, side)
     spread(narrow_delta, taps_delta, pairs + 1, 8, side)
@@ -213,27 +202,33 @@
             copies.append(pltpu.make_async_copy(source.at[slot], target.at[slot], sems.at[2 * slot + k]))
             copies[-1].start()
     for slot in range(slots):
-        upstream = wide_up[slot, 1 : pairs + 1, 16 : 16 + side, :].reshape(pairs * side, LANES)
+        own_in, own_up = (
+            wide[slot, 1 : pairs + 1, 16 : 16 + side, :].reshape(pairs * side, LANES).astype(BF16)
+            for wide in (wide_in, wide_up)
+        )
+        term_one = lax.dot_general(
+            own_in, across(taps_delta, slot, pairs, side), contract_first, preferred_element_type=F32
+        )
         term_two = lax.dot_general(
-            upstream.astype(BF16), across(taps_hidden, slot, pairs, side), contract_first,
-            preferred_element_type=F32,
-        )
-        deltas = own_delta[slot].reshape((pairs + 1) * tall, LANES)
-        term_one = lax.dot_general(
-            deltas, across(taps_in, slot, pairs + 1, tall), contract_first, preferred_element_type=F32
+            own_up, across(taps_hidden, slot, pairs, side), contract_first, preferred_element_type=F32
         )
         first_grad = term_one if first_grad is None else first_grad + term_one
         second_grad = term_two if second_grad is None else second_grad + term_two
 
     total = grads_ref.shape[0]
-    lane = lax.broadcasted_iota(jnp.int32, (192, LANES), 1)
+    lane = lax.broadcasted_iota(jnp.int32, (half, LANES), 1)
     for a in range(3):
-        lanes = slice(a * 256, (a + 1) * 256)
-        one = first_grad[:, lanes].T
-        two = second_grad[:, lanes].T
-        left = one[0:192] + pltpu.roll(one[64:256], half, 1)
-        right = pltpu.roll(two[0:192], half, 1) + two[64:256]
-        grads_ref[a * 192 : (a + 1) * 192, :] = jnp.where(lane < half, left, right).astype(BF16)
+        one = first_grad[:, (2 - a) * 256 : (3 - a) * 256]
+        two = second_grad[:, a * 256 : (a + 1) * 256].T
+        blocks = [one[:half, 0:LANES], one[:half, LANES:256], one[half:, 0:LANES], one[half:, LANES:256]]
+        turned = [pltpu.roll(block, half, 1) for block in blocks]
+        left = (blocks[0] + turned[2], turned[0] + blocks[3], blocks[1] + turned[3])
+        for b in range(3):
+            upper = two[b * half : (b + 1) * half]
+            lower = two[(b + 1) * half : (b + 2) * half]
+            right = pltpu.roll(upper, half, 1) + lower
+            rows = slice((a * 3 + b) * half, (a * 3 + b + 1) * half)
+            grads_ref[rows, :] = jnp.where(lane < half, left[2 - b], right).astype(BF16)
     if total > 576:
         grads_ref[576:total, :] = jnp.zeros((total - 576, LANES), BF16)
     for copy in copies:
@@ -274,24 +269,25 @@
             jax.ShapeDtypeStruct((slots, side, width), BF16),
             jax.ShapeDtypeStruct((total, LANES), BF16),
         ),
-        in_specs=[SMEM, SMEM] + [VMEM] * 5,
+        in_specs=[ANY, ANY] + [VMEM] * 5,
         out_specs=(ANY, ANY, VMEM),
         scratch_shapes=[
+            pltpu.SMEM(links.shape, jnp.int32),
+            pltpu.SMEM(tissue.shape, jnp.int32),
             pltpu.VMEM((slots, pairs + 2, side + 32, LANES), F32),
             pltpu.VMEM((slots, pairs + 2, side + 32, LANES), F32),
             pltpu.VMEM((slots, pairs + 1, tall, LANES), F32),
             pltpu.VMEM((slots, pairs + 1, tall, LANES), F32),
-            pltpu.VMEM((slots, pairs + 1, tall, LANES), BF16),
-            pltpu.VMEM((slots, pairs + 3, tall, 768), BF16),
-            pltpu.VMEM((slots, pairs + 3, tall, 768), BF16),
-            pltpu.VMEM((slots, pairs + 2, side, 768), BF16),
-            pltpu.VMEM((slots, pairs + 2, side, 768), BF16),
+            pltpu.VMEM((slots, 3, pairs + 2, tall, LANES), BF16),
+            pltpu.VMEM((slots, 3, pairs + 2, tall, LANES), BF16),
+            pltpu.VMEM((slots, 3, pairs + 1, side, LANES), BF16),
+            pltpu.VMEM((slots, 3, pairs + 1, side, LANES), BF16),
             pltpu.VMEM((2, 768, LANES), BF16),
             pltpu.VMEM((2, LANES, 768), BF16),
-            pltpu.VMEM((2, pairs + 1, tall, LANES), F32),
+            pltpu.VMEM((slots, 2, pairs + 1, tall, LANES), F32),
             pltpu.VMEM((slots, side, width), BF16),
             pltpu.VMEM((slots, side, width), BF16),
-            pltpu.SemaphoreType.DMA((2 * slots,)),
+            pltpu.SemaphoreType.DMA((2 * slots + 2,)),
         ],
         compiler_params=pltpu.CompilerParams(vmem_limit_bytes=48 * 2**20),
         name="mix",

time: 49.8 us -> 48.8 us (0.980)
  Pallas kernels: 6.79 us -> 5.84 us
    pallas_call x1, Pallas kernels: 4.76 us -> 3.81 us  [local(): pl.pallas_call(mix_kernel, out_shape=(jax.ShapeDtypeStruct((slots, side,...]
where the time goes in v7:
time: 48.8 us; the launch traced here: 48.6 us
  blocking collectives  40.7 us (83%)
  Pallas kernels  5.84 us (12%)
  local copies, waits for them, and re-layouts  1.01 us (2%)
  between operations  0.73 us (1%)
    all_to_all x1, blocking collectives, local(): halo = lax.all_to_all(packed, 'tile', 0, 0, tiled=True)  19.5 us
    all_to_all x1, blocking collectives, local(): lax.all_to_all(grads.reshape(devices, chunk, 2, LANES), ('slide', 'tile')...  10.9 us
    all_to_all x1, blocking collectives, local(): whole = lax.all_to_all(sums, ('slide', 'tile'), 0, 0, tiled=True)  10.4 us
    pallas_call x1, Pallas kernels, local(): pl.pallas_call(mix_kernel, out_shape=(jax.ShapeDtypeStruct((slots, side,...  3.81 us
    pallas_call x1, Pallas kernels, local(): pl.pallas_call(pack_kernel, out_shape=jax.ShapeDtypeStruct((devices_tile,...  2.03 us

profile of v7, /device:TPU:0, one launch (start us, length us, event | category | flops | bytes accessed | tf_op | source)
XLA Modules:
  0.0 48.6 jit_solution(10617523339965281955)
XLA Ops:
  0.6 0.0 copy-start.3
  0.6 2.0 %pack.1 = bf16[8,192,128]{2,1,0:T(8,128)(2,1)} custom-call(s32[2,8]{1,0:T(2,128)} %bitcast.15, bf16[2,32,2048]{2,1,0:T(8,128)(2,1)} %bitcast.10, bf16[2,32,2048]{2,1,0:T(8,128)(2,1)} %bitcast.12), custom_call_target="tpu_custom_call" | custom-call | tf_op jit(solution)/shard_map/pack/pallas_call | solution.py:246
  2.7 0.0 copy-start
  2.7 0.0 copy-start.1
  2.7 0.0 copy-start.2
  2.7 0.0 copy-start.4
  2.7 0.0 copy-start.5
  2.7 19.5 %all_to_all.15.halo_ref = bf16[8,192,128]{2,1,0:T(8,128)(2,1)S(1)} all-to-all(bf16[8,192,128]{2,1,0:T(8,128)(2,1)} %pack.1), channel_id=1, replica_groups=mesh['slide'=4,'tile'=8] {'tile'}, dimensions={0} | all-to-all | bytes 786432 | tf_op jit(solution)/shard_map/all_to_all | solution.py:261
  22.2 0.0 copy-done.3
  22.2 0.0 copy-done
  22.3 0.0 copy-done.1
  22.3 0.0 copy-done.2
  22.3 0.0 copy-done.4
  22.3 0.0 copy-done.5
  22.3 3.8 %mix.1 = (bf16[2,32,2048]{2,1,0:T(8,128)(2,1)}, bf16[2,32,2048]{2,1,0:T(8,128)(2,1)}, bf16[576,128]{1,0:T(8,128)(2,1)S(1)}) custom-call(s32[2,8]{1,0:T(2,128)S(1)} %bitcast.16, s32[1,2]{1,0:T(1,128)S(1)} %copy-done.5, bf16[2,32,2048]{2,1,0:T(8,128)(2,1)S(1)} %bitcast.11, bf16[2,32,2048]{2,1,0:T(8,128)(2,1)S(1)} %bitcast.13, ...), custom_call_target="tpu_custom_call" | custom-call | tf_op jit(solution)/shard_map/mix/pallas_call | solution.py:265
  26.1 10.9 %all_to_all.16 = bf16[32,9,2,128]{3,2,1,0:T(2,128)(2,1)S(1)} all-to-all(bf16[32,9,2,128]{3,2,1,0:T(2,128)(2,1)S(1)} %bitcast.14), channel_id=1, replica_groups=mesh['slide'=4,'tile'=8] {'slide','tile'}, dimensions={0} | all-to-all | bytes 294912 | tf_op jit(solution)/shard_map/all_to_all | solution.py:296
  37.0 0.1 convert_element_type.16
  37.1 0.1 reduce_sum.9
  37.2 0.1 broadcast_in_dim.14
  37.3 10.4 %all_to_all.17 = bf16[32,9,2,128]{3,2,1,0:T(2,128)(2,1)S(1)} all-to-all(bf16[32,9,2,128]{3,2,1,0:T(2,128)(2,1)S(1)} %broadcast_in_dim.14), channel_id=1, replica_groups=mesh['slide'=4,'tile'=8] {'slide','tile'}, dimensions={0} | all-to-all | bytes 294912 | tf_op jit(solution)/shard_map/all_to_all | solution.py:299
  47.7 0.9 %fusion = (f32[576,64]{1,0:T(8,128)}, f32[576,64]{1,0:T(8,128)}) fusion(f32[576,128]{1,0:T(8,128)S(1)} %convert.1), kind=kLoop, calls=%fused_computation | loop fusion | bytes 589824 | tf_op jit(solution)/shard_map/slice | solution.py:302
  (1 shorter events, 0.0 us)
Async XLA Ops:
  0.6 21.6 %copy-start.3 = (bf16[3,3,64,64]{3,2,1,0:T(8,128)(2,1)S(1)}, bf16[3,3,64,64]{3,2,1,0:T(8,128)(2,1)}, u32[]{:S(2)}) copy-start(bf16[3,3,64,64]{3,2,1,0:T(8,128)(2,1)} %two_ref.1) | copy-start | bytes 221188
  2.7 19.6 %copy-start = (bf16[1,2,32,2048]{3,2,1,0:T(8,128)(2,1)S(1)}, bf16[1,2,32,2048]{3,2,1,0:T(8,128)(2,1)}, u32[]{:S(2)}) copy-start(bf16[1,2,32,2048]{3,2,1,0:T(8,128)(2,1)} %param.6) | copy-start | bytes 786436
  2.7 19.6 %copy-start.1 = (bf16[1,2,32,2048]{3,2,1,0:T(8,128)(2,1)S(1)}, bf16[1,2,32,2048]{3,2,1,0:T(8,128)(2,1)}, u32[]{:S(2)}) copy-start(bf16[1,2,32,2048]{3,2,1,0:T(8,128)(2,1)} %param.7) | copy-start | bytes 786436
  2.7 19.6 %copy-start.2 = (bf16[3,3,64,64]{3,2,1,0:T(8,128)(2,1)S(1)}, bf16[3,3,64,64]{3,2,1,0:T(8,128)(2,1)}, u32[]{:S(2)}) copy-start(bf16[3,3,64,64]{3,2,1,0:T(8,128)(2,1)} %one_ref.1) | copy-start | bytes 221188
  2.7 19.6 %copy-start.4 = (s32[1,2,8]{2,1,0:T(2,128)S(1)}, s32[1,2,8]{2,1,0:T(2,128)}, u32[]{:S(2)}) copy-start(s32[1,2,8]{2,1,0:T(2,128)} %param.11) | copy-start | bytes 196
  2.7 19.6 %copy-start.5 = (s32[1,2]{1,0:T(1,128)S(1)}, s32[1,2]{1,0:T(1,128)}, u32[]{:S(2)}) copy-start(s32[1,2]{1,0:T(1,128)} %tissue_hbm.1) | copy-start | bytes 28

commit v8 on v7

--- a/solution.py
+++ b/solution.py
@@ -26,18 +26,36 @@
     return field * 96 + 64
 
 
-def band_weights(source, forward, back):
-    half = LANES // 2
-    zero = jnp.zeros((half, half), BF16)
+def forward_weights(source, forward):
+    zero = jnp.zeros((LANES // 2, LANES // 2), BF16)
     for a in range(3):
         taps = [source[a, b] for b in range(3)]
         left = jnp.concatenate(taps + [zero], axis=0)
         right = jnp.concatenate([zero] + taps, axis=0)
         forward[a * 256 : (a + 1) * 256, :] = jnp.concatenate([left, right], axis=1)
+
+
+def back_weights(source, back):
+    zero = jnp.zeros((LANES // 2, LANES // 2), BF16)
+    for a in range(3):
         turned = [source[2 - a, 2 - b] for b in range(3)]
         upper = jnp.concatenate(turned + [zero], axis=1)
         lower = jnp.concatenate([zero] + turned, axis=1)
         back[:, a * 256 : (a + 1) * 256] = jnp.concatenate([upper, lower], axis=0)
+
+
+def across(taps, slot, count):
+    rows = taps.shape[3]
+    parts = [
+        taps[slot, a, right : count + right].reshape(count * rows, LANES)
+        for a in range(3)
+        for right in range(2)
+    ]
+    return jnp.concatenate(parts, axis=1)
+
+
+CONTRACT_FIRST = (((0,), (0,)), ((), ()))
+CONTRACT_LAST = (((1,), (1,)), ((), ()))
 
 
 def pack_kernel(
@@ -84,9 +102,9 @@
 
 def mix_kernel(
     links_hbm, tissue_hbm, image_ref, cotangent_ref, halo_ref, one_ref, two_ref,
-    output_hbm, grad_input_hbm, grads_ref,
+    grads_ref, taps_hidden, taps_delta,
     links_ref, tissue_ref, wide_in, wide_up, narrow_hidden, narrow_delta,
-    taps_in, taps_up, taps_hidden, taps_delta, forward_ref, back_ref, acc_ref, output_ref, grad_input_ref, sems,
+    taps_in, taps_up, forward_ref, back_ref, acc_ref, sems,
 ):
     slots, side, width = image_ref.shape
     pairs = width // LANES
@@ -95,13 +113,13 @@
     me = lax.axis_index("tile")
 
     small = [
-        pltpu.make_async_copy(tissue_hbm, tissue_ref, sems.at[2 * slots]),
-        pltpu.make_async_copy(links_hbm, links_ref, sems.at[2 * slots + 1]),
+        pltpu.make_async_copy(tissue_hbm, tissue_ref, sems.at[0]),
+        pltpu.make_async_copy(links_hbm, links_ref, sems.at[1]),
     ]
     for copy in small:
         copy.start()
-    band_weights(one_ref, forward_ref.at[0], back_ref.at[0])
-    band_weights(two_ref, forward_ref.at[1], back_ref.at[1])
+    forward_weights(one_ref, forward_ref)
+    back_weights(two_ref, back_ref)
     for copy in small:
         copy.wait()
 
@@ -148,15 +166,6 @@
         value = jnp.where(row == 7, north, jnp.where(row == 8 + side, south, here))
         return jnp.where((row >= 7) & (row <= 8 + side), value, 0)
 
-    def across(taps, slot, count, rows):
-        parts = [
-            taps[slot, a, right : count + right].reshape(count * rows, LANES)
-            for a in range(3)
-            for right in range(2)
-        ]
-        return jnp.concatenate(parts, axis=1)
-
-    contract_last = (((1,), (1,)), ((), ()))
     for slot in range(slots):
         there = [(links_ref[slot, k] >= 0).astype(jnp.int32) for k in range(8)]
         own = tissue_ref[0, slot]
@@ -165,11 +174,11 @@
         east = jnp.where(lane < half, middle, column_mask(there[5], there[3], there[7]))
 
         first = jnp.dot(
-            across(taps_in, slot, pairs + 1, tall), forward_ref[0], preferred_element_type=F32
+            across(taps_in, slot, pairs + 1), forward_ref[...], preferred_element_type=F32
         )
         acc_ref[slot, 0] = first.reshape(pairs + 1, tall, LANES)
         second = lax.dot_general(
-            across(taps_up, slot, pairs + 1, tall), back_ref[1], contract_last,
+            across(taps_up, slot, pairs + 1), back_ref[...], CONTRACT_LAST,
             preferred_element_type=F32,
         )
         acc_ref[slot, 1] = second.reshape(pairs + 1, tall, LANES)
@@ -186,31 +195,16 @@
 
     first_grad = None
     second_grad = None
-    copies = []
-    contract_first = (((0,), (0,)), ((), ()))
-    for slot in range(slots):
-        out = jnp.dot(across(taps_hidden, slot, pairs, side), forward_ref[1], preferred_element_type=F32)
-        back = lax.dot_general(
-            across(taps_delta, slot, pairs, side), back_ref[0], contract_last, preferred_element_type=F32
-        )
-        for pair in range(pairs):
-            lanes = slice(pair * LANES, (pair + 1) * LANES)
-            rows = slice(pair * side, (pair + 1) * side)
-            output_ref[slot, :, lanes] = out[rows].astype(BF16)
-            grad_input_ref[slot, :, lanes] = back[rows].astype(BF16)
-        for k, (source, target) in enumerate(((output_ref, output_hbm), (grad_input_ref, grad_input_hbm))):
-            copies.append(pltpu.make_async_copy(source.at[slot], target.at[slot], sems.at[2 * slot + k]))
-            copies[-1].start()
     for slot in range(slots):
         own_in, own_up = (
             wide[slot, 1 : pairs + 1, 16 : 16 + side, :].reshape(pairs * side, LANES).astype(BF16)
             for wide in (wide_in, wide_up)
         )
         term_one = lax.dot_general(
-            own_in, across(taps_delta, slot, pairs, side), contract_first, preferred_element_type=F32
+            own_in, across(taps_delta, slot, pairs), CONTRACT_FIRST, preferred_element_type=F32
         )
         term_two = lax.dot_general(
-            own_up, across(taps_hidden, slot, pairs, side), contract_first, preferred_element_type=F32
+            own_up, across(taps_hidden, slot, pairs), CONTRACT_FIRST, preferred_element_type=F32
         )
         first_grad = term_one if first_grad is None else first_grad + term_one
         second_grad = term_two if second_grad is None else second_grad + term_two
@@ -231,6 +225,31 @@
             grads_ref[rows, :] = jnp.where(lane < half, left[2 - b], right).astype(BF16)
     if total > 576:
         grads_ref[576:total, :] = jnp.zeros((total - 576, LANES), BF16)
+
+
+def outer_kernel(
+    taps_hidden, taps_delta, one_ref, two_ref,
+    output_hbm, grad_input_hbm,
+    forward_ref, back_ref, output_ref, grad_input_ref, sems,
+):
+    slots, side, width = output_ref.shape
+    pairs = width // LANES
+    forward_weights(two_ref, forward_ref)
+    back_weights(one_ref, back_ref)
+    copies = []
+    for slot in range(slots):
+        out = jnp.dot(across(taps_hidden, slot, pairs), forward_ref[...], preferred_element_type=F32)
+        back = lax.dot_general(
+            across(taps_delta, slot, pairs), back_ref[...], CONTRACT_LAST, preferred_element_type=F32
+        )
+        for pair in range(pairs):
+            lanes = slice(pair * LANES, (pair + 1) * LANES)
+            rows = slice(pair * side, (pair + 1) * side)
+            output_ref[slot, :, lanes] = out[rows].astype(BF16)
+            grad_input_ref[slot, :, lanes] = back[rows].astype(BF16)
+        for k, (source, target) in enumerate(((output_ref, output_hbm), (grad_input_ref, grad_input_hbm))):
+            copies.append(pltpu.make_async_copy(source.at[slot], target.at[slot], sems.at[2 * slot + k]))
+            copies[-1].start()
     for copy in copies:
         copy.wait()
 
@@ -262,15 +281,12 @@
 
     chunk = -(-576 // (2 * devices))
     total = 2 * chunk * devices
-    output, grad_input, grads = pl.pallas_call(
+    taps = jax.ShapeDtypeStruct((slots, 3, pairs + 1, side, LANES), BF16)
+    grads, taps_hidden, taps_delta = pl.pallas_call(
         mix_kernel,
-        out_shape=(
-            jax.ShapeDtypeStruct((slots, side, width), BF16),
-            jax.ShapeDtypeStruct((slots, side, width), BF16),
-            jax.ShapeDtypeStruct((total, LANES), BF16),
-        ),
+        out_shape=(jax.ShapeDtypeStruct((total, LANES), BF16), taps, taps),
         in_specs=[ANY, ANY] + [VMEM] * 5,
-        out_specs=(ANY, ANY, VMEM),
+        out_specs=(VMEM,) * 3,
         scratch_shapes=[
             pltpu.SMEM(links.shape, jnp.int32),
             pltpu.SMEM(tissue.shape, jnp.int32),
@@ -280,18 +296,31 @@
             pltpu.VMEM((slots, pairs + 1, tall, LANES), F32),
             pltpu.VMEM((slots, 3, pairs + 2, tall, LANES), BF16),
             pltpu.VMEM((slots, 3, pairs + 2, tall, LANES), BF16),
-            pltpu.VMEM((slots, 3, pairs + 1, side, LANES), BF16),
-            pltpu.VMEM((slots, 3, pairs + 1, side, LANES), BF16),
-            pltpu.VMEM((2, 768, LANES), BF16),
-            pltpu.VMEM((2, LANES, 768), BF16),
+            pltpu.VMEM((768, LANES), BF16),
+            pltpu.VMEM((LANES, 768), BF16),
             pltpu.VMEM((slots, 2, pairs + 1, tall, LANES), F32),
+            pltpu.SemaphoreType.DMA((2,)),
+        ],
+        compiler_params=pltpu.CompilerParams(vmem_limit_bytes=40 * 2**20),
+        cost_estimate=pl.CostEstimate(flops=4 * 10**9, bytes_accessed=10**7, transcendentals=0),
+        name="mix",
+    )(links, tissue, image, upstream, halo, weight_one, weight_two)
+    output, grad_input = pl.pallas_call(
+        outer_kernel,
+        out_shape=(jax.ShapeDtypeStruct((slots, side, width), BF16),) * 2,
+        in_specs=[VMEM] * 4,
+        out_specs=(ANY, ANY),
+        scratch_shapes=[
+            pltpu.VMEM((768, LANES), BF16),
+            pltpu.VMEM((LANES, 768), BF16),
             pltpu.VMEM((slots, side, width), BF16),
             pltpu.VMEM((slots, side, width), BF16),
-            pltpu.SemaphoreType.DMA((2 * slots + 2,)),
+            pltpu.SemaphoreType.DMA((2 * slots,)),
         ],
-        compiler_params=pltpu.CompilerParams(vmem_limit_bytes=48 * 2**20),
-        name="mix",
-    )(links, tissue, image, upstream, halo, weight_one, weight_two)
+        compiler_params=pltpu.CompilerParams(vmem_limit_bytes=24 * 2**20),
+        cost_estimate=pl.CostEstimate(flops=4 * 10**9, bytes_accessed=10**7, transcendentals=0),
+        name="outer",
+    )(taps_hidden, taps_delta, weight_one, weight_two)
 
     parts = lax.all_to_all(grads.reshape(devices, chunk, 2, LANES), ("slide", "tile"), 0, 0, tiled=True)
     mine = jnp.sum(lax.optimization_barrier(parts.astype(F32)), axis=0).astype(BF16)

time: 48.8 us -> 49.1 us (level)
  blocking collectives: 40.7 us -> 30.4 us
  waiting for transfers between devices: 0 us -> 6 us
  starting transfers between devices: 0 us -> 2.72 us
  Pallas kernels: 5.84 us -> 7.01 us
  local copies, waits for them, and re-layouts: 1.01 us -> 1.67 us
    all_to_all x1 -> x0, blocking collectives: 10.4 us -> none  [local(): whole = lax.all_to_all(sums, ('slide', 'tile'), 0, 0, tiled=True)]
    all_to_all x0 -> x1, waiting for transfers between devices: none -> 6 us  [local(): whole = lax.all_to_all(sums, ('slide', 'tile'), 0, 0, tiled=True)]
    all_to_all x0 -> x1, starting transfers between devices: none -> 2.72 us  [local(): whole = lax.all_to_all(sums, ('slide', 'tile'), 0, 0, tiled=True)]
    pallas_call x1 -> x2, Pallas kernels: 3.81 us -> 4.98 us  [the longest x1 3.17 us: local(): pl.pallas_call(mix_kernel, out_shape=(jax.ShapeDtypeStruct((total, LANES)...]
    broadcast_in_dim x1, local copies, waits for them, and re-layouts: 0.08 us -> 0.74 us  [local(): sums = jnp.broadcast_to(mine[None], parts.shape)]
  transfers between devices with their start and end apart: 0 -> 1, of which waited for: 0 -> 1; matrix products, arithmetic and copies ran while one was open for 0% -> 0% of each run, Pallas kernels for 0% -> 4%
where the time goes in v8:
time: 49.1 us; the launch traced here: 48.8 us
  blocking collectives  30.4 us (62%)
  Pallas kernels  7.01 us (14%)
  waiting for transfers between devices  6 us (12%)
  starting transfers between devices  2.72 us (6%)
  local copies, waits for them, and re-layouts  1.67 us (3%)
  between operations  0.75 us (2%)
    all_to_all x1, blocking collectives, local(): halo = lax.all_to_all(packed, 'tile', 0, 0, tiled=True)  19.5 us
    all_to_all x1, blocking collectives, local(): lax.all_to_all(grads.reshape(devices, chunk, 2, LANES), ('slide', 'tile')...  10.9 us
    all_to_all x1, waiting for transfers between devices, local(): whole = lax.all_to_all(sums, ('slide', 'tile'), 0, 0, tiled=True)  6 us
    pallas_call x1, Pallas kernels, local(): pl.pallas_call(mix_kernel, out_shape=(jax.ShapeDtypeStruct((total, LANES)...  3.17 us
    all_to_all x1, starting transfers between devices, local(): whole = lax.all_to_all(sums, ('slide', 'tile'), 0, 0, tiled=True)  2.72 us
    pallas_call x1, Pallas kernels, local(): pl.pallas_call(pack_kernel, out_shape=jax.ShapeDtypeStruct((devices_tile,...  2.03 us
    pallas_call x1, Pallas kernels, local(): pl.pallas_call(outer_kernel, out_shape=(jax.ShapeDtypeStruct((slots, side...  1.81 us
  transfers between devices with their start and end apart: 1, of which 1 were waited for; matrix products, arithmetic and copies ran while one was open for 0% of the time, Pallas kernels for 4%

profile of v8, /device:TPU:0, one launch (start us, length us, event | category | flops | bytes accessed | tf_op | source)
XLA Modules:
  0.0 48.8 jit_solution(10218560083829837723)
XLA Ops:
  0.6 0.0 copy-start.4
  0.6 2.0 %pack.1 = bf16[8,192,128]{2,1,0:T(8,128)(2,1)} custom-call(s32[2,8]{1,0:T(2,128)} %bitcast.15, bf16[2,32,2048]{2,1,0:T(8,128)(2,1)} %bitcast.10, bf16[2,32,2048]{2,1,0:T(8,128)(2,1)} %bitcast.12), custom_call_target="tpu_custom_call" | custom-call | tf_op jit(solution)/shard_map/pack/pallas_call | solution.py:265
  2.7 0.0 copy-start
  2.7 0.0 copy-start.1
  2.7 0.0 copy-start.2
  2.7 0.0 copy-start.3
  2.7 0.0 copy-start.5
  2.7 19.5 %all_to_all.15.halo_ref = bf16[8,192,128]{2,1,0:T(8,128)(2,1)S(1)} all-to-all(bf16[8,192,128]{2,1,0:T(8,128)(2,1)} %pack.1), channel_id=1, replica_groups=mesh['slide'=4,'tile'=8] {'tile'}, dimensions={0} | all-to-all | bytes 786432 | tf_op jit(solution)/shard_map/all_to_all | solution.py:280
  22.2 0.0 copy-done.4
  22.2 0.0 copy-done
  22.2 0.0 copy-done.1
  22.2 0.0 copy-done.2
  22.2 0.0 copy-done.3
  22.2 0.0 copy-done.5
  22.3 3.2 %mix.1 = (bf16[576,128]{1,0:T(8,128)(2,1)S(1)}, bf16[2,3,17,32,128]{4,3,2,1,0:T(8,128)(2,1)S(1)}, bf16[2,3,17,32,128]{4,3,2,1,0:T(8,128)(2,1)S(1)}) custom-call(s32[2,8]{1,0:T(2,128)S(1)} %bitcast.16, s32[1,2]{1,0:T(1,128)S(1)} %copy-done.5, bf16[2,32,2048]{2,1,0:T(8,128)(2,1)S(1)} %bitcast.11, bf16[2,32,2048]{2,1,0:T(8,128)(2,1)S(1)} %bitcast.13, ...), custom_call_target="tpu_custom_call" | custom-call | flops 4000000000 | bytes 10000000 | tf_op jit(solution)/shard_map/mix/pallas_call | solution.py:285
  25.4 10.9 %all_to_all.16 = bf16[32,9,2,128]{3,2,1,0:T(2,128)(2,1)S(1)} all-to-all(bf16[32,9,2,128]{3,2,1,0:T(2,128)(2,1)S(1)} %bitcast.14), channel_id=1, replica_groups=mesh['slide'=4,'tile'=8] {'slide','tile'}, dimensions={0} | all-to-all | bytes 294912 | tf_op jit(solution)/shard_map/all_to_all | solution.py:325
  36.3 0.1 convert_element_type.16
  36.5 0.1 reduce_sum.9
  36.6 0.7 %broadcast_in_dim.14 = bf16[32,9,2,128]{3,2,1,0:T(2,128)(2,1)} broadcast(bf16[9,2,128]{2,1,0:T(2,128)(2,1)S(1)} %reduce_sum.9), dimensions={1,2,3} | broadcast | bytes 152064 | tf_op jit(solution)/shard_map/broadcast_in_dim | solution.py:327
  37.3 2.7 %all-to-all-start.2 = ((bf16[32,9,2,128]{3,2,1,0:T(2,128)(2,1)}), bf16[32,9,2,128]{3,2,1,0:T(2,128)(2,1)S(1)}, u32[]{:S(2)}, u32[]{:S(2)}) async-start(bf16[32,9,2,128]{3,2,1,0:T(2,128)(2,1)} %broadcast_in_dim.14), calls=%async_computation.2 | async-start | bytes 294912 | tf_op jit(solution)/shard_map/all_to_all | solution.py:328
  40.0 1.8 %outer.1 = (bf16[2,32,2048]{2,1,0:T(8,128)(2,1)}, bf16[2,32,2048]{2,1,0:T(8,128)(2,1)}) custom-call(bf16[2,3,17,32,128]{4,3,2,1,0:T(8,128)(2,1)S(1)} %get-tuple-element.9.taps_hidden, bf16[2,3,17,32,128]{4,3,2,1,0:T(8,128)(2,1)S(1)} %get-tuple-element.10.taps_delta, bf16[3,3,64,64]{3,2,1,0:T(8,128)(2,1)S(1)} %copy-done.3, bf16[3,3,64,64]{3,2,1,0:T(8,128)(2,1)S(1)} %copy-done.4), custom_call_target="tpu_custom_call" | custom-call | flops 4000000000 | bytes 10000000 | tf_op jit(solution)/shard_map/outer/pallas_call | solution.py:308
  41.9 6.0 %all-to-all-done.2 = bf16[32,9,2,128]{3,2,1,0:T(2,128)(2,1)S(1)} async-done(((bf16[32,9,2,128]{3,2,1,0:T(2,128)(2,1)}), bf16[32,9,2,128]{3,2,1,0:T(2,128)(2,1)S(1)}, u32[]{:S(2)}, u32[]{:S(2)}) %all-to-all-start.2) | async-done | bytes 147488 | tf_op jit(solution)/shard_map/all_to_all | solution.py:328
  47.9 0.9 %fusion = (f32[576,64]{1,0:T(8,128)}, f32[576,64]{1,0:T(8,128)}) fusion(f32[576,128]{1,0:T(8,128)S(1)} %convert.1), kind=kLoop, calls=%fused_computation | loop fusion | bytes 589824 | tf_op jit(solution)/shard_map/slice | solution.py:331
  (1 shorter events, 0.0 us)
Async XLA Ops:
  0.6 21.6 %copy-start.4 = (bf16[3,3,64,64]{3,2,1,0:T(8,128)(2,1)S(1)}, bf16[3,3,64,64]{3,2,1,0:T(8,128)(2,1)}, u32[]{:S(2)}) copy-start(bf16[3,3,64,64]{3,2,1,0:T(8,128)(2,1)} %two_ref.3) | copy-start | bytes 221188
  2.7 19.5 %copy-start = (bf16[1,2,32,2048]{3,2,1,0:T(8,128)(2,1)S(1)}, bf16[1,2,32,2048]{3,2,1,0:T(8,128)(2,1)}, u32[]{:S(2)}) copy-start(bf16[1,2,32,2048]{3,2,1,0:T(8,128)(2,1)} %param.6) | copy-start | bytes 786436
  2.7 19.5 %copy-start.1 = (bf16[1,2,32,2048]{3,2,1,0:T(8,128)(2,1)S(1)}, bf16[1,2,32,2048]{3,2,1,0:T(8,128)(2,1)}, u32[]{:S(2)}) copy-start(bf16[1,2,32,2048]{3,2,1,0:T(8,128)(2,1)} %param.7) | copy-start | bytes 786436
  2.7 19.5 %copy-start.2 = (s32[1,2,8]{2,1,0:T(2,128)S(1)}, s32[1,2,8]{2,1,0:T(2,128)}, u32[]{:S(2)}) copy-start(s32[1,2,8]{2,1,0:T(2,128)} %param.11) | copy-start | bytes 196
  2.7 19.5 %copy-start.3 = (bf16[3,3,64,64]{3,2,1,0:T(8,128)(2,1)S(1)}, bf16[3,3,64,64]{3,2,1,0:T(8,128)(2,1)}, u32[]{:S(2)}) copy-start(bf16[3,3,64,64]{3,2,1,0:T(8,128)(2,1)} %one_ref.3) | copy-start | bytes 221188
  2.7 19.5 %copy-start.5 = (s32[1,2]{1,0:T(1,128)S(1)}, s32[1,2]{1,0:T(1,128)}, u32[]{:S(2)}) copy-start(s32[1,2]{1,0:T(1,128)} %tissue_hbm.1) | copy-start | bytes 28
  37.3 10.6 %all-to-all-start.2 = ((bf16[32,9,2,128]{3,2,1,0:T(2,128)(2,1)}), bf16[32,9,2,128]{3,2,1,0:T(2,128)(2,1)S(1)}, u32[]{:S(2)}, u32[]{:S(2)}) async-start(bf16[32,9,2,128]{3,2,1,0:T(2,128)(2,1)} %broadcast_in_dim.14), calls=%async_computation.2 | async-start | bytes 294912 | tf_op jit(solution)/shard_map/all_to_all | solution.py:328

commit v9 on v8

v9 whole, which is shorter than its diff:
```python
import functools

import jax
import jax.numpy as jnp
from jax import lax
from jax.experimental import pallas as pl
from jax.experimental.pallas import tpu as pltpu
from jax.sharding import PartitionSpec as P

F32 = jnp.float32
BF16 = jnp.bfloat16
LANES = 128
VMEM = pl.BlockSpec(memory_space=pltpu.VMEM)
ANY = pl.BlockSpec(memory_space=pl.ANY)
PACK_LIMIT = 60 * 2**20


BLOCK = 2 * 48


def strip_row(field, slot):
    return field * 48 + slot * 16


def column_row(field):
    return field * 48 + 32


def forward_weights(source, forward):
    zero = jnp.zeros((LANES // 2, LANES // 2), BF16)
    for a in range(3):
        taps = [source[a, b] for b in range(3)]
        left = jnp.concatenate(taps + [zero], axis=0)
        right = jnp.concatenate([zero] + taps, axis=0)
        forward[a * 256 : (a + 1) * 256, :] = jnp.concatenate([left, right], axis=1)


def back_weights(source, back):
    zero = jnp.zeros((LANES // 2, LANES // 2), BF16)
    for a in range(3):
        turned = [source[2 - a, 2 - b] for b in range(3)]
        upper = jnp.concatenate(turned + [zero], axis=1)
        lower = jnp.concatenate([zero] + turned, axis=1)
        back[:, a * 256 : (a + 1) * 256] = jnp.concatenate([upper, lower], axis=0)


def across(taps, slot, count):
    rows = taps.shape[3]
    parts = [
        taps[slot, a, right : count + right].reshape(count * rows, LANES)
        for a in range(3)
        for right in range(2)
    ]
    return jnp.concatenate(parts, axis=1)


CONTRACT_FIRST = (((0,), (0,)), ((), ()))
CONTRACT_LAST = (((1,), (1,)), ((), ()))


def pack_kernel(
    links_hbm, image_hbm, cotangent_hbm, inner_ref, outer_ref,
    links_ref, image_ref, cotangent_ref, strip_ref, sems,
):
    slots, side, width = image_ref.shape
    pairs = width // LANES
    half = LANES // 2
    copies = [pltpu.make_async_copy(links_hbm, links_ref, sems.at[2 * slots])]
    copies[0].start()
    fields = ((image_hbm, image_ref), (cotangent_hbm, cotangent_ref))
    for field, (source, target) in enumerate(fields):
        for slot in range(slots):
            copy = pltpu.make_async_copy(source.at[slot], target.at[slot], sems.at[field * slots + slot])
            copy.start()
            copies.append(copy)
    me = lax.axis_index("tile")
    left = lax.broadcasted_iota(jnp.int32, (16, LANES), 1) < half
    copies[0].wait()
    for field, (_, ref) in enumerate(fields):
        for slot in range(slots):
            copies[1 + field * slots + slot].wait()
            top = ref[slot, 0:16, :].astype(F32)
            bottom = ref[slot, side - 16 : side, :].astype(F32)
            for pair in range(pairs):
                lanes = slice(pair * LANES, (pair + 1) * LANES)
                strip_ref[0, pair : pair + 1, :] = top[0:1, lanes]
                strip_ref[1, pair : pair + 1, :] = top[1:2, lanes]
                strip_ref[2, pair : pair + 1, :] = bottom[15:16, lanes]
                strip_ref[3, pair : pair + 1, :] = bottom[14:15, lanes]
            for direction in range(8):
                link = links_ref[slot, direction]

                @pl.when(link >= 0)
                def _(slot=slot, direction=direction, link=link, field=field, ref=ref):
                    device = link // slots
                    if direction in (2, 3):
                        first = jnp.where(device == me, strip_row(field, slot), column_row(field))
                        at = pl.ds(pl.multiple_of(first, 16), 16)
                        lanes = slice(0, LANES) if direction == 2 else slice(width - LANES, width)
                        block = ref[slot, :, lanes].astype(F32)
                        other = pltpu.roll(block, half, 1)
                        low = jnp.where(left, block[0:16], other[16:32]).astype(BF16)
                        high = jnp.where(left, other[0:16], block[16:32]).astype(BF16)
                        inner_ref[device, at, :] = low if direction == 2 else high
                        outer_ref[device, at, :] = high if direction == 2 else low
                    else:
                        which = 0 if direction in (0, 4, 5) else 2
                        first = strip_row(field, slot)
                        inner_ref[device, first : first + 16, :] = strip_ref[which].astype(BF16)
                        outer_ref[device, first : first + 16, :] = strip_ref[which + 1].astype(BF16)


def place_halo(links_ref, halos, wide, slot, field, slots, side, pairs, me):
    half = LANES // 2
    left = lax.broadcasted_iota(jnp.int32, (16, LANES), 1) < half
    none = jnp.zeros((16, LANES), F32)
    for direction in range(8):
        link = links_ref[slot, direction]
        device, there = jnp.maximum(link, 0) // slots, jnp.maximum(link, 0) % slots
        first = strip_row(field, 0) + there * 16
        if direction in (2, 3):
            first = jnp.where(device == me, first, column_row(field))
        at = pl.ds(pl.multiple_of(first, 16), 16)
        got = [jnp.where(link >= 0, halo[device, at, :].astype(F32), 0.0) for halo in halos]
        if direction in (2, 3):
            inner, outer = got[0], got[1] if len(got) > 1 else none
            low, high = (outer, inner) if direction == 2 else (inner, outer)
            column = 0 if direction == 2 else pairs + 1
            wide[slot, column, 16:32, :] = jnp.where(left, low, pltpu.roll(high, half, 1))
            wide[slot, column, 32:48, :] = jnp.where(left, pltpu.roll(low, half, 1), high)
        else:
            north = direction in (0, 4, 5)
            for ring, strip in enumerate(got):
                row = 15 - ring if north else 16 + side + ring
                if direction < 2:
                    for pair in range(pairs):
                        wide[slot, pair + 1, row : row + 1, :] = strip[pair : pair + 1, :]
                elif direction in (4, 6):
                    wide[slot, 0, row : row + 1, :] = strip[pairs - 1 : pairs, :]
                else:
                    wide[slot, pairs + 1, row : row + 1, :] = strip[0:1, :]


def place_own(tissue_ref, ref, wide, slot, side, pairs):
    present = tissue_ref[0, slot] > 0
    for pair in range(pairs):
        block = ref[slot, :, pair * LANES : (pair + 1) * LANES].astype(F32)
        wide[slot, pair + 1, 16 : 16 + side, :] = jnp.where(present, block, 0.0)


def shift_rows(field, taps, count, start, rows):
    for pair in range(count):
        for slot in range(field.shape[0]):
            for a in range(3):
                taps[slot, a, pair] = field[slot, pair, start + a - 1 : start + a - 1 + rows, :].astype(BF16)


def grads_kernel(
    links_hbm, tissue_hbm, image_ref, cotangent_ref, inner_ref, one_ref, two_ref,
    grads_ref,
    links_ref, tissue_ref, wide_in, wide_up, own_hidden, own_delta,
    taps_in, taps_up, forward_ref, back_ref, acc_ref, sems,
):
    slots, side, width = image_ref.shape
    pairs = width // LANES
    half = LANES // 2
    me = lax.axis_index("tile")

    small = [
        pltpu.make_async_copy(tissue_hbm, tissue_ref, sems.at[0]),
        pltpu.make_async_copy(links_hbm, links_ref, sems.at[1]),
    ]
    for copy in small:
        copy.start()
    forward_weights(one_ref, forward_ref)
    back_weights(two_ref, back_ref)
    for copy in small:
        copy.wait()
    for field, (ref, wide) in enumerate(((image_ref, wide_in), (cotangent_ref, wide_up))):
        for slot in range(slots):
            place_own(tissue_ref, ref, wide, slot, side, pairs)
            place_halo(links_ref, (inner_ref,), wide, slot, field, slots, side, pairs, me)
    shift_rows(wide_in, taps_in, pairs + 2, 16, side)
    shift_rows(wide_up, taps_up, pairs + 2, 16, side)

    left = lax.broadcasted_iota(jnp.int32, (side, LANES), 1) < half
    first_grad = None
    second_grad = None
    for slot in range(slots):
        before = jnp.dot(across(taps_in, slot, pairs + 1), forward_ref[...], preferred_element_type=F32)
        acc_ref[slot, 0] = before.reshape(pairs + 1, side, LANES)
        after = lax.dot_general(
            across(taps_up, slot, pairs + 1), back_ref[...], CONTRACT_LAST, preferred_element_type=F32
        )
        acc_ref[slot, 1] = after.reshape(pairs + 1, side, LANES)
        for pair in range(pairs + 1):
            hidden = jnp.maximum(acc_ref[slot, 0, pair], 0.0)
            if pair == 0:
                hidden = jnp.where(left, 0.0, hidden)
            if pair == pairs:
                hidden = jnp.where(left, hidden, 0.0)
            hidden = hidden.astype(BF16)
            own_hidden[slot, pair] = hidden
            delta = jnp.where(hidden.astype(F32) > 0, acc_ref[slot, 1, pair], 0.0)
            own_delta[slot, pair] = delta.astype(BF16)
        term_one = lax.dot_general(
            own_delta[slot].reshape((pairs + 1) * side, LANES), across(taps_in, slot, pairs + 1),
            CONTRACT_FIRST, preferred_element_type=F32,
        )
        term_two = lax.dot_general(
            own_hidden[slot].reshape((pairs + 1) * side, LANES), across(taps_up, slot, pairs + 1),
            CONTRACT_FIRST, preferred_element_type=F32,
        )
        first_grad = term_one if first_grad is None else first_grad + term_one
        second_grad = term_two if second_grad is None else second_grad + term_two

    total = grads_ref.shape[0]
    left = lax.broadcasted_iota(jnp.int32, (half, LANES), 1) < half
    for a in range(3):
        one = first_grad[:, a * 256 : (a + 1) * 256].T
        two = second_grad[:, (2 - a) * 256 : (3 - a) * 256]
        blocks = [two[:half, 0:LANES], two[:half, LANES:256], two[half:, 0:LANES], two[half:, LANES:256]]
        turned = [pltpu.roll(block, half, 1) for block in blocks]
        right = (turned[0] + blocks[2], blocks[0] + turned[3], turned[1] + blocks[3])
        for b in range(3):
            upper = one[b * half : (b + 1) * half]
            lower = one[(b + 1) * half : (b + 2) * half]
            rows = slice((a * 3 + b) * half, (a * 3 + b + 1) * half)
            both = jnp.where(left, upper + pltpu.roll(lower, half, 1), right[2 - b])
            grads_ref[rows, :] = both.astype(BF16)
    if total > 576:
        grads_ref[576:total, :] = jnp.zeros((total - 576, LANES), BF16)


def fields_kernel(
    links_hbm, tissue_hbm, image_ref, cotangent_ref, inner_ref, outer_ref, one_ref, two_ref,
    output_hbm, grad_input_hbm,
    links_ref, tissue_ref, wide_in, wide_up, narrow_hidden, narrow_delta,
    taps_in, taps_up, taps_hidden, taps_delta, forward_one, forward_two, back_one, back_two,
    acc_ref, output_ref, grad_input_ref, sems,
):
    slots, side, width = image_ref.shape
    pairs = width // LANES
    half = LANES // 2
    tall = side + 16
    me = lax.axis_index("tile")

    small = [
        pltpu.make_async_copy(tissue_hbm, tissue_ref, sems.at[2 * slots]),
        pltpu.make_async_copy(links_hbm, links_ref, sems.at[2 * slots + 1]),
    ]
    for copy in small:
        copy.start()
    forward_weights(one_ref, forward_one)
    forward_weights(two_ref, forward_two)
    back_weights(one_ref, back_one)
    back_weights(two_ref, back_two)
    for copy in small:
        copy.wait()
    for field, (ref, wide) in enumerate(((image_ref, wide_in), (cotangent_ref, wide_up))):
        wide[:, :, 0:16, :] = jnp.zeros((slots, pairs + 2, 16, LANES), F32)
        wide[:, :, 16 + side : 32 + side, :] = jnp.zeros((slots, pairs + 2, 16, LANES), F32)
        for slot in range(slots):
            place_own(tissue_ref, ref, wide, slot, side, pairs)
            place_halo(links_ref, (inner_ref, outer_ref), wide, slot, field, slots, side, pairs, me)
    shift_rows(wide_in, taps_in, pairs + 2, 8, tall)
    shift_rows(wide_up, taps_up, pairs + 2, 8, tall)

    row = lax.broadcasted_iota(jnp.int32, (tall, LANES), 0)
    lane = lax.broadcasted_iota(jnp.int32, (tall, LANES), 1)

    def column_mask(north, here, south):
        value = jnp.where(row == 7, north, jnp.where(row == 8 + side, south, here))
        return jnp.where((row >= 7) & (row <= 8 + side), value, 0)

    for slot in range(slots):
        there = [(links_ref[slot, k] >= 0).astype(jnp.int32) for k in range(8)]
        own = tissue_ref[0, slot]
        middle = column_mask(there[0], own, there[1])
        west = jnp.where(lane < half, column_mask(there[4], there[2], there[6]), middle)
        east = jnp.where(lane < half, middle, column_mask(there[5], there[3], there[7]))
        before = jnp.dot(across(taps_in, slot, pairs + 1), forward_one[...], preferred_element_type=F32)
        acc_ref[slot, 0] = before.reshape(pairs + 1, tall, LANES)
        after = lax.dot_general(
            across(taps_up, slot, pairs + 1), back_two[...], CONTRACT_LAST, preferred_element_type=F32
        )
        acc_ref[slot, 1] = after.reshape(pairs + 1, tall, LANES)
        for pair in range(pairs + 1):
            mask = west if pair == 0 else east if pair == pairs else middle
            hidden = jnp.where(mask > 0, jnp.maximum(acc_ref[slot, 0, pair], 0.0), 0.0)
            hidden = hidden.astype(BF16).astype(F32)
            narrow_hidden[slot, pair] = hidden
            narrow_delta[slot, pair] = jnp.where(hidden > 0, acc_ref[slot, 1, pair], 0.0)
    shift_rows(narrow_hidden, taps_hidden, pairs + 1, 8, side)
    shift_rows(narrow_delta, taps_delta, pairs + 1, 8, side)

    copies = []
    for slot in range(slots):
        out = jnp.dot(across(taps_hidden, slot, pairs), forward_two[...], preferred_element_type=F32)
        back = lax.dot_general(
            across(taps_delta, slot, pairs), back_one[...], CONTRACT_LAST, preferred_element_type=F32
        )
        for pair in range(pairs):
            lanes = slice(pair * LANES, (pair + 1) * LANES)
            rows = slice(pair * side, (pair + 1) * side)
            output_ref[slot, :, lanes] = out[rows].astype(BF16)
            grad_input_ref[slot, :, lanes] = back[rows].astype(BF16)
        for k, (source, target) in enumerate(((output_ref, output_hbm), (grad_input_ref, grad_input_hbm))):
            copies.append(pltpu.make_async_copy(source.at[slot], target.at[slot], sems.at[2 * slot + k]))
            copies[-1].start()
    for copy in copies:
        copy.wait()


def local(slide_image, cotangent, weight_one, weight_two, tissue, neighbours):
    devices_tile = lax.axis_size("tile")
    devices = devices_tile * lax.axis_size("slide")
    _, slots, side, width = slide_image.shape
    pairs = width // LANES
    tall = side + 16
    image, upstream = slide_image[0], cotangent[0]
    links = neighbours[0]
    block = jax.ShapeDtypeStruct((devices_tile, BLOCK, LANES), BF16)
    packed_inner, packed_outer = pl.pallas_call(
        pack_kernel,
        out_shape=(block, block),
        in_specs=[ANY] * 3,
        out_specs=(VMEM, VMEM),
        scratch_shapes=[
            pltpu.SMEM(links.shape, jnp.int32),
            pltpu.VMEM(image.shape, BF16),
            pltpu.VMEM(image.shape, BF16),
            pltpu.VMEM((4, 16, LANES), F32),
            pltpu.SemaphoreType.DMA((2 * slots + 1,)),
        ],
        compiler_params=pltpu.CompilerParams(vmem_limit_bytes=PACK_LIMIT),
        name="pack",
    )(links, image, upstream)
    inner = lax.all_to_all(packed_inner, "tile", 0, 0, tiled=True)
    outer = lax.all_to_all(packed_outer, "tile", 0, 0, tiled=True)

    chunk = -(-576 // (2 * devices))
    total = 2 * chunk * devices
    wide = pltpu.VMEM((slots, pairs + 2, side + 32, LANES), F32)
    weights = [pltpu.VMEM((768, LANES), BF16), pltpu.VMEM((LANES, 768), BF16)]
    cost = pl.CostEstimate(flops=4 * 10**9, bytes_accessed=10**7, transcendentals=0)
    grads = pl.pallas_call(
        grads_kernel,
        out_shape=jax.ShapeDtypeStruct((total, LANES), BF16),
        in_specs=[ANY, ANY] + [VMEM] * 5,
        out_specs=VMEM,
        scratch_shapes=[
            pltpu.SMEM(links.shape, jnp.int32),
            pltpu.SMEM(tissue.shape, jnp.int32),
            wide,
            wide,
            pltpu.VMEM((slots, pairs + 1, side, LANES), BF16),
            pltpu.VMEM((slots, pairs + 1, side, LANES), BF16),
            pltpu.VMEM((slots, 3, pairs + 2, side, LANES), BF16),
            pltpu.VMEM((slots, 3, pairs + 2, side, LANES), BF16),
            *weights,
            pltpu.VMEM((slots, 2, pairs + 1, side, LANES), F32),
            pltpu.SemaphoreType.DMA((2,)),
        ],
        compiler_params=pltpu.CompilerParams(vmem_limit_bytes=32 * 2**20),
        cost_estimate=cost,
        name="grads",
    )(links, tissue, image, upstream, inner, weight_one, weight_two)
    output, grad_input = pl.pallas_call(
        fields_kernel,
        out_shape=(jax.ShapeDtypeStruct((slots, side, width), BF16),) * 2,
        in_specs=[ANY, ANY] + [VMEM] * 6,
        out_specs=(ANY, ANY),
        scratch_shapes=[
            pltpu.SMEM(links.shape, jnp.int32),
            pltpu.SMEM(tissue.shape, jnp.int32),
            wide,
            wide,
            pltpu.VMEM((slots, pairs + 1, tall, LANES), F32),
            pltpu.VMEM((slots, pairs + 1, tall, LANES), F32),
            pltpu.VMEM((slots, 3, pairs + 2, tall, LANES), BF16),
            pltpu.VMEM((slots, 3, pairs + 2, tall, LANES), BF16),
            pltpu.VMEM((slots, 3, pairs + 1, side, LANES), BF16),
            pltpu.VMEM((slots, 3, pairs + 1, side, LANES), BF16),
            weights[0],
            weights[0],
            weights[1],
            weights[1],
            pltpu.VMEM((slots, 2, pairs + 1, tall, LANES), F32),
            pltpu.VMEM((slots, side, width), BF16),
            pltpu.VMEM((slots, side, width), BF16),
            pltpu.SemaphoreType.DMA((2 * slots + 2,)),
        ],
        compiler_params=pltpu.CompilerParams(vmem_limit_bytes=40 * 2**20),
        cost_estimate=cost,
        name="fields",
    )(links, tissue, image, upstream, inner, outer, weight_one, weight_two)

    parts = lax.all_to_all(grads.reshape(devices, chunk, 2, LANES), ("slide", "tile"), 0, 0, tiled=True)
    mine = jnp.sum(lax.optimization_barrier(parts.astype(F32)), axis=0).astype(BF16)
    sums = jnp.broadcast_to(mine[None], parts.shape)
    whole = lax.all_to_all(sums, ("slide", "tile"), 0, 0, tiled=True)
    whole = lax.optimization_barrier(whole.reshape(total, LANES).astype(F32))
    grad_one = whole[:576, : LANES // 2]
    grad_two = whole[:576, LANES // 2 :]
    shape = weight_one.shape
    return output[None], grad_input[None], grad_one.reshape(shape), grad_two.reshape(shape)


def solution(mesh):
    placed = (
        P("slide", "tile", None, None),
        P("slide", "tile", None, None),
        P(),
        P(),
        P("slide", "tile"),
        P("slide", "tile", None),
    )
    return jax.shard_map(
        local,
        mesh=mesh,
        in_specs=placed,
        out_specs=(P("slide", "tile", None, None), P("slide", "tile", None, None), P(), P()),
        check_vma=False,
    )
```

time: 49.1 us -> 56.2 us (1.14)
  waiting for transfers between devices: 6 us -> 11.9 us
  blocking collectives: 30.4 us -> 26.1 us
  starting transfers between devices: 2.72 us -> 6.25 us
  Pallas kernels: 7.01 us -> 8.96 us
    all_to_all x0 -> x1, waiting for transfers between devices: none -> 8.05 us  [local(): outer = lax.all_to_all(packed_outer, 'tile', 0, 0, tiled=True)]
    all_to_all x1, blocking collectives: 19.5 us -> 15.3 us  [local(): inner = lax.all_to_all(packed_inner, 'tile', 0, 0, tiled=True)]
    all_to_all x0 -> x1, starting transfers between devices: none -> 3.58 us  [local(): outer = lax.all_to_all(packed_outer, 'tile', 0, 0, tiled=True)]
    all_to_all x1, waiting for transfers between devices: 6 us -> 3.81 us  [local(): whole = lax.all_to_all(sums, ('slide', 'tile'), 0, 0, tiled=True)]
    pallas_call x3, Pallas kernels: 7.01 us -> 8.96 us  [the longest x1 4.01 us: local(): pl.pallas_call(fields_kernel, out_shape=(jax.ShapeDtypeStruct((slots, sid...]
  transfers between devices with their start and end apart: 1 -> 2, of which waited for: 1 -> 2; matrix products, arithmetic and copies ran while one was open for 0% -> 0% of each run, Pallas kernels for 4% -> 7%
where the time goes in v9:
time: 56.2 us; the launch traced here: 55.8 us
  blocking collectives  26.1 us (46%)
  waiting for transfers between devices  11.9 us (21%)
  Pallas kernels  8.96 us (16%)
  starting transfers between devices  6.25 us (11%)
  local copies, waits for them, and re-layouts  1.66 us (3%)
  between operations  0.75 us (1%)
    all_to_all x1, blocking collectives, local(): inner = lax.all_to_all(packed_inner, 'tile', 0, 0, tiled=True)  15.3 us
    all_to_all x1, blocking collectives, local(): lax.all_to_all(grads.reshape(devices, chunk, 2, LANES), ('slide', 'tile')...  10.8 us
    all_to_all x1, waiting for transfers between devices, local(): outer = lax.all_to_all(packed_outer, 'tile', 0, 0, tiled=True)  8.05 us
    pallas_call x1, Pallas kernels, local(): pl.pallas_call(fields_kernel, out_shape=(jax.ShapeDtypeStruct((slots, sid...  4.01 us
    all_to_all x1, waiting for transfers between devices, local(): whole = lax.all_to_all(sums, ('slide', 'tile'), 0, 0, tiled=True)  3.81 us
    all_to_all x1, starting transfers between devices, local(): outer = lax.all_to_all(packed_outer, 'tile', 0, 0, tiled=True)  3.58 us
    pallas_call x1, Pallas kernels, local(): pl.pallas_call(grads_kernel, out_shape=jax.ShapeDtypeStruct((total, LANES...  2.82 us
    all_to_all x1, starting transfers between devices, local(): whole = lax.all_to_all(sums, ('slide', 'tile'), 0, 0, tiled=True)  2.66 us
  transfers between devices with their start and end apart: 2, of which 2 were waited for; matrix products, arithmetic and copies ran while one was open for 0% of the time, Pallas kernels for 7%

profile of v9, /device:TPU:0, one launch (start us, length us, event | category | flops | bytes accessed | tf_op | source)
XLA Modules:
  0.0 55.8 jit_solution(4983521068960849164)
XLA Ops:
  0.6 0.0 copy-start.1
  0.6 0.0 copy-start.3
  0.7 0.0 copy-start.4
  0.7 2.1 %pack.1 = (bf16[8,96,128]{2,1,0:T(8,128)(2,1)}, bf16[8,96,128]{2,1,0:T(8,128)(2,1)}) custom-call(s32[2,8]{1,0:T(2,128)} %bitcast.17, bf16[2,32,2048]{2,1,0:T(8,128)(2,1)} %bitcast.10, bf16[2,32,2048]{2,1,0:T(8,128)(2,1)} %bitcast.13), custom_call_target="tpu_custom_call" | custom-call | tf_op jit(solution)/shard_map/pack/pallas_call | solution.py:324
  2.8 0.0 copy-start
  2.8 0.0 copy-start.2
  2.8 0.0 copy-start.5
  2.8 15.3 %all_to_all.20.inner_ref = bf16[8,96,128]{2,1,0:T(8,128)(2,1)S(1)} all-to-all(bf16[8,96,128]{2,1,0:T(8,128)(2,1)} %get-tuple-element.8), channel_id=1, replica_groups=mesh['slide'=4,'tile'=8] {'tile'}, dimensions={0} | all-to-all | bytes 393216 | tf_op jit(solution)/shard_map/all_to_all | solution.py:339
  18.1 0.0 copy-done.1
  18.1 0.0 copy-done.3
  18.1 0.0 copy-done.4
  18.1 0.0 copy-done
  18.2 0.0 copy-done.2
  18.2 0.0 copy-done.5
  18.2 2.8 %grads.1 = bf16[576,128]{1,0:T(8,128)(2,1)S(1)} custom-call(s32[2,8]{1,0:T(2,128)S(1)} %bitcast.18, s32[1,2]{1,0:T(1,128)S(1)} %copy-done.5, bf16[2,32,2048]{2,1,0:T(8,128)(2,1)S(1)} %bitcast.11, bf16[2,32,2048]{2,1,0:T(8,128)(2,1)S(1)} %bitcast.14, bf16[8,96,128]{2,1,0:T(8,128)(2,1)S(1)} %all_to_all.20.inner_ref, bf16[3,3,64,64]{3,2,1,0:T(8,128)(2,1)S(1)} %copy-done.3, ...), custom_call_target="tpu_custom_call" | custom-call | flops 4000000000 | bytes 10000000 | tf_op jit(solution)/shard_map/grads/pallas_call | solution.py:347
  21.0 10.8 %all_to_all.21 = bf16[32,9,2,128]{3,2,1,0:T(2,128)(2,1)S(1)} all-to-all(bf16[32,9,2,128]{3,2,1,0:T(2,128)(2,1)S(1)} %bitcast.16), channel_id=1, replica_groups=mesh['slide'=4,'tile'=8] {'slide','tile'}, dimensions={0} | all-to-all | bytes 294912 | tf_op jit(solution)/shard_map/all_to_all | solution.py:399
  31.8 3.6 %all-to-all-start.1 = ((bf16[8,96,128]{2,1,0:T(8,128)(2,1)}), bf16[8,96,128]{2,1,0:T(8,128)(2,1)S(1)}, u32[]{:S(2)}, u32[]{:S(2)}) async-start(bf16[8,96,128]{2,1,0:T(8,128)(2,1)} %get-tuple-element.9), calls=%async_computation.1 | async-start | bytes 393216 | tf_op jit(solution)/shard_map/all_to_all | solution.py:340
  35.4 0.1 convert_element_type.16
  35.5 0.1 reduce_sum.9
  35.6 8.1 %all-to-all-done.1.outer_ref = bf16[8,96,128]{2,1,0:T(8,128)(2,1)S(1)} async-done(((bf16[8,96,128]{2,1,0:T(8,128)(2,1)}), bf16[8,96,128]{2,1,0:T(8,128)(2,1)S(1)}, u32[]{:S(2)}, u32[]{:S(2)}) %all-to-all-start.1) | async-done | bytes 196640 | tf_op jit(solution)/shard_map/all_to_all | solution.py:340
  43.7 0.7 %broadcast_in_dim.14 = bf16[32,9,2,128]{3,2,1,0:T(2,128)(2,1)} broadcast(bf16[9,2,128]{2,1,0:T(2,128)(2,1)S(1)} %reduce_sum.9), dimensions={1,2,3} | broadcast | bytes 152064 | tf_op jit(solution)/shard_map/broadcast_in_dim | solution.py:401
  44.4 2.7 %all-to-all-start.3 = ((bf16[32,9,2,128]{3,2,1,0:T(2,128)(2,1)}), bf16[32,9,2,128]{3,2,1,0:T(2,128)(2,1)S(1)}, u32[]{:S(2)}, u32[]{:S(2)}) async-start(bf16[32,9,2,128]{3,2,1,0:T(2,128)(2,1)} %broadcast_in_dim.14), calls=%async_computation.3 | async-start | bytes 294912 | tf_op jit(solution)/shard_map/all_to_all | solution.py:402
  47.1 4.0 %fields.1 = (bf16[2,32,2048]{2,1,0:T(8,128)(2,1)}, bf16[2,32,2048]{2,1,0:T(8,128)(2,1)}) custom-call(s32[2,8]{1,0:T(2,128)S(1)} %bitcast.19, s32[1,2]{1,0:T(1,128)S(1)} %copy-done.5, bf16[2,32,2048]{2,1,0:T(8,128)(2,1)S(1)} %bitcast.12, bf16[2,32,2048]{2,1,0:T(8,128)(2,1)S(1)} %bitcast.15, bf16[8,96,128]{2,1,0:T(8,128)(2,1)S(1)} %all_to_all.20.inner_ref, ...), custom_call_target="tpu_custom_call" | custom-call | flops 4000000000 | bytes 10000000 | tf_op jit(solution)/shard_map/fields/pallas_call | solution.py:369
  51.1 3.8 %all-to-all-done.3 = bf16[32,9,2,128]{3,2,1,0:T(2,128)(2,1)S(1)} async-done(((bf16[32,9,2,128]{3,2,1,0:T(2,128)(2,1)}), bf16[32,9,2,128]{3,2,1,0:T(2,128)(2,1)S(1)}, u32[]{:S(2)}, u32[]{:S(2)}) %all-to-all-start.3) | async-done | bytes 147488 | tf_op jit(solution)/shard_map/all_to_all | solution.py:402
  55.0 0.9 %fusion = (f32[576,64]{1,0:T(8,128)}, f32[576,64]{1,0:T(8,128)}) fusion(f32[576,128]{1,0:T(8,128)S(1)} %convert.1), kind=kLoop, calls=%fused_computation | loop fusion | bytes 589824 | tf_op jit(solution)/shard_map/slice | solution.py:405
  (1 shorter events, 0.0 us)
Async XLA Ops:
  0.6 17.5 %copy-start.1 = (bf16[1,2,32,2048]{3,2,1,0:T(8,128)(2,1)S(1)}, bf16[1,2,32,2048]{3,2,1,0:T(8,128)(2,1)}, u32[]{:S(2)}) copy-start(bf16[1,2,32,2048]{3,2,1,0:T(8,128)(2,1)} %param.7) | copy-start | bytes 786436
  0.6 17.5 %copy-start.3 = (bf16[3,3,64,64]{3,2,1,0:T(8,128)(2,1)S(1)}, bf16[3,3,64,64]{3,2,1,0:T(8,128)(2,1)}, u32[]{:S(2)}) copy-start(bf16[3,3,64,64]{3,2,1,0:T(8,128)(2,1)} %one_ref.3) | copy-start | bytes 221188
  0.7 17.5 %copy-start.4 = (bf16[3,3,64,64]{3,2,1,0:T(8,128)(2,1)S(1)}, bf16[3,3,64,64]{3,2,1,0:T(8,128)(2,1)}, u32[]{:S(2)}) copy-start(bf16[3,3,64,64]{3,2,1,0:T(8,128)(2,1)} %two_ref.3) | copy-start | bytes 221188
  2.8 15.3 %copy-start = (bf16[1,2,32,2048]{3,2,1,0:T(8,128)(2,1)S(1)}, bf16[1,2,32,2048]{3,2,1,0:T(8,128)(2,1)}, u32[]{:S(2)}) copy-start(bf16[1,2,32,2048]{3,2,1,0:T(8,128)(2,1)} %param.6) | copy-start | bytes 786436
  2.8 15.3 %copy-start.2 = (s32[1,2,8]{2,1,0:T(2,128)S(1)}, s32[1,2,8]{2,1,0:T(2,128)}, u32[]{:S(2)}) copy-start(s32[1,2,8]{2,1,0:T(2,128)} %param.11) | copy-start | bytes 196
  2.8 15.3 %copy-start.5 = (s32[1,2]{1,0:T(1,128)S(1)}, s32[1,2]{1,0:T(1,128)}, u32[]{:S(2)}) copy-start(s32[1,2]{1,0:T(1,128)} %tissue_hbm.3) | copy-start | bytes 28
  31.8 11.9 %all-to-all-start.1 = ((bf16[8,96,128]{2,1,0:T(8,128)(2,1)}), bf16[8,96,128]{2,1,0:T(8,128)(2,1)S(1)}, u32[]{:S(2)}, u32[]{:S(2)}) async-start(bf16[8,96,128]{2,1,0:T(8,128)(2,1)} %get-tuple-element.9), calls=%async_computation.1 | async-start | bytes 393216 | tf_op jit(solution)/shard_map/all_to_all | solution.py:340
  44.4 10.5 %all-to-all-start.3 = ((bf16[32,9,2,128]{3,2,1,0:T(2,128)(2,1)}), bf16[32,9,2,128]{3,2,1,0:T(2,128)(2,1)S(1)}, u32[]{:S(2)}, u32[]{:S(2)}) async-start(bf16[32,9,2,128]{3,2,1,0:T(2,128)(2,1)} %broadcast_in_dim.14), calls=%async_computation.3 | async-start | bytes 294912 | tf_op jit(solution)/shard_map/all_to_all | solution.py:402

commit v10 on v7

--- a/solution.py
+++ b/solution.py
@@ -233,6 +233,16 @@
         grads_ref[576:total, :] = jnp.zeros((total - 576, LANES), BF16)
     for copy in copies:
         copy.wait()
+
+
+def summed(blocks, axis):
+    parts = lax.all_to_all(blocks, axis, 0, 0, tiled=True)
+    return jnp.sum(lax.optimization_barrier(parts.astype(F32)), axis=0).astype(BF16)
+
+
+def gathered(share, count, axis):
+    copies = jnp.broadcast_to(share[None], (count,) + share.shape)
+    return lax.all_to_all(copies, axis, 0, 0, tiled=True)
 
 
 def local(slide_image, cotangent, weight_one, weight_two, tissue, neighbours):
@@ -293,11 +303,12 @@
         name="mix",
     )(links, tissue, image, upstream, halo, weight_one, weight_two)
 
-    parts = lax.all_to_all(grads.reshape(devices, chunk, 2, LANES), ("slide", "tile"), 0, 0, tiled=True)
-    mine = jnp.sum(lax.optimization_barrier(parts.astype(F32)), axis=0).astype(BF16)
-    sums = jnp.broadcast_to(mine[None], parts.shape)
-    whole = lax.all_to_all(sums, ("slide", "tile"), 0, 0, tiled=True)
-    whole = lax.optimization_barrier(whole.reshape(total, LANES).astype(F32))
+    slides = devices // devices_tile
+    share = summed(grads.reshape(slides, devices_tile * chunk, 2, LANES), "slide")
+    share = summed(share.reshape(devices_tile, chunk, 2, LANES), "tile")
+    share = gathered(share, devices_tile, "tile").reshape(devices_tile * chunk, 2, LANES)
+    whole = gathered(share, slides, "slide").reshape(total, LANES)
+    whole = lax.optimization_barrier(whole.astype(F32))
     grad_one = whole[:576, : LANES // 2]
     grad_two = whole[:576, LANES // 2 :]
     shape = weight_one.shape

time: 48.8 us -> 61.2 us (1.25)
  blocking collectives: 40.7 us -> 52.8 us
    all_to_all x2 -> x4, blocking collectives: 21.2 us -> 33.3 us  [the longest x2 17.1 us: summed(): parts = lax.all_to_all(blocks, axis, 0, 0, tiled=True)]
where the time goes in v10:
time: 61.2 us; the launch traced here: 60.8 us
  blocking collectives  52.8 us (86%)
  Pallas kernels  5.86 us (10%)
  local copies, waits for them, and re-layouts  1.03 us (2%)
  between operations  0.76 us (1%)
    all_to_all x1, blocking collectives, local(): halo = lax.all_to_all(packed, 'tile', 0, 0, tiled=True)  19.5 us
    all_to_all x2, blocking collectives, summed(): parts = lax.all_to_all(blocks, axis, 0, 0, tiled=True)  17.1 us
    all_to_all x2, blocking collectives, gathered(): return lax.all_to_all(copies, axis, 0, 0, tiled=True)  16.2 us
    pallas_call x1, Pallas kernels, local(): pl.pallas_call(mix_kernel, out_shape=(jax.ShapeDtypeStruct((slots, side,...  3.81 us
    pallas_call x1, Pallas kernels, local(): pl.pallas_call(pack_kernel, out_shape=jax.ShapeDtypeStruct((devices_tile,...  2.05 us

profile of v10, /device:TPU:0, one launch (start us, length us, event | category | flops | bytes accessed | tf_op | source)
XLA Modules:
  0.0 60.8 jit_solution(15775841720955583959)
XLA Ops:
  0.6 0.0 copy-start.3
  0.6 2.0 %pack.1 = bf16[8,192,128]{2,1,0:T(8,128)(2,1)} custom-call(s32[2,8]{1,0:T(2,128)} %bitcast.17, bf16[2,32,2048]{2,1,0:T(8,128)(2,1)} %bitcast.12, bf16[2,32,2048]{2,1,0:T(8,128)(2,1)} %bitcast.14), custom_call_target="tpu_custom_call" | custom-call | tf_op jit(solution)/shard_map/pack/pallas_call | solution.py:256
  2.7 0.0 copy-start
  2.7 0.0 copy-start.1
  2.7 0.0 copy-start.2
  2.7 0.0 copy-start.4
  2.7 0.0 copy-start.5
  2.8 19.5 %all_to_all.25.halo_ref = bf16[8,192,128]{2,1,0:T(8,128)(2,1)S(1)} all-to-all(bf16[8,192,128]{2,1,0:T(8,128)(2,1)} %pack.1), channel_id=1, replica_groups=mesh['slide'=4,'tile'=8] {'tile'}, dimensions={0} | all-to-all | bytes 786432 | tf_op jit(solution)/shard_map/all_to_all | solution.py:271
  22.3 0.0 copy-done.3
  22.3 0.0 copy-done
  22.3 0.0 copy-done.1
  22.3 0.0 copy-done.2
  22.3 0.0 copy-done.4
  22.3 0.0 copy-done.5
  22.3 3.8 %mix.1 = (bf16[2,32,2048]{2,1,0:T(8,128)(2,1)}, bf16[2,32,2048]{2,1,0:T(8,128)(2,1)}, bf16[576,128]{1,0:T(8,128)(2,1)S(1)}) custom-call(s32[2,8]{1,0:T(2,128)S(1)} %bitcast.18, s32[1,2]{1,0:T(1,128)S(1)} %copy-done.5, bf16[2,32,2048]{2,1,0:T(8,128)(2,1)S(1)} %bitcast.13, bf16[2,32,2048]{2,1,0:T(8,128)(2,1)S(1)} %bitcast.15, ...), custom_call_target="tpu_custom_call" | custom-call | tf_op jit(solution)/shard_map/mix/pallas_call | solution.py:275
  26.1 7.3 %all_to_all.26 = bf16[4,72,2,128]{3,2,1,0:T(2,128)(2,1)S(1)} all-to-all(bf16[4,72,2,128]{3,2,1,0:T(2,128)(2,1)S(1)} %bitcast.16), channel_id=1, replica_groups=mesh['slide'=4,'tile'=8] {'slide'}, dimensions={0} | all-to-all | bytes 294912 | tf_op jit(solution)/shard_map/all_to_all | solution.py:239
  33.5 0.1 convert_element_type.26
  33.6 0.1 reduce_sum.18
  33.7 9.7 %all_to_all.27 = bf16[8,9,2,128]{3,2,1,0:T(2,128)(2,1)S(1)} all-to-all(bf16[8,9,2,128]{3,2,1,0:T(2,128)(2,1)S(1)} %bitcast.22), channel_id=1, replica_groups=mesh['slide'=4,'tile'=8] {'tile'}, dimensions={0} | all-to-all | bytes 73728 | tf_op jit(solution)/shard_map/all_to_all | solution.py:239
  43.6 9.1 %all_to_all.28 = bf16[8,9,2,128]{3,2,1,0:T(2,128)(2,1)S(1)} all-to-all(bf16[8,9,2,128]{3,2,1,0:T(2,128)(2,1)S(1)} %broadcast_in_dim.21), channel_id=1, replica_groups=mesh['slide'=4,'tile'=8] {'tile'}, dimensions={0} | all-to-all | bytes 73728 | tf_op jit(solution)/shard_map/all_to_all | solution.py:245
  52.6 0.1 broadcast_in_dim.23
  52.7 7.2 %all_to_all.29 = bf16[4,72,2,128]{3,2,1,0:T(2,128)(2,1)S(1)} all-to-all(bf16[4,72,2,128]{3,2,1,0:T(2,128)(2,1)S(1)} %broadcast_in_dim.23), channel_id=1, replica_groups=mesh['slide'=4,'tile'=8] {'slide'}, dimensions={0} | all-to-all | bytes 294912 | tf_op jit(solution)/shard_map/all_to_all | solution.py:245
  59.9 0.9 %fusion = (f32[576,64]{1,0:T(8,128)}, f32[576,64]{1,0:T(8,128)}) fusion(f32[576,128]{1,0:T(8,128)S(1)} %convert.1), kind=kLoop, calls=%fused_computation | loop fusion | bytes 589824 | tf_op jit(solution)/shard_map/slice | solution.py:313
  (4 shorter events, 0.1 us)
Async XLA Ops:
  0.6 21.7 %copy-start.3 = (bf16[3,3,64,64]{3,2,1,0:T(8,128)(2,1)S(1)}, bf16[3,3,64,64]{3,2,1,0:T(8,128)(2,1)}, u32[]{:S(2)}) copy-start(bf16[3,3,64,64]{3,2,1,0:T(8,128)(2,1)} %two_ref.1) | copy-start | bytes 221188
  2.7 19.6 %copy-start = (bf16[1,2,32,2048]{3,2,1,0:T(8,128)(2,1)S(1)}, bf16[1,2,32,2048]{3,2,1,0:T(8,128)(2,1)}, u32[]{:S(2)}) copy-start(bf16[1,2,32,2048]{3,2,1,0:T(8,128)(2,1)} %param.6) | copy-start | bytes 786436
  2.7 19.6 %copy-start.1 = (bf16[1,2,32,2048]{3,2,1,0:T(8,128)(2,1)S(1)}, bf16[1,2,32,2048]{3,2,1,0:T(8,128)(2,1)}, u32[]{:S(2)}) copy-start(bf16[1,2,32,2048]{3,2,1,0:T(8,128)(2,1)} %param.7) | copy-start | bytes 786436
  2.7 19.6 %copy-start.2 = (bf16[3,3,64,64]{3,2,1,0:T(8,128)(2,1)S(1)}, bf16[3,3,64,64]{3,2,1,0:T(8,128)(2,1)}, u32[]{:S(2)}) copy-start(bf16[3,3,64,64]{3,2,1,0:T(8,128)(2,1)} %one_ref.1) | copy-start | bytes 221188
  2.7 19.6 %copy-start.4 = (s32[1,2,8]{2,1,0:T(2,128)S(1)}, s32[1,2,8]{2,1,0:T(2,128)}, u32[]{:S(2)}) copy-start(s32[1,2,8]{2,1,0:T(2,128)} %param.11) | copy-start | bytes 196
  2.7 19.6 %copy-start.5 = (s32[1,2]{1,0:T(1,128)S(1)}, s32[1,2]{1,0:T(1,128)}, u32[]{:S(2)}) copy-start(s32[1,2]{1,0:T(1,128)} %tissue_hbm.1) | copy-start | bytes 28

commit v11 on v7

--- a/solution.py
+++ b/solution.py
@@ -15,15 +15,11 @@
 PACK_LIMIT = 60 * 2**20
 
 
-BLOCK = 2 * 96
+BLOCK = 2 * 64
 
 
 def strip_row(field, slot):
-    return field * 96 + slot * 32
-
-
-def column_row(field):
-    return field * 96 + 64
+    return field * 64 + slot * 32
 
 
 def band_weights(source, forward, back):
@@ -54,7 +50,6 @@
             copy = pltpu.make_async_copy(source.at[slot], target.at[slot], sems.at[field * slots + slot])
             copy.start()
             copies.append(copy)
-    me = lax.axis_index("tile")
     copies[0].wait()
     for field, (_, ref) in enumerate(fields):
         for slot in range(slots):
@@ -66,24 +61,41 @@
                 rows = slice(2 * pair, 2 * pair + 2)
                 strip_ref[0, rows, :] = top[0:2, lanes]
                 strip_ref[1, rows, :] = bottom[14:16, lanes]
-            for direction in range(8):
+            for direction in (0, 1, 4, 5, 6, 7):
                 link = links_ref[slot, direction]
 
                 @pl.when(link >= 0)
-                def _(slot=slot, direction=direction, link=link, field=field, ref=ref):
-                    device = link // slots
-                    if direction in (2, 3):
-                        first = jnp.where(device == me, strip_row(field, slot), column_row(field))
-                        lanes = slice(0, LANES) if direction == 2 else slice(width - LANES, width)
-                        out_ref[device, pl.ds(pl.multiple_of(first, 32), 32), :] = ref[slot, :, lanes]
-                    else:
-                        which = 0 if direction in (0, 4, 5) else 1
-                        first = strip_row(field, slot)
-                        out_ref[device, first : first + 32, :] = strip_ref[which].astype(BF16)
+                def _(slot=slot, direction=direction, link=link, field=field):
+                    which = 0 if direction in (0, 4, 5) else 1
+                    first = strip_row(field, slot)
+                    out_ref[link // slots, first : first + 32, :] = strip_ref[which].astype(BF16)
+
+
+def columns_kernel(tissue_hbm, image_hbm, cotangent_hbm, east_ref, west_ref, tissue_ref, edge_ref, sems):
+    slots, side, _ = edge_ref.shape[2:]
+    width = image_hbm.shape[2]
+    copies = [pltpu.make_async_copy(tissue_hbm, tissue_ref, sems.at[4])]
+    for field, source in enumerate((image_hbm, cotangent_hbm)):
+        for end, first in enumerate((width - LANES, 0)):
+            copies.append(
+                pltpu.make_async_copy(
+                    source.at[:, :, first : first + LANES], edge_ref.at[field, end], sems.at[2 * field + end]
+                )
+            )
+    for copy in copies:
+        copy.start()
+    for copy in copies:
+        copy.wait()
+    for field in range(2):
+        last = edge_ref[field, 0, 0].astype(F32)
+        for slot in range(1, slots):
+            last = jnp.where(tissue_ref[0, slot] > 0, edge_ref[field, 0, slot].astype(F32), last)
+        east_ref[field] = last.astype(BF16)
+        west_ref[field] = edge_ref[field, 1, 0]
 
 
 def mix_kernel(
-    links_hbm, tissue_hbm, image_ref, cotangent_ref, halo_ref, one_ref, two_ref,
+    links_hbm, tissue_hbm, image_ref, cotangent_ref, halo_ref, from_west_ref, from_east_ref, one_ref, two_ref,
     output_hbm, grad_input_hbm, grads_ref,
     links_ref, tissue_ref, wide_in, wide_up, narrow_hidden, narrow_delta,
     taps_in, taps_up, taps_hidden, taps_delta, forward_ref, back_ref, acc_ref, output_ref, grad_input_ref, sems,
@@ -116,10 +128,13 @@
             for direction in range(8):
                 link = links_ref[slot, direction]
                 device, there = jnp.maximum(link, 0) // slots, jnp.maximum(link, 0) % slots
-                first = strip_row(field, 0) + there * 32
                 if direction in (2, 3):
-                    first = jnp.where(device == me, first, column_row(field))
-                got = halo_ref[device, pl.ds(pl.multiple_of(first, 32), 32), :].astype(F32)
+                    lanes = slice(width - LANES, width) if direction == 2 else slice(0, LANES)
+                    far = (from_west_ref if direction == 2 else from_east_ref)[field].astype(F32)
+                    got = jnp.where(device == me, ref[there, :, lanes].astype(F32), far)
+                else:
+                    first = pl.multiple_of(strip_row(field, 0) + there * 32, 32)
+                    got = halo_ref[device, pl.ds(first, 32), :].astype(F32)
                 got = jnp.where(link >= 0, got, 0.0)
                 row = 14 if direction in (0, 4, 5) else 16 + side
                 if direction in (2, 3):
@@ -258,7 +273,27 @@
         compiler_params=pltpu.CompilerParams(vmem_limit_bytes=PACK_LIMIT),
         name="pack",
     )(links, image, upstream)
+    packed, tissue_after = lax.optimization_barrier((packed, tissue))
     halo = lax.all_to_all(packed, "tile", 0, 0, tiled=True)
+
+    edge = jax.ShapeDtypeStruct((2, side, LANES), BF16)
+    east, west = pl.pallas_call(
+        columns_kernel,
+        out_shape=(edge, edge),
+        in_specs=[ANY] * 3,
+        out_specs=(VMEM, VMEM),
+        scratch_shapes=[
+            pltpu.SMEM(tissue.shape, jnp.int32),
+            pltpu.VMEM((2, 2, slots, side, LANES), BF16),
+            pltpu.SemaphoreType.DMA((5,)),
+        ],
+        compiler_params=pltpu.CompilerParams(vmem_limit_bytes=PACK_LIMIT),
+        cost_estimate=pl.CostEstimate(flops=4 * 10**9, bytes_accessed=10**7, transcendentals=0),
+        name="columns",
+    )(tissue_after, image, upstream)
+    onward = [(k, k + 1) for k in range(devices_tile - 1)]
+    from_west = lax.ppermute(east, "tile", onward)
+    from_east = lax.ppermute(west, "tile", [(k + 1, k) for k, _ in onward])
 
     chunk = -(-576 // (2 * devices))
     total = 2 * chunk * devices
@@ -269,7 +304,7 @@
             jax.ShapeDtypeStruct((slots, side, width), BF16),
             jax.ShapeDtypeStruct((total, LANES), BF16),
         ),
-        in_specs=[ANY, ANY] + [VMEM] * 5,
+        in_specs=[ANY, ANY] + [VMEM] * 7,
         out_specs=(ANY, ANY, VMEM),
         scratch_shapes=[
             pltpu.SMEM(links.shape, jnp.int32),
@@ -291,7 +326,7 @@
         ],
         compiler_params=pltpu.CompilerParams(vmem_limit_bytes=48 * 2**20),
         name="mix",
-    )(links, tissue, image, upstream, halo, weight_one, weight_two)
+    )(links, tissue, image, upstream, halo, from_west, from_east, weight_one, weight_two)
 
     parts = lax.all_to_all(grads.reshape(devices, chunk, 2, LANES), ("slide", "tile"), 0, 0, tiled=True)
     mine = jnp.sum(lax.optimization_barrier(parts.astype(F32)), axis=0).astype(BF16)

time: 48.8 us -> 50 us (1.025)
  blocking collectives: 40.7 us -> 23.5 us
  starting transfers between devices: 0 us -> 12.5 us
  waiting for transfers between devices: 0 us -> 4.54 us
  Pallas kernels: 5.84 us -> 7.2 us
    all_to_all x1 -> x0, blocking collectives: 19.5 us -> none  [local(): halo = lax.all_to_all(packed, 'tile', 0, 0, tiled=True)]
    all_to_all x0 -> x1, starting transfers between devices: none -> 7.26 us  [local(): halo = lax.all_to_all(packed, 'tile', 0, 0, tiled=True)]
    ppermute x0 -> x2, starting transfers between devices: none -> 5.2 us  [the longest x1 3.91 us: local(): from_west = lax.ppermute(east, 'tile', onward)]
    ppermute x0 -> x2, waiting for transfers between devices: none -> 4.54 us  [the longest x1 4.21 us: local(): from_east = lax.ppermute(west, 'tile', [(k + 1, k) for k, _ in onward])]
    all_to_all x1, blocking collectives: 10.9 us -> 13.1 us  [local(): lax.all_to_all(grads.reshape(devices, chunk, 2, LANES), ('slide', 'tile')...]
    pallas_call x0 -> x1, Pallas kernels: none -> 1.49 us  [local(): pl.pallas_call(columns_kernel, out_shape=(edge, edge), in_specs=[ANY] * 3...]
  transfers between devices with their start and end apart: 0 -> 3, of which waited for: 0 -> 2; matrix products, arithmetic and copies ran while one was open for 0% -> 0% of each run, Pallas kernels for 0% -> 3%
where the time goes in v11:
time: 50 us; the launch traced here: 49.7 us
  blocking collectives  23.5 us (47%)
  starting transfers between devices  12.5 us (25%)
  Pallas kernels  7.2 us (14%)
  waiting for transfers between devices  4.54 us (9%)
  local copies, waits for them, and re-layouts  1.01 us (2%)
  between operations  0.76 us (2%)
    all_to_all x1, blocking collectives, local(): lax.all_to_all(grads.reshape(devices, chunk, 2, LANES), ('slide', 'tile')...  13.1 us
    all_to_all x1, blocking collectives, local(): whole = lax.all_to_all(sums, ('slide', 'tile'), 0, 0, tiled=True)  10.4 us
    all_to_all x1, starting transfers between devices, local(): halo = lax.all_to_all(packed, 'tile', 0, 0, tiled=True)  7.26 us
    ppermute x1, waiting for transfers between devices, local(): from_east = lax.ppermute(west, 'tile', [(k + 1, k) for k, _ in onward])  4.21 us
    ppermute x1, starting transfers between devices, local(): from_west = lax.ppermute(east, 'tile', onward)  3.91 us
    pallas_call x1, Pallas kernels, local(): pl.pallas_call(mix_kernel, out_shape=(jax.ShapeDtypeStruct((slots, side,...  3.81 us
    pallas_call x1, Pallas kernels, local(): pl.pallas_call(pack_kernel, out_shape=jax.ShapeDtypeStruct((devices_tile,...  1.89 us
    pallas_call x1, Pallas kernels, local(): pl.pallas_call(columns_kernel, out_shape=(edge, edge), in_specs=[ANY] * 3...  1.49 us
  transfers between devices with their start and end apart: 3, of which 2 were waited for; matrix products, arithmetic and copies ran while one was open for 0% of the time, Pallas kernels for 3%

profile of v11, /device:TPU:0, one launch (start us, length us, event | category | flops | bytes accessed | tf_op | source)
XLA Modules:
  0.0 49.7 jit_solution(12496773990252363101)
XLA Ops:
  0.6 1.9 %pack.1 = bf16[8,128,128]{2,1,0:T(8,128)(2,1)} custom-call(s32[2,8]{1,0:T(2,128)} %bitcast.17, bf16[2,32,2048]{2,1,0:T(8,128)(2,1)} %bitcast.10, bf16[2,32,2048]{2,1,0:T(8,128)(2,1)} %bitcast.13), custom_call_target="tpu_custom_call" | custom-call | tf_op jit(solution)/shard_map/pack/pallas_call | solution.py:261
  2.5 7.3 %all-to-all-start = ((bf16[8,128,128]{2,1,0:T(8,128)(2,1)}), bf16[8,128,128]{2,1,0:T(8,128)(2,1)S(1)}, u32[]{:S(2)}, u32[]{:S(2)}) async-start(bf16[8,128,128]{2,1,0:T(8,128)(2,1)} %pack.1), calls=%async_computation | async-start | bytes 524288 | tf_op jit(solution)/shard_map/all_to_all | solution.py:277
  9.8 0.0 copy-start
  9.8 0.0 copy-start.1
  9.8 0.0 copy-start.2
  9.8 0.0 copy-start.3
  9.8 1.5 %columns.1 = (bf16[2,32,128]{2,1,0:T(8,128)(2,1)}, bf16[2,32,128]{2,1,0:T(8,128)(2,1)}) custom-call(s32[1,2]{1,0:T(1,128)} %tissue_hbm.2, bf16[2,32,2048]{2,1,0:T(8,128)(2,1)} %bitcast.11, bf16[2,32,2048]{2,1,0:T(8,128)(2,1)} %bitcast.14), custom_call_target="tpu_custom_call" | custom-call | flops 4000000000 | bytes 10000000 | tf_op jit(solution)/shard_map/columns/pallas_call | solution.py:280
  11.3 0.0 copy-start.4
  11.3 0.0 copy-start.5
  11.4 3.9 %collective-permute-start = (bf16[2,32,128]{2,1,0:T(8,128)(2,1)}, bf16[2,32,128]{2,1,0:T(8,128)(2,1)S(1)}, u32[]{:S(2)}, u32[]{:S(2)}) collective-permute-start(bf16[2,32,128]{2,1,0:T(8,128)(2,1)} %get-tuple-element.13), channel_id=1, source_target_pairs={{0,1},{1,2},{2,3},{3,4},{4,5},{5,6},{6,7},{8,9},{9,10},{10,11},{11... | collective-permute-start | bytes 49160 | tf_op jit(solution)/shard_map/ppermute | solution.py:295
  15.3 1.3 %collective-permute-start.1 = (bf16[2,32,128]{2,1,0:T(8,128)(2,1)}, bf16[2,32,128]{2,1,0:T(8,128)(2,1)S(1)}, u32[]{:S(2)}, u32[]{:S(2)}) collective-permute-start(bf16[2,32,128]{2,1,0:T(8,128)(2,1)} %get-tuple-element.14), channel_id=1, source_target_pairs={{1,0},{2,1},{3,2},{4,3},{5,4},{6,5},{7,6},{9,8},{10,9},{11,10},{12... | collective-permute-start | bytes 49160 | tf_op jit(solution)/shard_map/ppermute | solution.py:296
  16.6 0.3 collective-permute-done.from_west_ref
  16.9 4.2 %collective-permute-done.1.from_east_ref = bf16[2,32,128]{2,1,0:T(8,128)(2,1)S(1)} collective-permute-done((bf16[2,32,128]{2,1,0:T(8,128)(2,1)}, bf16[2,32,128]{2,1,0:T(8,128)(2,1)S(1)}, u32[]{:S(2)}, u32[]{:S(2)}) %collective-permute-start.1) | collective-permute-done | bytes 16416 | tf_op jit(solution)/shard_map/ppermute | solution.py:296
  21.1 0.0 all-to-all-done.halo_ref
  21.1 0.0 copy-done
  21.1 0.0 copy-done.1
  21.1 0.0 copy-done.2
  21.1 0.0 copy-done.3
  21.2 0.0 copy-done.4
  21.2 0.0 copy-done.5
  21.2 3.8 %mix.1 = (bf16[2,32,2048]{2,1,0:T(8,128)(2,1)}, bf16[2,32,2048]{2,1,0:T(8,128)(2,1)}, bf16[576,128]{1,0:T(8,128)(2,1)S(1)}) custom-call(s32[2,8]{1,0:T(2,128)S(1)} %bitcast.18, s32[1,2]{1,0:T(1,128)S(1)} %copy-done.5, bf16[2,32,2048]{2,1,0:T(8,128)(2,1)S(1)} %bitcast.12, bf16[2,32,2048]{2,1,0:T(8,128)(2,1)S(1)} %bitcast.15, ...), custom_call_target="tpu_custom_call" | custom-call | tf_op jit(solution)/shard_map/mix/pallas_call | solution.py:300
  25.0 13.1 %all_to_all.15 = bf16[32,9,2,128]{3,2,1,0:T(2,128)(2,1)S(1)} all-to-all(bf16[32,9,2,128]{3,2,1,0:T(2,128)(2,1)S(1)} %bitcast.16), channel_id=1, replica_groups=mesh['slide'=4,'tile'=8] {'slide','tile'}, dimensions={0} | all-to-all | bytes 294912 | tf_op jit(solution)/shard_map/all_to_all | solution.py:331
  38.1 0.1 convert_element_type.16
  38.2 0.1 reduce_sum.9
  38.3 0.1 broadcast_in_dim.14
  38.4 10.4 %all_to_all.16 = bf16[32,9,2,128]{3,2,1,0:T(2,128)(2,1)S(1)} all-to-all(bf16[32,9,2,128]{3,2,1,0:T(2,128)(2,1)S(1)} %broadcast_in_dim.14), channel_id=1, replica_groups=mesh['slide'=4,'tile'=8] {'slide','tile'}, dimensions={0} | all-to-all | bytes 294912 | tf_op jit(solution)/shard_map/all_to_all | solution.py:334
  48.8 0.9 %fusion = (f32[576,64]{1,0:T(8,128)}, f32[576,64]{1,0:T(8,128)}) fusion(f32[576,128]{1,0:T(8,128)S(1)} %convert.1), kind=kLoop, calls=%fused_computation | loop fusion | bytes 589824 | tf_op jit(solution)/shard_map/slice | solution.py:337
  (1 shorter events, 0.0 us)
Async XLA Ops:
  2.5 18.6 %all-to-all-start = ((bf16[8,128,128]{2,1,0:T(8,128)(2,1)}), bf16[8,128,128]{2,1,0:T(8,128)(2,1)S(1)}, u32[]{:S(2)}, u32[]{:S(2)}) async-start(bf16[8,128,128]{2,1,0:T(8,128)(2,1)} %pack.1), calls=%async_computation | async-start | bytes 524288 | tf_op jit(solution)/shard_map/all_to_all | solution.py:277
  9.8 11.3 %copy-start = (bf16[1,2,32,2048]{3,2,1,0:T(8,128)(2,1)S(1)}, bf16[1,2,32,2048]{3,2,1,0:T(8,128)(2,1)}, u32[]{:S(2)}) copy-start(bf16[1,2,32,2048]{3,2,1,0:T(8,128)(2,1)} %param.6) | copy-start | bytes 786436
  9.8 11.3 %copy-start.1 = (bf16[1,2,32,2048]{3,2,1,0:T(8,128)(2,1)S(1)}, bf16[1,2,32,2048]{3,2,1,0:T(8,128)(2,1)}, u32[]{:S(2)}) copy-start(bf16[1,2,32,2048]{3,2,1,0:T(8,128)(2,1)} %param.7) | copy-start | bytes 786436
  9.8 11.3 %copy-start.2 = (bf16[3,3,64,64]{3,2,1,0:T(8,128)(2,1)S(1)}, bf16[3,3,64,64]{3,2,1,0:T(8,128)(2,1)}, u32[]{:S(2)}) copy-start(bf16[3,3,64,64]{3,2,1,0:T(8,128)(2,1)} %one_ref.1) | copy-start | bytes 221188
  9.8 11.3 %copy-start.3 = (bf16[3,3,64,64]{3,2,1,0:T(8,128)(2,1)S(1)}, bf16[3,3,64,64]{3,2,1,0:T(8,128)(2,1)}, u32[]{:S(2)}) copy-start(bf16[3,3,64,64]{3,2,1,0:T(8,128)(2,1)} %two_ref.1) | copy-start | bytes 221188
  11.3 9.8 %copy-start.4 = (s32[1,2,8]{2,1,0:T(2,128)S(1)}, s32[1,2,8]{2,1,0:T(2,128)}, u32[]{:S(2)}) copy-start(s32[1,2,8]{2,1,0:T(2,128)} %param.11) | copy-start | bytes 196
  11.3 9.8 %copy-start.5 = (s32[1,2]{1,0:T(1,128)S(1)}, s32[1,2]{1,0:T(1,128)}, u32[]{:S(2)}) copy-start(s32[1,2]{1,0:T(1,128)} %tissue_hbm.2) | copy-start | bytes 28
  11.4 5.6 %collective-permute-start = (bf16[2,32,128]{2,1,0:T(8,128)(2,1)}, bf16[2,32,128]{2,1,0:T(8,128)(2,1)S(1)}, u32[]{:S(2)}, u32[]{:S(2)}) collective-permute-start(bf16[2,32,128]{2,1,0:T(8,128)(2,1)} %get-tuple-element.13), channel_id=1, source_target_pairs={{0,1},{1,2},{2,3},{3,4},{4,5},{5,6},{6,7},{8,9},{9,10},{10,11},{11... | collective-permute-start | bytes 49160 | tf_op jit(solution)/shard_map/ppermute | solution.py:295
  15.3 5.8 %collective-permute-start.1 = (bf16[2,32,128]{2,1,0:T(8,128)(2,1)}, bf16[2,32,128]{2,1,0:T(8,128)(2,1)S(1)}, u32[]{:S(2)}, u32[]{:S(2)}) collective-permute-start(bf16[2,32,128]{2,1,0:T(8,128)(2,1)} %get-tuple-element.14), channel_id=1, source_target_pairs={{1,0},{2,1},{3,2},{4,3},{5,4},{6,5},{7,6},{9,8},{10,9},{11,10},{12... | collective-permute-start | bytes 49160 | tf_op jit(solution)/shard_map/ppermute | solution.py:296

commit v12 on v9

--- a/solution.py
+++ b/solution.py
@@ -15,7 +15,7 @@
 PACK_LIMIT = 60 * 2**20
 
 
-BLOCK = 2 * 48
+RING = 2 * 48
 
 
 def strip_row(field, slot):
@@ -59,7 +59,7 @@
 
 
 def pack_kernel(
-    links_hbm, image_hbm, cotangent_hbm, inner_ref, outer_ref,
+    links_hbm, image_hbm, cotangent_hbm, out_ref,
     links_ref, image_ref, cotangent_ref, strip_ref, sems,
 ):
     slots, side, width = image_ref.shape
@@ -95,22 +95,24 @@
                     device = link // slots
                     if direction in (2, 3):
                         first = jnp.where(device == me, strip_row(field, slot), column_row(field))
-                        at = pl.ds(pl.multiple_of(first, 16), 16)
+                        inner = pl.ds(pl.multiple_of(first, 16), 16)
+                        outer = pl.ds(pl.multiple_of(first + RING, 16), 16)
                         lanes = slice(0, LANES) if direction == 2 else slice(width - LANES, width)
                         block = ref[slot, :, lanes].astype(F32)
                         other = pltpu.roll(block, half, 1)
                         low = jnp.where(left, block[0:16], other[16:32]).astype(BF16)
                         high = jnp.where(left, other[0:16], block[16:32]).astype(BF16)
-                        inner_ref[device, at, :] = low if direction == 2 else high
-                        outer_ref[device, at, :] = high if direction == 2 else low
+                        out_ref[device, inner, :] = low if direction == 2 else high
+                        out_ref[device, outer, :] = high if direction == 2 else low
                     else:
                         which = 0 if direction in (0, 4, 5) else 2
                         first = strip_row(field, slot)
-                        inner_ref[device, first : first + 16, :] = strip_ref[which].astype(BF16)
-                        outer_ref[device, first : first + 16, :] = strip_ref[which + 1].astype(BF16)
-
-
-def place_halo(links_ref, halos, wide, slot, field, slots, side, pairs, me):
+                        out_ref[device, first : first + 16, :] = strip_ref[which].astype(BF16)
+                        first += RING
+                        out_ref[device, first : first + 16, :] = strip_ref[which + 1].astype(BF16)
+
+
+def place_halo(links_ref, halo_ref, rings, wide, slot, field, slots, side, pairs, me):
     half = LANES // 2
     left = lax.broadcasted_iota(jnp.int32, (16, LANES), 1) < half
     none = jnp.zeros((16, LANES), F32)
@@ -120,8 +122,10 @@
         first = strip_row(field, 0) + there * 16
         if direction in (2, 3):
             first = jnp.where(device == me, first, column_row(field))
-        at = pl.ds(pl.multiple_of(first, 16), 16)
-        got = [jnp.where(link >= 0, halo[device, at, :].astype(F32), 0.0) for halo in halos]
+        got = []
+        for ring in range(rings):
+            at = pl.ds(pl.multiple_of(first + ring * RING, 16), 16)
+            got.append(jnp.where(link >= 0, halo_ref[device, at, :].astype(F32), 0.0))
         if direction in (2, 3):
             inner, outer = got[0], got[1] if len(got) > 1 else none
             low, high = (outer, inner) if direction == 2 else (inner, outer)
@@ -156,7 +160,7 @@
 
 
 def grads_kernel(
-    links_hbm, tissue_hbm, image_ref, cotangent_ref, inner_ref, one_ref, two_ref,
+    links_hbm, tissue_hbm, image_ref, cotangent_ref, halo_ref, one_ref, two_ref,
     grads_ref,
     links_ref, tissue_ref, wide_in, wide_up, own_hidden, own_delta,
     taps_in, taps_up, forward_ref, back_ref, acc_ref, sems,
@@ -179,7 +183,7 @@
     for field, (ref, wide) in enumerate(((image_ref, wide_in), (cotangent_ref, wide_up))):
         for slot in range(slots):
             place_own(tissue_ref, ref, wide, slot, side, pairs)
-            place_halo(links_ref, (inner_ref,), wide, slot, field, slots, side, pairs, me)
+            place_halo(links_ref, halo_ref, 1, wide, slot, field, slots, side, pairs, me)
     shift_rows(wide_in, taps_in, pairs + 2, 16, side)
     shift_rows(wide_up, taps_up, pairs + 2, 16, side)
 
@@ -233,7 +237,7 @@
 
 
 def fields_kernel(
-    links_hbm, tissue_hbm, image_ref, cotangent_ref, inner_ref, outer_ref, one_ref, two_ref,
+    links_hbm, tissue_hbm, image_ref, cotangent_ref, halo_ref, one_ref, two_ref,
     output_hbm, grad_input_hbm,
     links_ref, tissue_ref, wide_in, wide_up, narrow_hidden, narrow_delta,
     taps_in, taps_up, taps_hidden, taps_delta, forward_one, forward_two, back_one, back_two,
@@ -262,7 +266,7 @@
         wide[:, :, 16 + side : 32 + side, :] = jnp.zeros((slots, pairs + 2, 16, LANES), F32)
         for slot in range(slots):
             place_own(tissue_ref, ref, wide, slot, side, pairs)
-            place_halo(links_ref, (inner_ref, outer_ref), wide, slot, field, slots, side, pairs, me)
+            place_halo(links_ref, halo_ref, 2, wide, slot, field, slots, side, pairs, me)
     shift_rows(wide_in, taps_in, pairs + 2, 8, tall)
     shift_rows(wide_up, taps_up, pairs + 2, 8, tall)
 
@@ -320,12 +324,11 @@
     tall = side + 16
     image, upstream = slide_image[0], cotangent[0]
     links = neighbours[0]
-    block = jax.ShapeDtypeStruct((devices_tile, BLOCK, LANES), BF16)
-    packed_inner, packed_outer = pl.pallas_call(
+    packed = pl.pallas_call(
         pack_kernel,
-        out_shape=(block, block),
+        out_shape=jax.ShapeDtypeStruct((devices_tile, 2 * RING, LANES), BF16),
         in_specs=[ANY] * 3,
-        out_specs=(VMEM, VMEM),
+        out_specs=VMEM,
         scratch_shapes=[
             pltpu.SMEM(links.shape, jnp.int32),
             pltpu.VMEM(image.shape, BF16),
@@ -336,8 +339,7 @@
         compiler_params=pltpu.CompilerParams(vmem_limit_bytes=PACK_LIMIT),
         name="pack",
     )(links, image, upstream)
-    inner = lax.all_to_all(packed_inner, "tile", 0, 0, tiled=True)
-    outer = lax.all_to_all(packed_outer, "tile", 0, 0, tiled=True)
+    halo = lax.all_to_all(packed, "tile", 0, 0, tiled=True)
 
     chunk = -(-576 // (2 * devices))
     total = 2 * chunk * devices
@@ -365,11 +367,11 @@
         compiler_params=pltpu.CompilerParams(vmem_limit_bytes=32 * 2**20),
         cost_estimate=cost,
         name="grads",
-    )(links, tissue, image, upstream, inner, weight_one, weight_two)
+    )(links, tissue, image, upstream, halo, weight_one, weight_two)
     output, grad_input = pl.pallas_call(
         fields_kernel,
         out_shape=(jax.ShapeDtypeStruct((slots, side, width), BF16),) * 2,
-        in_specs=[ANY, ANY] + [VMEM] * 6,
+        in_specs=[ANY, ANY] + [VMEM] * 5,
         out_specs=(ANY, ANY),
         scratch_shapes=[
             pltpu.SMEM(links.shape, jnp.int32),
@@ -394,10 +396,11 @@
         compiler_params=pltpu.CompilerParams(vmem_limit_bytes=40 * 2**20),
         cost_estimate=cost,
         name="fields",
-    )(links, tissue, image, upstream, inner, outer, weight_one, weight_two)
+    )(links, tissue, image, upstream, halo, weight_one, weight_two)
 
     parts = lax.all_to_all(grads.reshape(devices, chunk, 2, LANES), ("slide", "tile"), 0, 0, tiled=True)
     mine = jnp.sum(lax.optimization_barrier(parts.astype(F32)), axis=0).astype(BF16)
+    mine, output, grad_input = lax.optimization_barrier((mine, output, grad_input))
     sums = jnp.broadcast_to(mine[None], parts.shape)
     whole = lax.all_to_all(sums, ("slide", "tile"), 0, 0, tiled=True)
     whole = lax.optimization_barrier(whole.reshape(total, LANES).astype(F32))

time: 56.2 us -> 48.8 us (0.87)
  waiting for transfers between devices: 11.9 us -> 3.79 us
  blocking collectives: 26.1 us -> 29.9 us
  starting transfers between devices: 6.25 us -> 3.22 us
  Pallas kernels: 8.96 us -> 9.67 us
  local copies, waits for them, and re-layouts: 1.66 us -> 1.01 us
    all_to_all x2 -> x1, waiting for transfers between devices: 11.9 us -> 3.79 us  [local(): lax.all_to_all(grads.reshape(devices, chunk, 2, LANES), ('slide', 'tile')...]
    all_to_all x2, blocking collectives: 26.1 us -> 29.9 us  [the longest x1 19.5 us: local(): halo = lax.all_to_all(packed, 'tile', 0, 0, tiled=True)]
    all_to_all x2 -> x1, starting transfers between devices: 6.25 us -> 3.22 us  [local(): lax.all_to_all(grads.reshape(devices, chunk, 2, LANES), ('slide', 'tile')...]
    pallas_call x1, Pallas kernels: 2.82 us -> 3.52 us  [local(): pl.pallas_call(grads_kernel, out_shape=jax.ShapeDtypeStruct((total, LANES...]
    broadcast_in_dim x1, local copies, waits for them, and re-layouts: 0.74 us -> 0.08 us  [local(): sums = jnp.broadcast_to(mine[None], parts.shape)]
  transfers between devices with their start and end apart: 2 -> 1, of which waited for: 2 -> 1; matrix products, arithmetic and copies ran while one was open for 0% -> 0% of each run, Pallas kernels for 7% -> 8%
where the time goes in v12:
time: 48.8 us; the launch traced here: 48.6 us
  blocking collectives  29.9 us (61%)
  Pallas kernels  9.67 us (20%)
  waiting for transfers between devices  3.79 us (8%)
  starting transfers between devices  3.22 us (7%)
  local copies, waits for them, and re-layouts  1.01 us (2%)
  between operations  0.75 us (2%)
    all_to_all x1, blocking collectives, local(): halo = lax.all_to_all(packed, 'tile', 0, 0, tiled=True)  19.5 us
    all_to_all x1, blocking collectives, local(): whole = lax.all_to_all(sums, ('slide', 'tile'), 0, 0, tiled=True)  10.4 us
    pallas_call x1, Pallas kernels, local(): pl.pallas_call(fields_kernel, out_shape=(jax.ShapeDtypeStruct((slots, sid...  4.03 us
    all_to_all x1, waiting for transfers between devices, local(): lax.all_to_all(grads.reshape(devices, chunk, 2, LANES), ('slide', 'tile')...  3.79 us
    pallas_call x1, Pallas kernels, local(): pl.pallas_call(grads_kernel, out_shape=jax.ShapeDtypeStruct((total, LANES...  3.52 us
    all_to_all x1, starting transfers between devices, local(): lax.all_to_all(grads.reshape(devices, chunk, 2, LANES), ('slide', 'tile')...  3.22 us
    pallas_call x1, Pallas kernels, local(): pl.pallas_call(pack_kernel, out_shape=jax.ShapeDtypeStruct((devices_tile,...  2.12 us
  transfers between devices with their start and end apart: 1, of which 1 were waited for; matrix products, arithmetic and copies ran while one was open for 0% of the time, Pallas kernels for 8%

profile of v12, /device:TPU:0, one launch (start us, length us, event | category | flops | bytes accessed | tf_op | source)
XLA Modules:
  0.0 48.6 jit_solution(7679838170653830863)
XLA Ops:
  0.6 0.0 copy-start.4
  0.6 2.1 %pack.1 = bf16[8,192,128]{2,1,0:T(8,128)(2,1)} custom-call(s32[2,8]{1,0:T(2,128)} %bitcast.16, bf16[2,32,2048]{2,1,0:T(8,128)(2,1)} %bitcast.10, bf16[2,32,2048]{2,1,0:T(8,128)(2,1)} %bitcast.13), custom_call_target="tpu_custom_call" | custom-call | tf_op jit(solution)/shard_map/pack/pallas_call | solution.py:327
  2.8 0.0 copy-start
  2.8 0.0 copy-start.1
  2.8 0.0 copy-start.2
  2.8 0.0 copy-start.3
  2.8 0.0 copy-start.5
  2.8 19.5 %all_to_all.15.halo_ref = bf16[8,192,128]{2,1,0:T(8,128)(2,1)S(1)} all-to-all(bf16[8,192,128]{2,1,0:T(8,128)(2,1)} %pack.1), channel_id=1, replica_groups=mesh['slide'=4,'tile'=8] {'tile'}, dimensions={0} | all-to-all | bytes 786432 | tf_op jit(solution)/shard_map/all_to_all | solution.py:342
  22.4 0.0 copy-done.4
  22.4 0.0 copy-done
  22.4 0.0 copy-done.1
  22.4 0.0 copy-done.2
  22.4 0.0 copy-done.3
  22.4 0.0 copy-done.5
  22.4 3.5 %grads.1 = bf16[576,128]{1,0:T(8,128)(2,1)} custom-call(s32[2,8]{1,0:T(2,128)S(1)} %bitcast.17, s32[1,2]{1,0:T(1,128)S(1)} %copy-done.5, bf16[2,32,2048]{2,1,0:T(8,128)(2,1)S(1)} %bitcast.11, bf16[2,32,2048]{2,1,0:T(8,128)(2,1)S(1)} %bitcast.14, bf16[8,192,128]{2,1,0:T(8,128)(2,1)S(1)} %all_to_all.15.halo_ref, bf16[3,3,64,64]{3,2,1,0:T(8,128)(2,1)S(1)} %copy-done.3, ...), custom_call_target="tpu_custom_call" | custom-call | flops 4000000000 | bytes 10000000 | tf_op jit(solution)/shard_map/grads/pallas_call | solution.py:349
  25.9 3.2 %all-to-all-start.1 = ((bf16[32,9,2,128]{3,2,1,0:T(2,128)(2,1)}), bf16[32,9,2,128]{3,2,1,0:T(2,128)(2,1)S(1)}, u32[]{:S(2)}, u32[]{:S(2)}) async-start(bf16[32,9,2,128]{3,2,1,0:T(2,128)(2,1)} %bitcast.3), calls=%async_computation.1 | async-start | bytes 294912 | tf_op jit(solution)/shard_map/all_to_all | solution.py:401
  29.2 4.0 %fields.1 = (bf16[2,32,2048]{2,1,0:T(8,128)(2,1)}, bf16[2,32,2048]{2,1,0:T(8,128)(2,1)}) custom-call(s32[2,8]{1,0:T(2,128)S(1)} %bitcast.18, s32[1,2]{1,0:T(1,128)S(1)} %copy-done.5, bf16[2,32,2048]{2,1,0:T(8,128)(2,1)S(1)} %bitcast.12, bf16[2,32,2048]{2,1,0:T(8,128)(2,1)S(1)} %bitcast.15, bf16[8,192,128]{2,1,0:T(8,128)(2,1)S(1)} %all_to_all.15.halo_ref, ...), custom_call_target="tpu_custom_call" | custom-call | flops 4000000000 | bytes 10000000 | tf_op jit(solution)/shard_map/fields/pallas_call | solution.py:371
  33.2 3.8 %all-to-all-done.1 = bf16[32,9,2,128]{3,2,1,0:T(2,128)(2,1)S(1)} async-done(((bf16[32,9,2,128]{3,2,1,0:T(2,128)(2,1)}), bf16[32,9,2,128]{3,2,1,0:T(2,128)(2,1)S(1)}, u32[]{:S(2)}, u32[]{:S(2)}) %all-to-all-start.1) | async-done | bytes 147488 | tf_op jit(solution)/shard_map/all_to_all | solution.py:401
  37.0 0.1 convert_element_type.12
  37.1 0.1 reduce_sum.9
  37.2 0.1 broadcast_in_dim.14
  37.3 10.4 %all_to_all.16 = bf16[32,9,2,128]{3,2,1,0:T(2,128)(2,1)S(1)} all-to-all(bf16[32,9,2,128]{3,2,1,0:T(2,128)(2,1)S(1)} %broadcast_in_dim.14), channel_id=1, replica_groups=mesh['slide'=4,'tile'=8] {'slide','tile'}, dimensions={0} | all-to-all | bytes 294912 | tf_op jit(solution)/shard_map/all_to_all | solution.py:405
  47.7 0.9 %fusion = (f32[576,64]{1,0:T(8,128)}, f32[576,64]{1,0:T(8,128)}) fusion(f32[576,128]{1,0:T(8,128)S(1)} %convert.1), kind=kLoop, calls=%fused_computation | loop fusion | bytes 589824 | tf_op jit(solution)/shard_map/slice | solution.py:408
  (1 shorter events, 0.0 us)
Async XLA Ops:
  0.6 21.7 %copy-start.4 = (bf16[3,3,64,64]{3,2,1,0:T(8,128)(2,1)S(1)}, bf16[3,3,64,64]{3,2,1,0:T(8,128)(2,1)}, u32[]{:S(2)}) copy-start(bf16[3,3,64,64]{3,2,1,0:T(8,128)(2,1)} %two_ref.3) | copy-start | bytes 221188
  2.8 19.6 %copy-start = (bf16[1,2,32,2048]{3,2,1,0:T(8,128)(2,1)S(1)}, bf16[1,2,32,2048]{3,2,1,0:T(8,128)(2,1)}, u32[]{:S(2)}) copy-start(bf16[1,2,32,2048]{3,2,1,0:T(8,128)(2,1)} %param.6) | copy-start | bytes 786436
  2.8 19.6 %copy-start.1 = (bf16[1,2,32,2048]{3,2,1,0:T(8,128)(2,1)S(1)}, bf16[1,2,32,2048]{3,2,1,0:T(8,128)(2,1)}, u32[]{:S(2)}) copy-start(bf16[1,2,32,2048]{3,2,1,0:T(8,128)(2,1)} %param.7) | copy-start | bytes 786436
  2.8 19.6 %copy-start.2 = (s32[1,2,8]{2,1,0:T(2,128)S(1)}, s32[1,2,8]{2,1,0:T(2,128)}, u32[]{:S(2)}) copy-start(s32[1,2,8]{2,1,0:T(2,128)} %param.11) | copy-start | bytes 196
  2.8 19.6 %copy-start.3 = (bf16[3,3,64,64]{3,2,1,0:T(8,128)(2,1)S(1)}, bf16[3,3,64,64]{3,2,1,0:T(8,128)(2,1)}, u32[]{:S(2)}) copy-start(bf16[3,3,64,64]{3,2,1,0:T(8,128)(2,1)} %one_ref.3) | copy-start | bytes 221188
  2.8 19.6 %copy-start.5 = (s32[1,2]{1,0:T(1,128)S(1)}, s32[1,2]{1,0:T(1,128)}, u32[]{:S(2)}) copy-start(s32[1,2]{1,0:T(1,128)} %tissue_hbm.3) | copy-start | bytes 28
  25.9 11.1 %all-to-all-start.1 = ((bf16[32,9,2,128]{3,2,1,0:T(2,128)(2,1)}), bf16[32,9,2,128]{3,2,1,0:T(2,128)(2,1)S(1)}, u32[]{:S(2)}, u32[]{:S(2)}) async-start(bf16[32,9,2,128]{3,2,1,0:T(2,128)(2,1)} %bitcast.3), calls=%async_computation.1 | async-start | bytes 294912 | tf_op jit(solution)/shard_map/all_to_all | solution.py:401

commit v13 on v12

--- a/solution.py
+++ b/solution.py
@@ -16,10 +16,15 @@
 
 
 RING = 2 * 48
+BLOCK = RING + 2 * 32
 
 
 def strip_row(field, slot):
     return field * 48 + slot * 16
+
+
+def outer_row(field, slot):
+    return RING + field * 32 + slot * 16
 
 
 def column_row(field):
@@ -73,7 +78,6 @@
             copy = pltpu.make_async_copy(source.at[slot], target.at[slot], sems.at[field * slots + slot])
             copy.start()
             copies.append(copy)
-    me = lax.axis_index("tile")
     left = lax.broadcasted_iota(jnp.int32, (16, LANES), 1) < half
     copies[0].wait()
     for field, (_, ref) in enumerate(fields):
@@ -94,47 +98,74 @@
                 def _(slot=slot, direction=direction, link=link, field=field, ref=ref):
                     device = link // slots
                     if direction in (2, 3):
-                        first = jnp.where(device == me, strip_row(field, slot), column_row(field))
-                        inner = pl.ds(pl.multiple_of(first, 16), 16)
-                        outer = pl.ds(pl.multiple_of(first + RING, 16), 16)
+                        first = column_row(field)
                         lanes = slice(0, LANES) if direction == 2 else slice(width - LANES, width)
                         block = ref[slot, :, lanes].astype(F32)
                         other = pltpu.roll(block, half, 1)
-                        low = jnp.where(left, block[0:16], other[16:32]).astype(BF16)
-                        high = jnp.where(left, other[0:16], block[16:32]).astype(BF16)
-                        out_ref[device, inner, :] = low if direction == 2 else high
-                        out_ref[device, outer, :] = high if direction == 2 else low
+                        if direction == 2:
+                            inner = jnp.where(left, block[0:16], other[16:32])
+                        else:
+                            inner = jnp.where(left, other[0:16], block[16:32])
+                        out_ref[device, first : first + 16, :] = inner.astype(BF16)
                     else:
                         which = 0 if direction in (0, 4, 5) else 2
                         first = strip_row(field, slot)
                         out_ref[device, first : first + 16, :] = strip_ref[which].astype(BF16)
-                        first += RING
+                        first = outer_row(field, slot)
                         out_ref[device, first : first + 16, :] = strip_ref[which + 1].astype(BF16)
 
 
-def place_halo(links_ref, halo_ref, rings, wide, slot, field, slots, side, pairs, me):
+def columns_kernel(tissue_hbm, image_hbm, cotangent_hbm, east_ref, west_ref, tissue_ref, edge_ref, sems):
+    slots, side, _ = edge_ref.shape[2:]
+    width = image_hbm.shape[2]
+    copies = [pltpu.make_async_copy(tissue_hbm, tissue_ref, sems.at[4])]
+    for field, source in enumerate((image_hbm, cotangent_hbm)):
+        for end, first in enumerate((width - LANES, 0)):
+            copies.append(
+                pltpu.make_async_copy(
+                    source.at[:, :, first : first + LANES], edge_ref.at[field, end], sems.at[2 * field + end]
+                )
+            )
+    for copy in copies:
+        copy.start()
+    for copy in copies:
+        copy.wait()
+    for field in range(2):
+        last = edge_ref[field, 0, 0].astype(F32)
+        for slot in range(1, slots):
+            last = jnp.where(tissue_ref[0, slot] > 0, edge_ref[field, 0, slot].astype(F32), last)
+        east_ref[field] = last.astype(BF16)
+        west_ref[field] = edge_ref[field, 1, 0]
+
+
+def place_halo(links_ref, halo_ref, far_refs, ref, wide, slot, field, slots, side, pairs, me):
     half = LANES // 2
+    width = pairs * LANES
     left = lax.broadcasted_iota(jnp.int32, (16, LANES), 1) < half
-    none = jnp.zeros((16, LANES), F32)
     for direction in range(8):
         link = links_ref[slot, direction]
         device, there = jnp.maximum(link, 0) // slots, jnp.maximum(link, 0) % slots
-        first = strip_row(field, 0) + there * 16
         if direction in (2, 3):
-            first = jnp.where(device == me, first, column_row(field))
-        got = []
-        for ring in range(rings):
-            at = pl.ds(pl.multiple_of(first + ring * RING, 16), 16)
-            got.append(jnp.where(link >= 0, halo_ref[device, at, :].astype(F32), 0.0))
-        if direction in (2, 3):
-            inner, outer = got[0], got[1] if len(got) > 1 else none
-            low, high = (outer, inner) if direction == 2 else (inner, outer)
+            if far_refs:
+                far = far_refs[direction - 2][field].astype(F32)
+            else:
+                first = column_row(field)
+                inner = halo_ref[device, first : first + 16, :].astype(F32)
+                other = pltpu.roll(inner, half, 1)
+                if direction == 2:
+                    parts = [jnp.where(left, 0.0, other), jnp.where(left, 0.0, inner)]
+                else:
+                    parts = [jnp.where(left, inner, 0.0), jnp.where(left, other, 0.0)]
+                far = jnp.concatenate(parts, axis=0)
+            lanes = slice(width - LANES, width) if direction == 2 else slice(0, LANES)
+            got = jnp.where(device == me, ref[there, :, lanes].astype(F32), far)
             column = 0 if direction == 2 else pairs + 1
-            wide[slot, column, 16:32, :] = jnp.where(left, low, pltpu.roll(high, half, 1))
-            wide[slot, column, 32:48, :] = jnp.where(left, pltpu.roll(low, half, 1), high)
+            wide[slot, column, 16 : 16 + side, :] = jnp.where(link >= 0, got, 0.0)
         else:
             north = direction in (0, 4, 5)
-            for ring, strip in enumerate(got):
+            for ring, first in enumerate((strip_row(field, 0), outer_row(field, 0))[: 2 if far_refs else 1]):
+                at = pl.ds(pl.multiple_of(first + there * 16, 16), 16)
+                strip = jnp.where(link >= 0, halo_ref[device, at, :].astype(F32), 0.0)
                 row = 15 - ring if north else 16 + side + ring
                 if direction < 2:
                     for pair in range(pairs):
@@ -183,7 +214,7 @@
     for field, (ref, wide) in enumerate(((image_ref, wide_in), (cotangent_ref, wide_up))):
         for slot in range(slots):
             place_own(tissue_ref, ref, wide, slot, side, pairs)
-            place_halo(links_ref, halo_ref, 1, wide, slot, field, slots, side, pairs, me)
+            place_halo(links_ref, halo_ref, (), ref, wide, slot, field, slots, side, pairs, me)
     shift_rows(wide_in, taps_in, pairs + 2, 16, side)
     shift_rows(wide_up, taps_up, pairs + 2, 16, side)
 
@@ -237,7 +268,7 @@
 
 
 def fields_kernel(
-    links_hbm, tissue_hbm, image_ref, cotangent_ref, halo_ref, one_ref, two_ref,
+    links_hbm, tissue_hbm, image_ref, cotangent_ref, halo_ref, from_west_ref, from_east_ref, one_ref, two_ref,
     output_hbm, grad_input_hbm,
     links_ref, tissue_ref, wide_in, wide_up, narrow_hidden, narrow_delta,
     taps_in, taps_up, taps_hidden, taps_delta, forward_one, forward_two, back_one, back_two,
@@ -266,7 +297,7 @@
         wide[:, :, 16 + side : 32 + side, :] = jnp.zeros((slots, pairs + 2, 16, LANES), F32)
         for slot in range(slots):
             place_own(tissue_ref, ref, wide, slot, side, pairs)
-            place_halo(links_ref, halo_ref, 2, wide, slot, field, slots, side, pairs, me)
+            place_halo(links_ref, halo_ref, (from_west_ref, from_east_ref), ref, wide, slot, field, slots, side, pairs, me)
     shift_rows(wide_in, taps_in, pairs + 2, 8, tall)
     shift_rows(wide_up, taps_up, pairs + 2, 8, tall)
 
@@ -326,7 +357,7 @@
     links = neighbours[0]
     packed = pl.pallas_call(
         pack_kernel,
-        out_shape=jax.ShapeDtypeStruct((devices_tile, 2 * RING, LANES), BF16),
+        out_shape=jax.ShapeDtypeStruct((devices_tile, BLOCK, LANES), BF16),
         in_specs=[ANY] * 3,
         out_specs=VMEM,
         scratch_shapes=[
@@ -339,7 +370,28 @@
         compiler_params=pltpu.CompilerParams(vmem_limit_bytes=PACK_LIMIT),
         name="pack",
     )(links, image, upstream)
+    packed, tissue_after = lax.optimization_barrier((packed, tissue))
     halo = lax.all_to_all(packed, "tile", 0, 0, tiled=True)
+
+    edge = jax.ShapeDtypeStruct((2, side, LANES), BF16)
+    east, west = pl.pallas_call(
+        columns_kernel,
+        out_shape=(edge, edge),
+        in_specs=[ANY] * 3,
+        out_specs=(VMEM, VMEM),
+        scratch_shapes=[
+            pltpu.SMEM(tissue.shape, jnp.int32),
+            pltpu.VMEM((2, 2, slots, side, LANES), BF16),
+            pltpu.SemaphoreType.DMA((5,)),
+        ],
+        compiler_params=pltpu.CompilerParams(vmem_limit_bytes=PACK_LIMIT),
+        cost_estimate=pl.CostEstimate(flops=4 * 10**9, bytes_accessed=10**7, transcendentals=0),
+        name="columns",
+    )(tissue_after, image, upstream)
+    onward = [(k, k + 1) for k in range(devices_tile - 1)]
+    from_west = lax.ppermute(east, "tile", onward)
+    from_east = lax.ppermute(west, "tile", [(k + 1, k) for k, _ in onward])
+
 
     chunk = -(-576 // (2 * devices))
     total = 2 * chunk * devices
@@ -371,7 +423,7 @@
     output, grad_input = pl.pallas_call(
         fields_kernel,
         out_shape=(jax.ShapeDtypeStruct((slots, side, width), BF16),) * 2,
-        in_specs=[ANY, ANY] + [VMEM] * 5,
+        in_specs=[ANY, ANY] + [VMEM] * 7,
         out_specs=(ANY, ANY),
         scratch_shapes=[
             pltpu.SMEM(links.shape, jnp.int32),
@@ -396,11 +448,10 @@
         compiler_params=pltpu.CompilerParams(vmem_limit_bytes=40 * 2**20),
         cost_estimate=cost,
         name="fields",
-    )(links, tissue, image, upstream, halo, weight_one, weight_two)
+    )(links, tissue, image, upstream, halo, from_west, from_east, weight_one, weight_two)
 
     parts = lax.all_to_all(grads.reshape(devices, chunk, 2, LANES), ("slide", "tile"), 0, 0, tiled=True)
     mine = jnp.sum(lax.optimization_barrier(parts.astype(F32)), axis=0).astype(BF16)
-    mine, output, grad_input = lax.optimization_barrier((mine, output, grad_input))
     sums = jnp.broadcast_to(mine[None], parts.shape)
     whole = lax.all_to_all(sums, ("slide", "tile"), 0, 0, tiled=True)
     whole = lax.optimization_barrier(whole.reshape(total, LANES).astype(F32))

time: 48.8 us -> 51.1 us (1.047)
  blocking collectives: 29.9 us -> 18.4 us
  starting transfers between devices: 3.22 us -> 13.2 us
  waiting for transfers between devices: 3.79 us -> 5.17 us
  Pallas kernels: 9.67 us -> 11 us
  local copies, waits for them, and re-layouts: 1.01 us -> 1.68 us
    all_to_all x1 -> x0, blocking collectives: 10.4 us -> none  [local(): whole = lax.all_to_all(sums, ('slide', 'tile'), 0, 0, tiled=True)]
    all_to_all x0 -> x1, starting transfers between devices: none -> 5.31 us  [local(): whole = lax.all_to_all(sums, ('slide', 'tile'), 0, 0, tiled=True)]
    ppermute x0 -> x2, starting transfers between devices: none -> 4.96 us  [the longest x1 3.67 us: local(): from_west = lax.ppermute(east, 'tile', onward)]
    all_to_all x0 -> x1, waiting for transfers between devices: none -> 3.75 us  [local(): whole = lax.all_to_all(sums, ('slide', 'tile'), 0, 0, tiled=True)]
    all_to_all x1, waiting for transfers between devices: 3.79 us -> 1.41 us  [local(): lax.all_to_all(grads.reshape(devices, chunk, 2, LANES), ('slide', 'tile')...]
    pallas_call x0 -> x1, Pallas kernels: none -> 1.43 us  [local(): pl.pallas_call(columns_kernel, out_shape=(edge, edge), in_specs=[ANY] * 3...]
    all_to_all x1, blocking collectives: 19.5 us -> 18.4 us  [local(): halo = lax.all_to_all(packed, 'tile', 0, 0, tiled=True)]
    broadcast_in_dim x1, local copies, waits for them, and re-layouts: 0.08 us -> 0.74 us  [local(): sums = jnp.broadcast_to(mine[None], parts.shape)]
  transfers between devices with their start and end apart: 1 -> 4, of which waited for: 1 -> 2; matrix products, arithmetic and copies ran while one was open for 0% -> 2% of each run, Pallas kernels for 8% -> 11%
where the time goes in v13:
time: 51.1 us; the launch traced here: 50.5 us
  blocking collectives  18.4 us (36%)
  starting transfers between devices  13.2 us (26%)
  Pallas kernels  11 us (22%)
  waiting for transfers between devices  5.17 us (10%)
  local copies, waits for them, and re-layouts  1.68 us (3%)
  between operations  0.83 us (2%)
    all_to_all x1, blocking collectives, local(): halo = lax.all_to_all(packed, 'tile', 0, 0, tiled=True)  18.4 us
    all_to_all x1, starting transfers between devices, local(): whole = lax.all_to_all(sums, ('slide', 'tile'), 0, 0, tiled=True)  5.31 us
    pallas_call x1, Pallas kernels, local(): pl.pallas_call(fields_kernel, out_shape=(jax.ShapeDtypeStruct((slots, sid...  4.01 us
    all_to_all x1, waiting for transfers between devices, local(): whole = lax.all_to_all(sums, ('slide', 'tile'), 0, 0, tiled=True)  3.75 us
    ppermute x1, starting transfers between devices, local(): from_west = lax.ppermute(east, 'tile', onward)  3.67 us
    pallas_call x1, Pallas kernels, local(): pl.pallas_call(grads_kernel, out_shape=jax.ShapeDtypeStruct((total, LANES...  3.49 us
    all_to_all x1, starting transfers between devices, local(): lax.all_to_all(grads.reshape(devices, chunk, 2, LANES), ('slide', 'tile')...  2.94 us
    pallas_call x1, Pallas kernels, local(): pl.pallas_call(pack_kernel, out_shape=jax.ShapeDtypeStruct((devices_tile,...  2.1 us
  transfers between devices with their start and end apart: 4, of which 2 were waited for; matrix products, arithmetic and copies ran while one was open for 2% of the time, Pallas kernels for 11%

profile of v13, /device:TPU:0, one launch (start us, length us, event | category | flops | bytes accessed | tf_op | source)
XLA Modules:
  0.0 50.5 jit_solution(15565792733635211977)
XLA Ops:
  0.6 0.0 copy-start.5
  0.6 0.0 copy-start.6
  0.7 2.1 %pack.1 = bf16[8,160,128]{2,1,0:T(8,128)(2,1)} custom-call(s32[2,8]{1,0:T(2,128)} %bitcast.18, bf16[2,32,2048]{2,1,0:T(8,128)(2,1)} %bitcast.10, bf16[2,32,2048]{2,1,0:T(8,128)(2,1)} %bitcast.14), custom_call_target="tpu_custom_call" | custom-call | tf_op jit(solution)/shard_map/pack/pallas_call | solution.py:358
  2.8 0.0 copy-start
  2.8 0.0 copy-start.2
  2.8 0.0 copy-start.4
  2.8 0.0 copy-start.7
  2.8 18.4 %all_to_all.15.halo_ref = bf16[8,160,128]{2,1,0:T(8,128)(2,1)S(1)} all-to-all(bf16[8,160,128]{2,1,0:T(8,128)(2,1)} %pack.1), channel_id=1, replica_groups=mesh['slide'=4,'tile'=8] {'tile'}, dimensions={0} | all-to-all | bytes 655360 | tf_op jit(solution)/shard_map/all_to_all | solution.py:374
  21.2 0.0 copy-done.5
  21.2 0.0 copy-done.6
  21.2 0.0 copy-done
  21.2 0.0 copy-done.2
  21.2 0.0 copy-done.4
  21.2 0.0 copy-done.7
  21.2 3.5 %grads.1 = bf16[576,128]{1,0:T(8,128)(2,1)} custom-call(s32[2,8]{1,0:T(2,128)S(1)} %bitcast.19, s32[1,2]{1,0:T(1,128)S(1)} %copy-done.7, bf16[2,32,2048]{2,1,0:T(8,128)(2,1)S(1)} %bitcast.12, bf16[2,32,2048]{2,1,0:T(8,128)(2,1)S(1)} %bitcast.16, bf16[8,160,128]{2,1,0:T(8,128)(2,1)S(1)} %all_to_all.15.halo_ref, bf16[3,3,64,64]{3,2,1,0:T(8,128)(2,1)S(1)} %copy-done.5, ...), custom_call_target="tpu_custom_call" | custom-call | flops 4000000000 | bytes 10000000 | tf_op jit(solution)/shard_map/grads/pallas_call | solution.py:401
  24.7 2.9 %all-to-all-start.1 = ((bf16[32,9,2,128]{3,2,1,0:T(2,128)(2,1)}), bf16[32,9,2,128]{3,2,1,0:T(2,128)(2,1)S(1)}, u32[]{:S(2)}, u32[]{:S(2)}) async-start(bf16[32,9,2,128]{3,2,1,0:T(2,128)(2,1)} %bitcast.5), calls=%async_computation.1 | async-start | bytes 294912 | tf_op jit(solution)/shard_map/all_to_all | solution.py:453
  27.7 1.4 %columns.1 = (bf16[2,32,128]{2,1,0:T(8,128)(2,1)}, bf16[2,32,128]{2,1,0:T(8,128)(2,1)}) custom-call(s32[1,2]{1,0:T(1,128)} %tissue_hbm.4, bf16[2,32,2048]{2,1,0:T(8,128)(2,1)} %bitcast.11, bf16[2,32,2048]{2,1,0:T(8,128)(2,1)} %bitcast.15), custom_call_target="tpu_custom_call" | custom-call | flops 4000000000 | bytes 10000000 | tf_op jit(solution)/shard_map/columns/pallas_call | solution.py:377
  29.1 3.7 %collective-permute-start = (bf16[2,32,128]{2,1,0:T(8,128)(2,1)}, bf16[2,32,128]{2,1,0:T(8,128)(2,1)S(1)}, u32[]{:S(2)}, u32[]{:S(2)}) collective-permute-start(bf16[2,32,128]{2,1,0:T(8,128)(2,1)} %get-tuple-element.12), channel_id=1, source_target_pairs={{0,1},{1,2},{2,3},{3,4},{4,5},{5,6},{6,7},{8,9},{9,10},{10,11},{11... | collective-permute-start | bytes 49160 | tf_op jit(solution)/shard_map/ppermute | solution.py:392
  32.8 1.3 %collective-permute-start.1 = (bf16[2,32,128]{2,1,0:T(8,128)(2,1)}, bf16[2,32,128]{2,1,0:T(8,128)(2,1)S(1)}, u32[]{:S(2)}, u32[]{:S(2)}) collective-permute-start(bf16[2,32,128]{2,1,0:T(8,128)(2,1)} %get-tuple-element.13), channel_id=1, source_target_pairs={{1,0},{2,1},{3,2},{4,3},{5,4},{6,5},{7,6},{9,8},{10,9},{11,10},{12... | collective-permute-start | bytes 49160 | tf_op jit(solution)/shard_map/ppermute | solution.py:393
  34.1 1.4 %all-to-all-done.1 = bf16[32,9,2,128]{3,2,1,0:T(2,128)(2,1)S(1)} async-done(((bf16[32,9,2,128]{3,2,1,0:T(2,128)(2,1)}), bf16[32,9,2,128]{3,2,1,0:T(2,128)(2,1)S(1)}, u32[]{:S(2)}, u32[]{:S(2)}) %all-to-all-start.1) | async-done | bytes 147488 | tf_op jit(solution)/shard_map/all_to_all | solution.py:453
  35.5 0.1 convert_element_type.16
  35.6 0.0 copy-start.3
  35.6 0.1 reduce_sum.9
  35.7 0.0 copy-start.1
  35.7 0.7 %broadcast_in_dim.14 = bf16[32,9,2,128]{3,2,1,0:T(2,128)(2,1)} broadcast(bf16[9,2,128]{2,1,0:T(2,128)(2,1)S(1)} %reduce_sum.9), dimensions={1,2,3} | broadcast | bytes 152064 | tf_op jit(solution)/shard_map/broadcast_in_dim | solution.py:455
  36.5 0.0 copy-start.8
  36.5 5.3 %all-to-all-start.2 = ((bf16[32,9,2,128]{3,2,1,0:T(2,128)(2,1)}), bf16[32,9,2,128]{3,2,1,0:T(2,128)(2,1)S(1)}, u32[]{:S(2)}, u32[]{:S(2)}) async-start(bf16[32,9,2,128]{3,2,1,0:T(2,128)(2,1)} %broadcast_in_dim.14), calls=%async_computation.2 | async-start | bytes 294912 | tf_op jit(solution)/shard_map/all_to_all | solution.py:456
  41.8 0.0 collective-permute-done.from_west_ref
  41.8 0.0 collective-permute-done.1.from_east_ref
  41.8 0.0 copy-done.3
  41.8 0.0 copy-done.1
  41.8 0.0 copy-done.8
  41.8 4.0 %fields.1 = (bf16[2,32,2048]{2,1,0:T(8,128)(2,1)}, bf16[2,32,2048]{2,1,0:T(8,128)(2,1)}) custom-call(s32[2,8]{1,0:T(2,128)S(1)} %bitcast.20, s32[1,2]{1,0:T(1,128)S(1)} %copy-done.8, bf16[2,32,2048]{2,1,0:T(8,128)(2,1)S(1)} %bitcast.13, bf16[2,32,2048]{2,1,0:T(8,128)(2,1)S(1)} %bitcast.17, bf16[8,160,128]{2,1,0:T(8,128)(2,1)S(1)} %all_to_all.15.halo_ref, ...), custom_call_target="tpu_custom_call" | custom-call | flops 4000000000 | bytes 10000000 | tf_op jit(solution)/shard_map/fields/pallas_call | solution.py:423
  45.9 3.8 %all-to-all-done.2 = bf16[32,9,2,128]{3,2,1,0:T(2,128)(2,1)S(1)} async-done(((bf16[32,9,2,128]{3,2,1,0:T(2,128)(2,1)}), bf16[32,9,2,128]{3,2,1,0:T(2,128)(2,1)S(1)}, u32[]{:S(2)}, u32[]{:S(2)}) %all-to-all-start.2) | async-done | bytes 147488 | tf_op jit(solution)/shard_map/all_to_all | solution.py:456
  49.6 0.9 %fusion = (f32[576,64]{1,0:T(8,128)}, f32[576,64]{1,0:T(8,128)}) fusion(f32[576,128]{1,0:T(8,128)S(1)} %convert.1), kind=kLoop, calls=%fused_computation | loop fusion | bytes 589824 | tf_op jit(solution)/shard_map/slice | solution.py:459
  (1 shorter events, 0.0 us)
Async XLA Ops:
  0.6 20.5 %copy-start.5 = (bf16[3,3,64,64]{3,2,1,0:T(8,128)(2,1)S(1)}, bf16[3,3,64,64]{3,2,1,0:T(8,128)(2,1)}, u32[]{:S(2)}) copy-start(bf16[3,3,64,64]{3,2,1,0:T(8,128)(2,1)} %one_ref.3) | copy-start | bytes 221188
  0.6 20.5 %copy-start.6 = (bf16[3,3,64,64]{3,2,1,0:T(8,128)(2,1)S(1)}, bf16[3,3,64,64]{3,2,1,0:T(8,128)(2,1)}, u32[]{:S(2)}) copy-start(bf16[3,3,64,64]{3,2,1,0:T(8,128)(2,1)} %two_ref.3) | copy-start | bytes 221188
  2.8 18.4 %copy-start = (bf16[1,2,32,2048]{3,2,1,0:T(8,128)(2,1)S(1)}, bf16[1,2,32,2048]{3,2,1,0:T(8,128)(2,1)}, u32[]{:S(2)}) copy-start(bf16[1,2,32,2048]{3,2,1,0:T(8,128)(2,1)} %param.6) | copy-start | bytes 786436
  2.8 18.4 %copy-start.2 = (bf16[1,2,32,2048]{3,2,1,0:T(8,128)(2,1)S(1)}, bf16[1,2,32,2048]{3,2,1,0:T(8,128)(2,1)}, u32[]{:S(2)}) copy-start(bf16[1,2,32,2048]{3,2,1,0:T(8,128)(2,1)} %param.7) | copy-start | bytes 786436
  2.8 18.4 %copy-start.4 = (s32[1,2,8]{2,1,0:T(2,128)S(1)}, s32[1,2,8]{2,1,0:T(2,128)}, u32[]{:S(2)}) copy-start(s32[1,2,8]{2,1,0:T(2,128)} %param.11) | copy-start | bytes 196
  2.8 18.4 %copy-start.7 = (s32[1,2]{1,0:T(1,128)S(1)}, s32[1,2]{1,0:T(1,128)}, u32[]{:S(2)}) copy-start(s32[1,2]{1,0:T(1,128)} %tissue_hbm.4) | copy-start | bytes 28
  24.7 10.8 %all-to-all-start.1 = ((bf16[32,9,2,128]{3,2,1,0:T(2,128)(2,1)}), bf16[32,9,2,128]{3,2,1,0:T(2,128)(2,1)S(1)}, u32[]{:S(2)}, u32[]{:S(2)}) async-start(bf16[32,9,2,128]{3,2,1,0:T(2,128)(2,1)} %bitcast.5), calls=%async_computation.1 | async-start | bytes 294912 | tf_op jit(solution)/shard_map/all_to_all | solution.py:453
  29.1 12.7 %collective-permute-start = (bf16[2,32,128]{2,1,0:T(8,128)(2,1)}, bf16[2,32,128]{2,1,0:T(8,128)(2,1)S(1)}, u32[]{:S(2)}, u32[]{:S(2)}) collective-permute-start(bf16[2,32,128]{2,1,0:T(8,128)(2,1)} %get-tuple-element.12), channel_id=1, source_target_pairs={{0,1},{1,2},{2,3},{3,4},{4,5},{5,6},{6,7},{8,9},{9,10},{10,11},{11... | collective-permute-start | bytes 49160 | tf_op jit(solution)/shard_map/ppermute | solution.py:392
  32.8 9.0 %collective-permute-start.1 = (bf16[2,32,128]{2,1,0:T(8,128)(2,1)}, bf16[2,32,128]{2,1,0:T(8,128)(2,1)S(1)}, u32[]{:S(2)}, u32[]{:S(2)}) collective-permute-start(bf16[2,32,128]{2,1,0:T(8,128)(2,1)} %get-tuple-element.13), channel_id=1, source_target_pairs={{1,0},{2,1},{3,2},{4,3},{5,4},{6,5},{7,6},{9,8},{10,9},{11,10},{12... | collective-permute-start | bytes 49160 | tf_op jit(solution)/shard_map/ppermute | solution.py:393
  35.6 6.2 %copy-start.3 = (bf16[1,2,32,2048]{3,2,1,0:T(8,128)(2,1)S(1)}, bf16[1,2,32,2048]{3,2,1,0:T(8,128)(2,1)}, u32[]{:S(2)}) copy-start(bf16[1,2,32,2048]{3,2,1,0:T(8,128)(2,1)} %param.7) | copy-start | bytes 786436
  35.7 6.1 %copy-start.1 = (bf16[1,2,32,2048]{3,2,1,0:T(8,128)(2,1)S(1)}, bf16[1,2,32,2048]{3,2,1,0:T(8,128)(2,1)}, u32[]{:S(2)}) copy-start(bf16[1,2,32,2048]{3,2,1,0:T(8,128)(2,1)} %param.6) | copy-start | bytes 786436
  36.5 5.4 %copy-start.8 = (s32[1,2]{1,0:T(1,128)S(1)}, s32[1,2]{1,0:T(1,128)}, u32[]{:S(2)}) copy-start(s32[1,2]{1,0:T(1,128)} %tissue_hbm.4) | copy-start | bytes 28
  36.5 13.1 %all-to-all-start.2 = ((bf16[32,9,2,128]{3,2,1,0:T(2,128)(2,1)}), bf16[32,9,2,128]{3,2,1,0:T(2,128)(2,1)S(1)}, u32[]{:S(2)}, u32[]{:S(2)}) async-start(bf16[32,9,2,128]{3,2,1,0:T(2,128)(2,1)} %broadcast_in_dim.14), calls=%async_computation.2 | async-start | bytes 294912 | tf_op jit(solution)/shard_map/all_to_all | solution.py:456

commit v14 on v12

--- a/solution.py
+++ b/solution.py
@@ -161,8 +161,8 @@
 
 def grads_kernel(
     links_hbm, tissue_hbm, image_ref, cotangent_ref, halo_ref, one_ref, two_ref,
-    grads_ref,
-    links_ref, tissue_ref, wide_in, wide_up, own_hidden, own_delta,
+    grads_hbm,
+    grads_ref, links_ref, tissue_ref, wide_in, wide_up, own_hidden, own_delta,
     taps_in, taps_up, forward_ref, back_ref, acc_ref, sems,
 ):
     slots, side, width = image_ref.shape
@@ -219,6 +219,7 @@
         second_grad = term_two if second_grad is None else second_grad + term_two
 
     total = grads_ref.shape[0]
+    copies = []
     left = lax.broadcasted_iota(jnp.int32, (half, LANES), 1) < half
     for a in range(3):
         one = first_grad[:, a * 256 : (a + 1) * 256].T
@@ -232,8 +233,15 @@
             rows = slice((a * 3 + b) * half, (a * 3 + b + 1) * half)
             both = jnp.where(left, upper + pltpu.roll(lower, half, 1), right[2 - b])
             grads_ref[rows, :] = both.astype(BF16)
+        rows = slice(a * 192, (a + 1) * 192 if a < 2 else total)
+        copies.append(pltpu.make_async_copy(grads_ref.at[rows], grads_hbm.at[rows], sems.at[2 + a]))
+        if a < 2:
+            copies[a].start()
     if total > 576:
         grads_ref[576:total, :] = jnp.zeros((total - 576, LANES), BF16)
+    copies[2].start()
+    for copy in copies:
+        copy.wait()
 
 
 def fields_kernel(
@@ -350,8 +358,9 @@
         grads_kernel,
         out_shape=jax.ShapeDtypeStruct((total, LANES), BF16),
         in_specs=[ANY, ANY] + [VMEM] * 5,
-        out_specs=VMEM,
+        out_specs=ANY,
         scratch_shapes=[
+            pltpu.VMEM((total, LANES), BF16),
             pltpu.SMEM(links.shape, jnp.int32),
             pltpu.SMEM(tissue.shape, jnp.int32),
             wide,
@@ -362,7 +371,7 @@
             pltpu.VMEM((slots, 3, pairs + 2, side, LANES), BF16),
             *weights,
             pltpu.VMEM((slots, 2, pairs + 1, side, LANES), F32),
-            pltpu.SemaphoreType.DMA((2,)),
+            pltpu.SemaphoreType.DMA((5,)),
         ],
         compiler_params=pltpu.CompilerParams(vmem_limit_bytes=32 * 2**20),
         cost_estimate=cost,

time: 48.8 us -> 48.8 us (level)
  no operation moved by 1% of the time
where the time goes in v14:
time: 48.8 us; the launch traced here: 48.5 us
  blocking collectives  29.8 us (61%)
  Pallas kernels  9.65 us (20%)
  waiting for transfers between devices  3.79 us (8%)
  starting transfers between devices  3.21 us (7%)
  local copies, waits for them, and re-layouts  1.01 us (2%)
  between operations  0.75 us (2%)
    all_to_all x1, blocking collectives, local(): halo = lax.all_to_all(packed, 'tile', 0, 0, tiled=True)  19.5 us
    all_to_all x1, blocking collectives, local(): whole = lax.all_to_all(sums, ('slide', 'tile'), 0, 0, tiled=True)  10.4 us
    pallas_call x1, Pallas kernels, local(): pl.pallas_call(fields_kernel, out_shape=(jax.ShapeDtypeStruct((slots, sid...  4.03 us
    all_to_all x1, waiting for transfers between devices, local(): lax.all_to_all(grads.reshape(devices, chunk, 2, LANES), ('slide', 'tile')...  3.79 us
    pallas_call x1, Pallas kernels, local(): pl.pallas_call(grads_kernel, out_shape=jax.ShapeDtypeStruct((total, LANES...  3.5 us
    all_to_all x1, starting transfers between devices, local(): lax.all_to_all(grads.reshape(devices, chunk, 2, LANES), ('slide', 'tile')...  3.21 us
    pallas_call x1, Pallas kernels, local(): pl.pallas_call(pack_kernel, out_shape=jax.ShapeDtypeStruct((devices_tile,...  2.12 us
  transfers between devices with their start and end apart: 1, of which 1 were waited for; matrix products, arithmetic and copies ran while one was open for 0% of the time, Pallas kernels for 8%

profile of v14, /device:TPU:0, one launch (start us, length us, event | category | flops | bytes accessed | tf_op | source)
XLA Modules:
  0.0 48.5 jit_solution(12893517043619052387)
XLA Ops:
  0.6 0.0 copy-start.4
  0.6 2.1 %pack.1 = bf16[8,192,128]{2,1,0:T(8,128)(2,1)} custom-call(s32[2,8]{1,0:T(2,128)} %bitcast.16, bf16[2,32,2048]{2,1,0:T(8,128)(2,1)} %bitcast.10, bf16[2,32,2048]{2,1,0:T(8,128)(2,1)} %bitcast.13), custom_call_target="tpu_custom_call" | custom-call | tf_op jit(solution)/shard_map/pack/pallas_call | solution.py:335
  2.8 0.0 copy-start
  2.8 0.0 copy-start.1
  2.8 0.0 copy-start.2
  2.8 0.0 copy-start.3
  2.8 0.0 copy-start.5
  2.8 19.5 %all_to_all.15.halo_ref = bf16[8,192,128]{2,1,0:T(8,128)(2,1)S(1)} all-to-all(bf16[8,192,128]{2,1,0:T(8,128)(2,1)} %pack.1), channel_id=1, replica_groups=mesh['slide'=4,'tile'=8] {'tile'}, dimensions={0} | all-to-all | bytes 786432 | tf_op jit(solution)/shard_map/all_to_all | solution.py:350
  22.3 0.0 copy-done.4
  22.3 0.0 copy-done
  22.3 0.0 copy-done.1
  22.3 0.0 copy-done.2
  22.3 0.0 copy-done.3
  22.3 0.0 copy-done.5
  22.3 3.5 %grads.1 = bf16[576,128]{1,0:T(8,128)(2,1)} custom-call(s32[2,8]{1,0:T(2,128)S(1)} %bitcast.17, s32[1,2]{1,0:T(1,128)S(1)} %copy-done.5, bf16[2,32,2048]{2,1,0:T(8,128)(2,1)S(1)} %bitcast.11, bf16[2,32,2048]{2,1,0:T(8,128)(2,1)S(1)} %bitcast.14, bf16[8,192,128]{2,1,0:T(8,128)(2,1)S(1)} %all_to_all.15.halo_ref, bf16[3,3,64,64]{3,2,1,0:T(8,128)(2,1)S(1)} %copy-done.3, ...), custom_call_target="tpu_custom_call" | custom-call | flops 4000000000 | bytes 10000000 | tf_op jit(solution)/shard_map/grads/pallas_call | solution.py:357
  25.9 3.2 %all-to-all-start.1 = ((bf16[32,9,2,128]{3,2,1,0:T(2,128)(2,1)}), bf16[32,9,2,128]{3,2,1,0:T(2,128)(2,1)S(1)}, u32[]{:S(2)}, u32[]{:S(2)}) async-start(bf16[32,9,2,128]{3,2,1,0:T(2,128)(2,1)} %bitcast.3), calls=%async_computation.1 | async-start | bytes 294912 | tf_op jit(solution)/shard_map/all_to_all | solution.py:410
  29.1 4.0 %fields.1 = (bf16[2,32,2048]{2,1,0:T(8,128)(2,1)}, bf16[2,32,2048]{2,1,0:T(8,128)(2,1)}) custom-call(s32[2,8]{1,0:T(2,128)S(1)} %bitcast.18, s32[1,2]{1,0:T(1,128)S(1)} %copy-done.5, bf16[2,32,2048]{2,1,0:T(8,128)(2,1)S(1)} %bitcast.12, bf16[2,32,2048]{2,1,0:T(8,128)(2,1)S(1)} %bitcast.15, bf16[8,192,128]{2,1,0:T(8,128)(2,1)S(1)} %all_to_all.15.halo_ref, ...), custom_call_target="tpu_custom_call" | custom-call | flops 4000000000 | bytes 10000000 | tf_op jit(solution)/shard_map/fields/pallas_call | solution.py:380
  33.1 3.8 %all-to-all-done.1 = bf16[32,9,2,128]{3,2,1,0:T(2,128)(2,1)S(1)} async-done(((bf16[32,9,2,128]{3,2,1,0:T(2,128)(2,1)}), bf16[32,9,2,128]{3,2,1,0:T(2,128)(2,1)S(1)}, u32[]{:S(2)}, u32[]{:S(2)}) %all-to-all-start.1) | async-done | bytes 147488 | tf_op jit(solution)/shard_map/all_to_all | solution.py:410
  36.9 0.1 convert_element_type.12
  37.0 0.1 reduce_sum.9
  37.1 0.1 broadcast_in_dim.14
  37.2 10.4 %all_to_all.16 = bf16[32,9,2,128]{3,2,1,0:T(2,128)(2,1)S(1)} all-to-all(bf16[32,9,2,128]{3,2,1,0:T(2,128)(2,1)S(1)} %broadcast_in_dim.14), channel_id=1, replica_groups=mesh['slide'=4,'tile'=8] {'slide','tile'}, dimensions={0} | all-to-all | bytes 294912 | tf_op jit(solution)/shard_map/all_to_all | solution.py:414
  47.6 0.9 %fusion = (f32[576,64]{1,0:T(8,128)}, f32[576,64]{1,0:T(8,128)}) fusion(f32[576,128]{1,0:T(8,128)S(1)} %convert.1), kind=kLoop, calls=%fused_computation | loop fusion | bytes 589824 | tf_op jit(solution)/shard_map/slice | solution.py:417
  (1 shorter events, 0.0 us)
Async XLA Ops:
  0.6 21.7 %copy-start.4 = (bf16[3,3,64,64]{3,2,1,0:T(8,128)(2,1)S(1)}, bf16[3,3,64,64]{3,2,1,0:T(8,128)(2,1)}, u32[]{:S(2)}) copy-start(bf16[3,3,64,64]{3,2,1,0:T(8,128)(2,1)} %two_ref.3) | copy-start | bytes 221188
  2.8 19.5 %copy-start = (bf16[1,2,32,2048]{3,2,1,0:T(8,128)(2,1)S(1)}, bf16[1,2,32,2048]{3,2,1,0:T(8,128)(2,1)}, u32[]{:S(2)}) copy-start(bf16[1,2,32,2048]{3,2,1,0:T(8,128)(2,1)} %param.6) | copy-start | bytes 786436
  2.8 19.5 %copy-start.1 = (bf16[1,2,32,2048]{3,2,1,0:T(8,128)(2,1)S(1)}, bf16[1,2,32,2048]{3,2,1,0:T(8,128)(2,1)}, u32[]{:S(2)}) copy-start(bf16[1,2,32,2048]{3,2,1,0:T(8,128)(2,1)} %param.7) | copy-start | bytes 786436
  2.8 19.5 %copy-start.2 = (s32[1,2,8]{2,1,0:T(2,128)S(1)}, s32[1,2,8]{2,1,0:T(2,128)}, u32[]{:S(2)}) copy-start(s32[1,2,8]{2,1,0:T(2,128)} %param.11) | copy-start | bytes 196
  2.8 19.5 %copy-start.3 = (bf16[3,3,64,64]{3,2,1,0:T(8,128)(2,1)S(1)}, bf16[3,3,64,64]{3,2,1,0:T(8,128)(2,1)}, u32[]{:S(2)}) copy-start(bf16[3,3,64,64]{3,2,1,0:T(8,128)(2,1)} %one_ref.3) | copy-start | bytes 221188
  2.8 19.5 %copy-start.5 = (s32[1,2]{1,0:T(1,128)S(1)}, s32[1,2]{1,0:T(1,128)}, u32[]{:S(2)}) copy-start(s32[1,2]{1,0:T(1,128)} %tissue_hbm.3) | copy-start | bytes 28
  25.9 11.0 %all-to-all-start.1 = ((bf16[32,9,2,128]{3,2,1,0:T(2,128)(2,1)}), bf16[32,9,2,128]{3,2,1,0:T(2,128)(2,1)S(1)}, u32[]{:S(2)}, u32[]{:S(2)}) async-start(bf16[32,9,2,128]{3,2,1,0:T(2,128)(2,1)} %bitcast.3), calls=%async_computation.1 | async-start | bytes 294912 | tf_op jit(solution)/shard_map/all_to_all | solution.py:410

commit v15 on v12

--- a/solution.py
+++ b/solution.py
@@ -59,8 +59,8 @@
 
 
 def pack_kernel(
-    links_hbm, image_hbm, cotangent_hbm, out_ref,
-    links_ref, image_ref, cotangent_ref, strip_ref, sems,
+    links_hbm, image_hbm, cotangent_hbm, out_hbm,
+    out_ref, links_ref, image_ref, cotangent_ref, strip_ref, sems,
 ):
     slots, side, width = image_ref.shape
     pairs = width // LANES
@@ -76,6 +76,7 @@
     me = lax.axis_index("tile")
     left = lax.broadcasted_iota(jnp.int32, (16, LANES), 1) < half
     copies[0].wait()
+    sends = []
     for field, (_, ref) in enumerate(fields):
         for slot in range(slots):
             copies[1 + field * slots + slot].wait()
@@ -110,6 +111,15 @@
                         out_ref[device, first : first + 16, :] = strip_ref[which].astype(BF16)
                         first += RING
                         out_ref[device, first : first + 16, :] = strip_ref[which + 1].astype(BF16)
+        for ring in range(2):
+            rows = slice(ring * RING + field * 48, ring * RING + field * 48 + 48)
+            send = pltpu.make_async_copy(
+                out_ref.at[:, rows], out_hbm.at[:, rows], sems.at[2 * slots + 1 + 2 * field + ring]
+            )
+            send.start()
+            sends.append(send)
+    for send in sends:
+        send.wait()
 
 
 def place_halo(links_ref, halo_ref, rings, wide, slot, field, slots, side, pairs, me):
@@ -328,13 +338,14 @@
         pack_kernel,
         out_shape=jax.ShapeDtypeStruct((devices_tile, 2 * RING, LANES), BF16),
         in_specs=[ANY] * 3,
-        out_specs=VMEM,
+        out_specs=ANY,
         scratch_shapes=[
+            pltpu.VMEM((devices_tile, 2 * RING, LANES), BF16),
             pltpu.SMEM(links.shape, jnp.int32),
             pltpu.VMEM(image.shape, BF16),
             pltpu.VMEM(image.shape, BF16),
             pltpu.VMEM((4, 16, LANES), F32),
-            pltpu.SemaphoreType.DMA((2 * slots + 1,)),
+            pltpu.SemaphoreType.DMA((2 * slots + 5,)),
         ],
         compiler_params=pltpu.CompilerParams(vmem_limit_bytes=PACK_LIMIT),
         name="pack",

time: 48.8 us -> 48.8 us (level)
  no operation moved by 1% of the time
where the time goes in v15:
time: 48.8 us; the launch traced here: 48.5 us
  blocking collectives  30 us (61%)
  Pallas kernels  9.67 us (20%)
  waiting for transfers between devices  3.79 us (8%)
  starting transfers between devices  3.06 us (6%)
  local copies, waits for them, and re-layouts  1.01 us (2%)
  between operations  0.75 us (2%)
    all_to_all x1, blocking collectives, local(): halo = lax.all_to_all(packed, 'tile', 0, 0, tiled=True)  19.6 us
    all_to_all x1, blocking collectives, local(): whole = lax.all_to_all(sums, ('slide', 'tile'), 0, 0, tiled=True)  10.4 us
    pallas_call x1, Pallas kernels, local(): pl.pallas_call(fields_kernel, out_shape=(jax.ShapeDtypeStruct((slots, sid...  4.03 us
    all_to_all x1, waiting for transfers between devices, local(): lax.all_to_all(grads.reshape(devices, chunk, 2, LANES), ('slide', 'tile')...  3.79 us
    pallas_call x1, Pallas kernels, local(): pl.pallas_call(grads_kernel, out_shape=jax.ShapeDtypeStruct((total, LANES...  3.52 us
    all_to_all x1, starting transfers between devices, local(): lax.all_to_all(grads.reshape(devices, chunk, 2, LANES), ('slide', 'tile')...  3.06 us
    pallas_call x1, Pallas kernels, local(): pl.pallas_call(pack_kernel, out_shape=jax.ShapeDtypeStruct((devices_tile,...  2.12 us
  transfers between devices with their start and end apart: 1, of which 1 were waited for; matrix products, arithmetic and copies ran while one was open for 0% of the time, Pallas kernels for 8%

profile of v15, /device:TPU:0, one launch (start us, length us, event | category | flops | bytes accessed | tf_op | source)
XLA Modules:
  0.0 48.5 jit_solution(224152670433156959)
XLA Ops:
  0.6 0.0 copy-start.4
  0.6 2.1 %pack.1 = bf16[8,192,128]{2,1,0:T(8,128)(2,1)} custom-call(s32[2,8]{1,0:T(2,128)} %bitcast.16, bf16[2,32,2048]{2,1,0:T(8,128)(2,1)} %bitcast.10, bf16[2,32,2048]{2,1,0:T(8,128)(2,1)} %bitcast.13), custom_call_target="tpu_custom_call" | custom-call | tf_op jit(solution)/shard_map/pack/pallas_call | solution.py:337
  2.8 0.0 copy-start
  2.8 0.0 copy-start.1
  2.8 0.0 copy-start.2
  2.8 0.0 copy-start.3
  2.8 0.0 copy-start.5
  2.8 19.6 %all_to_all.15.halo_ref = bf16[8,192,128]{2,1,0:T(8,128)(2,1)S(1)} all-to-all(bf16[8,192,128]{2,1,0:T(8,128)(2,1)} %pack.1), channel_id=1, replica_groups=mesh['slide'=4,'tile'=8] {'tile'}, dimensions={0} | all-to-all | bytes 786432 | tf_op jit(solution)/shard_map/all_to_all | solution.py:353
  22.5 0.0 copy-done.4
  22.5 0.0 copy-done
  22.5 0.0 copy-done.1
  22.5 0.0 copy-done.2
  22.5 0.0 copy-done.3
  22.5 0.0 copy-done.5
  22.5 3.5 %grads.1 = bf16[576,128]{1,0:T(8,128)(2,1)} custom-call(s32[2,8]{1,0:T(2,128)S(1)} %bitcast.17, s32[1,2]{1,0:T(1,128)S(1)} %copy-done.5, bf16[2,32,2048]{2,1,0:T(8,128)(2,1)S(1)} %bitcast.11, bf16[2,32,2048]{2,1,0:T(8,128)(2,1)S(1)} %bitcast.14, bf16[8,192,128]{2,1,0:T(8,128)(2,1)S(1)} %all_to_all.15.halo_ref, bf16[3,3,64,64]{3,2,1,0:T(8,128)(2,1)S(1)} %copy-done.3, ...), custom_call_target="tpu_custom_call" | custom-call | flops 4000000000 | bytes 10000000 | tf_op jit(solution)/shard_map/grads/pallas_call | solution.py:360
  26.0 3.1 %all-to-all-start.1 = ((bf16[32,9,2,128]{3,2,1,0:T(2,128)(2,1)}), bf16[32,9,2,128]{3,2,1,0:T(2,128)(2,1)S(1)}, u32[]{:S(2)}, u32[]{:S(2)}) async-start(bf16[32,9,2,128]{3,2,1,0:T(2,128)(2,1)} %bitcast.3), calls=%async_computation.1 | async-start | bytes 294912 | tf_op jit(solution)/shard_map/all_to_all | solution.py:412
  29.1 4.0 %fields.1 = (bf16[2,32,2048]{2,1,0:T(8,128)(2,1)}, bf16[2,32,2048]{2,1,0:T(8,128)(2,1)}) custom-call(s32[2,8]{1,0:T(2,128)S(1)} %bitcast.18, s32[1,2]{1,0:T(1,128)S(1)} %copy-done.5, bf16[2,32,2048]{2,1,0:T(8,128)(2,1)S(1)} %bitcast.12, bf16[2,32,2048]{2,1,0:T(8,128)(2,1)S(1)} %bitcast.15, bf16[8,192,128]{2,1,0:T(8,128)(2,1)S(1)} %all_to_all.15.halo_ref, ...), custom_call_target="tpu_custom_call" | custom-call | flops 4000000000 | bytes 10000000 | tf_op jit(solution)/shard_map/fields/pallas_call | solution.py:382
  33.1 3.8 %all-to-all-done.1 = bf16[32,9,2,128]{3,2,1,0:T(2,128)(2,1)S(1)} async-done(((bf16[32,9,2,128]{3,2,1,0:T(2,128)(2,1)}), bf16[32,9,2,128]{3,2,1,0:T(2,128)(2,1)S(1)}, u32[]{:S(2)}, u32[]{:S(2)}) %all-to-all-start.1) | async-done | bytes 147488 | tf_op jit(solution)/shard_map/all_to_all | solution.py:412
  36.9 0.1 convert_element_type.12
  37.0 0.1 reduce_sum.9
  37.1 0.1 broadcast_in_dim.14
  37.2 10.4 %all_to_all.16 = bf16[32,9,2,128]{3,2,1,0:T(2,128)(2,1)S(1)} all-to-all(bf16[32,9,2,128]{3,2,1,0:T(2,128)(2,1)S(1)} %broadcast_in_dim.14), channel_id=1, replica_groups=mesh['slide'=4,'tile'=8] {'slide','tile'}, dimensions={0} | all-to-all | bytes 294912 | tf_op jit(solution)/shard_map/all_to_all | solution.py:416
  47.6 0.9 %fusion = (f32[576,64]{1,0:T(8,128)}, f32[576,64]{1,0:T(8,128)}) fusion(f32[576,128]{1,0:T(8,128)S(1)} %convert.1), kind=kLoop, calls=%fused_computation | loop fusion | bytes 589824 | tf_op jit(solution)/shard_map/slice | solution.py:419
  (1 shorter events, 0.0 us)
Async XLA Ops:
  0.6 21.8 %copy-start.4 = (bf16[3,3,64,64]{3,2,1,0:T(8,128)(2,1)S(1)}, bf16[3,3,64,64]{3,2,1,0:T(8,128)(2,1)}, u32[]{:S(2)}) copy-start(bf16[3,3,64,64]{3,2,1,0:T(8,128)(2,1)} %two_ref.3) | copy-start | bytes 221188
  2.8 19.7 %copy-start = (bf16[1,2,32,2048]{3,2,1,0:T(8,128)(2,1)S(1)}, bf16[1,2,32,2048]{3,2,1,0:T(8,128)(2,1)}, u32[]{:S(2)}) copy-start(bf16[1,2,32,2048]{3,2,1,0:T(8,128)(2,1)} %param.6) | copy-start | bytes 786436
  2.8 19.7 %copy-start.1 = (bf16[1,2,32,2048]{3,2,1,0:T(8,128)(2,1)S(1)}, bf16[1,2,32,2048]{3,2,1,0:T(8,128)(2,1)}, u32[]{:S(2)}) copy-start(bf16[1,2,32,2048]{3,2,1,0:T(8,128)(2,1)} %param.7) | copy-start | bytes 786436
  2.8 19.7 %copy-start.2 = (s32[1,2,8]{2,1,0:T(2,128)S(1)}, s32[1,2,8]{2,1,0:T(2,128)}, u32[]{:S(2)}) copy-start(s32[1,2,8]{2,1,0:T(2,128)} %param.11) | copy-start | bytes 196
  2.8 19.7 %copy-start.3 = (bf16[3,3,64,64]{3,2,1,0:T(8,128)(2,1)S(1)}, bf16[3,3,64,64]{3,2,1,0:T(8,128)(2,1)}, u32[]{:S(2)}) copy-start(bf16[3,3,64,64]{3,2,1,0:T(8,128)(2,1)} %one_ref.3) | copy-start | bytes 221188
  2.8 19.7 %copy-start.5 = (s32[1,2]{1,0:T(1,128)S(1)}, s32[1,2]{1,0:T(1,128)}, u32[]{:S(2)}) copy-start(s32[1,2]{1,0:T(1,128)} %tissue_hbm.3) | copy-start | bytes 28
  26.0 10.9 %all-to-all-start.1 = ((bf16[32,9,2,128]{3,2,1,0:T(2,128)(2,1)}), bf16[32,9,2,128]{3,2,1,0:T(2,128)(2,1)S(1)}, u32[]{:S(2)}, u32[]{:S(2)}) async-start(bf16[32,9,2,128]{3,2,1,0:T(2,128)(2,1)} %bitcast.3), calls=%async_computation.1 | async-start | bytes 294912 | tf_op jit(solution)/shard_map/all_to_all | solution.py:412
